TPU v7x, 32 devices: a whole 2x2x4 slice. The times are simulated.
32 devices in a mesh: section: 2 (over y), dp: 16 (over z, x, core).
Axes of the slice: x: 2, y: 2, z: 4, core: 2. Of those that a mesh axis runs over, the one named last changes fastest.
Arguments:
- tokens: bfloat16 [16384, 768], P('dp'), may hold values from -6 to 6
- cotangent: bfloat16 [16384, 768], P('dp'), may hold values from -6 to 6
- segment_ids: int32 [32, 512], P('dp'), may hold values from 0 to 3, as said below
- valid_mask: int32 [32, 512], P('dp'), may hold values from 0 to 1, as said below
- cluster_perm: int32 [2, 32, 12, 512], P('section', 'dp'), may hold values from 0 to 511, as said below
- query_weight: bfloat16 [2, 768, 768], P('section'), may hold values from -0.21875 to 0.21875
- query_bias: bfloat16 [2, 768], P('section'), may hold values from -3 to 3
- key_weight: bfloat16 [2, 768, 768], P('section'), may hold values from -0.21875 to 0.21875
- value_weight: bfloat16 [2, 768, 768], P('section'), may hold values from -0.21875 to 0.21875
- value_bias: bfloat16 [2, 768], P('section'), may hold values from -1.75 to 1.75
- output_weight: bfloat16 [2, 768, 768], P('section'), may hold values from -0.625 to 0.625
- output_bias: bfloat16 [2, 768], P('section'), may hold values from -1.75 to 1.75
- attention_gain: bfloat16 [2, 768], P('section'), may hold values from 0.5 to 1.5
- attention_shift: bfloat16 [2, 768], P('section'), may hold values from -1.75 to 1.75
- up_weight: bfloat16 [2, 768, 3072], P('section'), may hold values from -0.21875 to 0.21875
- up_bias: bfloat16 [2, 3072], P('section'), may hold values from -1.75 to 1.75
- down_weight: bfloat16 [2, 3072, 768], P('section'), may hold values from -0.109375 to 0.109375
- down_bias: bfloat16 [2, 768], P('section'), may hold values from -1.75 to 1.75
- final_gain: bfloat16 [2, 768], P('section'), may hold values from 0.5 to 1.5
- final_shift: bfloat16 [2, 768], P('section'), may hold values from -1.75 to 1.75
Outputs:
- block_output: bfloat16 [16384, 768], P('dp', 'section')
- input_gradient: bfloat16 [16384, 768], P('dp', 'section')
- query_weight_gradient: float32 [2, 768, 768], P('section', 'dp')
- query_bias_gradient: float32 [2, 768], P('section', 'dp')
- key_weight_gradient: float32 [2, 768, 768], P('section', 'dp')
- value_weight_gradient: float32 [2, 768, 768], P('section', 'dp')
- value_bias_gradient: float32 [2, 768], P('section', 'dp')
- output_weight_gradient: float32 [2, 768, 768], P('section', 'dp')
- output_bias_gradient: float32 [2, 768], P('section', 'dp')
- attention_gain_gradient: float32 [2, 768], P('section', 'dp')
- attention_shift_gradient: float32 [2, 768], P('section', 'dp')
- up_weight_gradient: float32 [2, 768, 3072], P('section', 'dp')
- up_bias_gradient: float32 [2, 3072], P('section', 'dp')
- down_weight_gradient: float32 [2, 3072, 768], P('section', 'dp')
- down_bias_gradient: float32 [2, 768], P('section', 'dp')
- final_gain_gradient: float32 [2, 768], P('section', 'dp')
- final_shift_gradient: float32 [2, 768], P('section', 'dp')
- root_means: float32 [2, 3], P('section')
Inputs may be any that keep to these rules, and one draw needn't show every extreme that they name: `segment_ids`: along each row the ids start at 0 and never fall, rising by at most one from a position to the next; equal ids mark one document, and every row holds exactly 4 documents. `valid_mask`: in each row the valid tokens are a prefix of 170 tokens or more. `cluster_perm`: for each layer, row and head, a permutation of the row's 512 positions.
All inputs are finite; a program needn't handle non-finite values.
Results may differ from a plain program's by a relative error of at most 0.025.
Values may be sent and summed in bfloat16 or wider, within the bound.
No kernel may reach another device: no remote copies, remote signals or barrier semaphores. Data moves between devices by JAX's collectives and lax.ppermute only.
A program may use at most 448 MiB of HBM per device.

v0:
```python
from functools import partial

import jax
import jax.numpy as jnp
from jax import lax
from jax.sharding import PartitionSpec as P

HEAD_DIM = 64
CLUSTER = 128
SEQ = 512
MICRO = 2


def shifted(block, axis, distance):
    devices = range(lax.axis_size(axis))
    route = [(i - distance, i) for i in devices if i - distance in devices]
    return lax.ppermute(block, axis, route)


def swapped(value, axis, stride):
    mask = 2**stride
    pairs = [(source, source ^ mask) for source in range(lax.axis_size(axis))]
    return lax.ppermute(value, axis, pairs)


def layer_norm(residual, norm_gain, norm_shift):
    centre = residual - jnp.mean(residual, axis=-1, keepdims=True)
    spread = jnp.mean(centre * centre, axis=-1, keepdims=True)
    return centre * lax.rsqrt(spread + 1e-05) * norm_gain + norm_shift


def project(left, right):
    return jnp.dot(left, right, preferred_element_type=jnp.float32)


def project_back(left, right):
    return jnp.einsum("rse,de->rsd", left, right, preferred_element_type=jnp.float32)


def arrange(field, orders):
    row_count, length, width = field.shape
    head_count = orders.shape[1]
    head_split = field.reshape(row_count, length, head_count, width // head_count).transpose(
        0, 2, 1, 3
    )
    picked = jnp.take_along_axis(head_split, orders[..., None], axis=2)
    return picked.reshape(row_count, head_count, length // CLUSTER, CLUSTER, width // head_count)


def restore(sorted_field, inverse):
    row_count, head_count, blocks, cluster_size, head_size = sorted_field.shape
    flat_field = sorted_field.reshape(row_count, head_count, blocks * cluster_size, head_size)
    back_order = jnp.take_along_axis(flat_field, inverse[..., None], axis=2)
    return back_order.transpose(0, 2, 1, 3).reshape(
        row_count, blocks * cluster_size, head_count * head_size
    )


def cluster_mask(orders, segment, valid):
    row_count, head_count, length = orders.shape
    mask_shape = (row_count, head_count, length // CLUSTER, CLUSTER)
    seg_sorted = jnp.take_along_axis(
        jnp.broadcast_to(segment[:, None, :], orders.shape), orders, axis=2
    ).reshape(mask_shape)
    live_sorted = jnp.take_along_axis(
        jnp.broadcast_to(valid[:, None, :], orders.shape), orders, axis=2
    ).reshape(mask_shape)
    same_doc = seg_sorted[..., :, None] == seg_sorted[..., None, :]
    return same_doc & (live_sorted[..., None, :] == 1) | jnp.eye(CLUSTER, dtype=bool)


def scores_of(sorted_query, sorted_key):
    return jnp.einsum(
        "rhcqd,rhckd->rhcqk", sorted_query, sorted_key, preferred_element_type=jnp.float32
    ) * HEAD_DIM ** (-0.5)


def attend_forward(queries, key_rows, value_rows, orders, inverse, allowed):
    sorted_value = arrange(value_rows, orders)
    scores = scores_of(arrange(queries, orders), arrange(key_rows, orders))
    masked = jnp.where(allowed, scores, -1000000000.0)
    row_max = jnp.max(masked, axis=-1, keepdims=True)
    row_total = jnp.sum(jnp.where(allowed, jnp.exp(masked - row_max), 0.0), axis=-1, keepdims=True)
    logsum = row_max + jnp.log(row_total)
    probabilities = jnp.where(allowed, jnp.exp(masked - logsum), 0.0)
    mixed_values = jnp.einsum(
        "rhcqk,rhckd->rhcqd",
        probabilities.astype(jnp.bfloat16),
        sorted_value,
        preferred_element_type=jnp.float32,
    )
    return (restore(mixed_values.astype(jnp.bfloat16), inverse), logsum)


def attend_backward(queries, key_rows, value_rows, orders, inverse, allowed, logsum, d_context):
    sorted_query = arrange(queries, orders)
    sorted_key = arrange(key_rows, orders)
    sorted_value = arrange(value_rows, orders)
    masked = jnp.where(allowed, scores_of(sorted_query, sorted_key), -1000000000.0)
    probabilities = jnp.where(allowed, jnp.exp(masked - logsum), 0.0)
    d_sorted = arrange(d_context, orders)
    d_probs = jnp.einsum(
        "rhcqd,rhckd->rhcqk", d_sorted, sorted_value, preferred_element_type=jnp.float32
    )
    d_sorted_value = jnp.einsum(
        "rhcqk,rhcqd->rhckd",
        probabilities.astype(jnp.bfloat16),
        d_sorted,
        preferred_element_type=jnp.float32,
    )
    row_delta = jnp.sum(probabilities * d_probs, axis=-1, keepdims=True)
    d_scores = (probabilities * (d_probs - row_delta)).astype(jnp.bfloat16)
    d_sorted_query = jnp.einsum(
        "rhcqk,rhckd->rhcqd", d_scores, sorted_key, preferred_element_type=jnp.float32
    ) * HEAD_DIM ** (-0.5)
    d_sorted_key = jnp.einsum(
        "rhcqk,rhcqd->rhckd", d_scores, sorted_query, preferred_element_type=jnp.float32
    ) * HEAD_DIM ** (-0.5)
    return (
        restore(d_sorted_query, inverse).astype(jnp.bfloat16),
        restore(d_sorted_key, inverse).astype(jnp.bfloat16),
        restore(d_sorted_value, inverse).astype(jnp.bfloat16),
    )


def layer_forward(inputs, params, orders, segment, valid):
    (
        w_query,
        b_query,
        w_key,
        w_value,
        b_value,
        w_output,
        b_output,
        gain_one,
        shift_one,
        w_upper,
        b_upper,
        w_lower,
        b_lower,
        gain_two,
        shift_two,
    ) = params
    queries = (project(inputs, w_query) + b_query).astype(jnp.bfloat16)
    key_rows = project(inputs, w_key).astype(jnp.bfloat16)
    value_rows = (project(inputs, w_value) + b_value).astype(jnp.bfloat16)
    inverse = jnp.argsort(orders, axis=-1)
    allowed = cluster_mask(orders, segment, valid)
    context, logsum = attend_forward(queries, key_rows, value_rows, orders, inverse, allowed)
    branch = project(context, w_output) + b_output
    first_sum = inputs.astype(jnp.float32) + branch
    hidden = layer_norm(first_sum, gain_one, shift_one)
    hidden_low = hidden.astype(jnp.bfloat16)
    upper = project(hidden_low, w_upper) + b_upper
    active = jax.nn.gelu(upper, approximate=False).astype(jnp.bfloat16)
    feed = project(active, w_lower) + b_lower
    second_sum = hidden + feed
    result = layer_norm(second_sum, gain_two, shift_two)
    live = valid.astype(jnp.float32)[..., None]
    stats = jnp.stack(
        [
            jnp.sum(live * branch * branch),
            jnp.sum(live * feed * feed),
            jnp.sum(live * result * result),
        ]
    )
    cache = (
        inputs,
        queries,
        key_rows,
        value_rows,
        logsum,
        context,
        first_sum,
        hidden_low,
        upper,
        active,
        second_sum,
    )
    return (result, stats, cache)


def layer_backward(grad_out, params, cache, orders, segment, valid):
    (
        w_query,
        b_query,
        w_key,
        w_value,
        b_value,
        w_output,
        b_output,
        gain_one,
        shift_one,
        w_upper,
        b_upper,
        w_lower,
        b_lower,
        gain_two,
        shift_two,
    ) = params
    (
        inputs,
        queries,
        key_rows,
        value_rows,
        logsum,
        context,
        first_sum,
        hidden_low,
        upper,
        active,
        second_sum,
    ) = cache
    inverse = jnp.argsort(orders, axis=-1)
    allowed = cluster_mask(orders, segment, valid)
    _, norm_two = jax.vjp(layer_norm, second_sum, gain_two, shift_two)
    d_second, d_gain_two, d_shift_two = norm_two(grad_out)
    d_feed = d_second.astype(jnp.bfloat16)
    d_active = project_back(d_feed, w_lower)
    _, gelu_back = jax.vjp(partial(jax.nn.gelu, approximate=False), upper)
    d_upper = gelu_back(d_active)[0].astype(jnp.bfloat16)
    d_hidden = d_second + project_back(d_upper, w_upper)
    _, norm_one = jax.vjp(layer_norm, first_sum, gain_one, shift_one)
    d_first, d_gain_one, d_shift_one = norm_one(d_hidden)
    d_branch = d_first.astype(jnp.bfloat16)
    d_context = project_back(d_branch, w_output).astype(jnp.bfloat16)
    d_query, d_key, d_value = attend_backward(
        queries, key_rows, value_rows, orders, inverse, allowed, logsum, d_context
    )
    d_inputs = (
        d_first
        + project_back(d_query, w_query)
        + project_back(d_key, w_key)
        + project_back(d_value, w_value)
    )
    terms = (
        inputs,
        d_query,
        d_key,
        d_value,
        context,
        d_branch,
        hidden_low,
        d_upper,
        active,
        d_feed,
    )
    norm_grads = (d_gain_one, d_shift_one, d_gain_two, d_shift_two)
    return (d_inputs, terms, norm_grads)


def collect(terms, norm_grads):
    inputs, d_query, d_key, d_value, context, d_branch, hidden_low, d_upper, active, d_feed = terms

    def outer(left, right):
        return jnp.einsum("rsd,rse->de", left, right, preferred_element_type=jnp.float32)

    def column_sum(field):
        return jnp.sum(field.astype(jnp.float32), axis=(0, 1))

    d_gain_one, d_shift_one, d_gain_two, d_shift_two = norm_grads
    return (
        outer(inputs, d_query),
        column_sum(d_query),
        outer(inputs, d_key),
        outer(inputs, d_value),
        column_sum(d_value),
        outer(context, d_branch),
        column_sum(d_branch),
        d_gain_one,
        d_shift_one,
        outer(hidden_low, d_upper),
        column_sum(d_upper),
        outer(active, d_feed),
        column_sum(d_feed),
        d_gain_two,
        d_shift_two,
    )


def run_if(active_flag, compute):
    probe = compute()
    empty = jax.tree.map(lambda leaf: jnp.zeros(leaf.shape, leaf.dtype), probe)
    return lax.cond(active_flag, compute, lambda: empty)


def sum_end(parts):
    return (
        lax.psum_scatter(parts[0], "dp", scatter_dimension=0, tiled=True),
        lax.psum_scatter(parts[1], "dp", scatter_dimension=0, tiled=True),
        lax.psum_scatter(parts[2], "dp", scatter_dimension=0, tiled=True),
        lax.psum_scatter(parts[3], "dp", scatter_dimension=0, tiled=True),
        lax.psum_scatter(parts[4], "dp", scatter_dimension=0, tiled=True),
        lax.psum_scatter(parts[5], "dp", scatter_dimension=0, tiled=True),
        lax.psum_scatter(parts[6], "dp", scatter_dimension=0, tiled=True),
        lax.psum_scatter(parts[7], "dp", scatter_dimension=0, tiled=True),
        lax.psum_scatter(parts[8], "dp", scatter_dimension=0, tiled=True),
        lax.psum_scatter(parts[9], "dp", scatter_dimension=0, tiled=True),
        lax.psum_scatter(parts[10], "dp", scatter_dimension=0, tiled=True),
        lax.psum_scatter(parts[11], "dp", scatter_dimension=0, tiled=True),
        lax.psum_scatter(parts[12], "dp", scatter_dimension=0, tiled=True),
        lax.psum_scatter(parts[13], "dp", scatter_dimension=0, tiled=True),
        lax.psum_scatter(parts[14], "dp", scatter_dimension=0, tiled=True),
    )


def add_all(running, fresh):
    return tuple((total + extra for total, extra in zip(running, fresh)))


def take_rows(array, index, count):
    return lax.dynamic_slice_in_dim(array, index * count, count, 0)


def on_device(
    tokens,
    cotangent,
    segment_ids,
    valid_mask,
    cluster_perm,
    query_weight,
    query_bias,
    key_weight,
    value_weight,
    value_bias,
    output_weight,
    output_bias,
    attention_gain,
    attention_shift,
    up_weight,
    up_bias,
    down_weight,
    down_bias,
    final_gain,
    final_shift,
):
    section_index = lax.axis_index("section")
    raw_params = (
        query_weight,
        query_bias,
        key_weight,
        value_weight,
        value_bias,
        output_weight,
        output_bias,
        attention_gain,
        attention_shift,
        up_weight,
        up_bias,
        down_weight,
        down_bias,
        final_gain,
        final_shift,
    )
    params = tuple(
        (tensor[0].astype(jnp.float32) if tensor.ndim == 2 else tensor[0] for tensor in raw_params)
    )
    model_width = tokens.shape[1]
    local_rows = segment_ids.shape[0]
    batch_rows = local_rows // MICRO
    token_rows = tokens.reshape(local_rows, SEQ, model_width)
    seed_rows = cotangent.reshape(local_rows, SEQ, model_width)
    orders_all = cluster_perm[0]
    received = jnp.zeros((batch_rows, SEQ, model_width), jnp.bfloat16)
    layer_out = jnp.zeros((local_rows, SEQ, model_width), jnp.bfloat16)
    stats = jnp.zeros((3,), jnp.float32)
    caches = []
    for step_index in range(MICRO + 1):
        micro_index = step_index - section_index
        active_flag = (micro_index >= 0) & (micro_index < MICRO)
        slot_index = jnp.clip(micro_index, 0, MICRO - 1)
        inputs = jnp.where(
            section_index == 0, take_rows(token_rows, slot_index, batch_rows), received
        )
        orders = take_rows(orders_all, slot_index, batch_rows)
        segment = take_rows(segment_ids, slot_index, batch_rows)
        valid = take_rows(valid_mask, slot_index, batch_rows)
        result, part_stats, cache = run_if(
            active_flag, lambda: layer_forward(inputs, params, orders, segment, valid)
        )
        stats = stats + part_stats
        caches.append(cache)
        sent = result.astype(jnp.bfloat16)
        placed = lax.dynamic_update_slice_in_dim(layer_out, sent, slot_index * batch_rows, 0)
        layer_out = jnp.where(active_flag & (section_index == 1), placed, layer_out)
        if step_index < MICRO:
            received = shifted(sent, "section", 1)
    stacked = jax.tree.map(lambda *pieces: jnp.stack(pieces), *caches)
    running = tuple((jnp.zeros(tensor.shape, jnp.float32) for tensor in params))
    incoming = jnp.zeros((batch_rows, SEQ, model_width), jnp.bfloat16)
    input_grads = jnp.zeros((local_rows, SEQ, model_width), jnp.bfloat16)
    for step_index in range(MICRO + 1):
        micro_index = step_index - 1 + section_index
        active_flag = (micro_index >= 0) & (micro_index < MICRO)
        slot_index = jnp.clip(micro_index, 0, MICRO - 1)
        cache_slot = jnp.clip(step_index - 1 + 2 * section_index, 0, MICRO)
        cache = jax.tree.map(lambda stack_item: stack_item[cache_slot], stacked)
        seed = take_rows(seed_rows, slot_index, batch_rows)
        grad_out = jnp.where(
            section_index == 1, seed.astype(jnp.float32), incoming.astype(jnp.float32)
        )
        orders = take_rows(orders_all, slot_index, batch_rows)
        segment = take_rows(segment_ids, slot_index, batch_rows)
        valid = take_rows(valid_mask, slot_index, batch_rows)
        d_inputs, terms, norm_grads = run_if(
            active_flag, lambda: layer_backward(grad_out, params, cache, orders, segment, valid)
        )
        fresh = run_if(active_flag, lambda: collect(terms, norm_grads))
        running = add_all(running, fresh)
        sent = d_inputs.astype(jnp.bfloat16)
        placed = lax.dynamic_update_slice_in_dim(input_grads, sent, slot_index * batch_rows, 0)
        input_grads = jnp.where(active_flag & (section_index == 0), placed, input_grads)
        if step_index < MICRO:
            incoming = shifted(sent, "section", -1)
    running = sum_end(running)
    count = jnp.sum(valid_mask.astype(jnp.float32))
    totals = lax.psum((stats, count), "dp")
    root_means = jnp.sqrt(totals[0] / (totals[1] * model_width))[None, :]
    half_width = model_width // 2
    grads_flat = input_grads.reshape(local_rows * SEQ, model_width)
    output_flat = layer_out.reshape(local_rows * SEQ, model_width)
    outgoing = jnp.where(
        section_index == 0, grads_flat[:, half_width:], output_flat[:, :half_width]
    )
    arrived = swapped(outgoing, "section", 0)
    block_part = jnp.where(section_index == 0, arrived, output_flat[:, half_width:])
    grad_part = jnp.where(section_index == 0, grads_flat[:, :half_width], arrived)
    return (block_part, grad_part) + tuple((share[None] for share in running)) + (root_means,)


def solution(mesh):
    return jax.shard_map(
        on_device,
        mesh=mesh,
        in_specs=(
            P("dp", None),
            P("dp", None),
            P("dp", None),
            P("dp", None),
            P("section", "dp", None, None),
            P("section", None, None),
            P("section", None),
            P("section", None, None),
            P("section", None, None),
            P("section", None),
            P("section", None, None),
            P("section", None),
            P("section", None),
            P("section", None),
            P("section", None, None),
            P("section", None),
            P("section", None, None),
            P("section", None),
            P("section", None),
            P("section", None),
        ),
        out_specs=(
            P("dp", "section"),
            P("dp", "section"),
            P("section", "dp", None),
            P("section", "dp"),
            P("section", "dp", None),
            P("section", "dp", None),
            P("section", "dp"),
            P("section", "dp", None),
            P("section", "dp"),
            P("section", "dp"),
            P("section", "dp"),
            P("section", "dp", None),
            P("section", "dp"),
            P("section", "dp", None),
            P("section", "dp"),
            P("section", "dp"),
            P("section", "dp"),
            P("section", None),
        ),
        check_vma=False,
    )
```

profile of v0, /device:TPU:0, one launch (start us, length us, event | category | flops | bytes accessed | tf_op | source)
XLA Modules:
  0.0 3467.2 jit_solution(15860979967900258134)
XLA Ops:
  12.7 439.7 %conditional.9 = (f32[3]{0:T(128)S(1)}, bf16[1,512,768]{2,1,0:T(8,128)(2,1)}, bf16[1,1,512,768]{3,2,1,0:T(8,128)(2,1)S(1)}, f32[1,1,12,4,128,1]{4,3,2,5,1,0:T(4,...) conditional(s32[]{:T(128)} %convert_element_type.684, ...), branch_computations={%region_0.1_spmd, %region_1.14_spmd} | conditional | flops 7591783936 | bytes 148217376 | solution.py:284
  15.6 48.9 %gather_fusion.1 = s32[6144]{0:T(1024)S(1)} fusion(s32[12,512]{1,0:T(8,128)S(1)} %broadcast.3927, s32[6144]{0:T(1024)S(1)} %reshape.4002), kind=kCustom, calls=%fused_computation.3.clone | custom fusion | bytes 98304 | tf_op jit(solution)/shard_map/cond/branch_1_fun/jit(take_along_axis)/gather | solution.py:65
  64.6 48.9 %gather_fusion = s32[6144]{0:T(1024)S(1)} fusion(s32[12,512]{1,0:T(8,128)S(1)} %broadcast.3926, s32[6144]{0:T(1024)S(1)} %reshape.4002), kind=kCustom, calls=%fused_computation.clone | custom fusion | bytes 98304 | tf_op jit(solution)/shard_map/cond/branch_1_fun/jit(take_along_axis)/gather | solution.py:62
  120.8 60.4 %gather_fusion.4 = bf16[6144,64]{1,0:T(8,128)(2,1)} fusion(bf16[12,512,64]{2,1,0:T(8,128)(2,1)S(1)} %bitcast.1288, s32[6144]{0:T(1024)S(1)} %reshape.4014), kind=kCustom, calls=%fused_computation.15.clone | custom fusion | bytes 1622016 | tf_op jit(solution)/shard_map/cond/branch_1_fun/jit(take_along_axis)/gather | solution.py:46
  188.6 60.4 %gather_fusion.3 = bf16[6144,64]{1,0:T(8,128)(2,1)} fusion(bf16[12,512,64]{2,1,0:T(8,128)(2,1)S(1)} %bitcast.1300, s32[6144]{0:T(1024)S(1)} %reshape.4014), kind=kCustom, calls=%fused_computation.14.clone | custom fusion | bytes 1622016 | tf_op jit(solution)/shard_map/cond/branch_1_fun/jit(take_along_axis)/gather | solution.py:46
  256.4 60.4 %gather_fusion.2 = bf16[6144,64]{1,0:T(8,128)(2,1)} fusion(bf16[12,512,64]{2,1,0:T(8,128)(2,1)S(1)} %bitcast.1294, s32[6144]{0:T(1024)S(1)} %reshape.4014), kind=kCustom, calls=%fused_computation.1.clone | custom fusion | bytes 1622016 | tf_op jit(solution)/shard_map/cond/branch_1_fun/jit(take_along_axis)/gather | solution.py:46
  347.2 60.4 %gather_fusion.5 = bf16[6144,64]{1,0:T(8,128)(2,1)} fusion(bf16[12,512,64]{2,1,0:T(8,128)(2,1)S(1)} %bitcast.1282, s32[6144]{0:T(1024)S(1)} %reshape.4032), kind=kCustom, calls=%fused_computation.16.clone | custom fusion | bytes 1622016 | tf_op jit(solution)/shard_map/cond/branch_1_fun/jit(take_along_axis)/gather | solution.py:53
  483.9 435.0 %conditional.10 = (f32[3]{0:T(128)S(1)}, bf16[1,512,768]{2,1,0:T(8,128)(2,1)}, bf16[1,1,512,768]{3,2,1,0:T(8,128)(2,1)S(1)}, f32[1,1,12,4,128,1]{4,3,2,5,1,0:T(4...) conditional(s32[]{:T(128)} %convert_element_type.703, ...), branch_computations={%region_12.15_spmd, %region_13.26_spmd} | conditional | flops 7591783936 | bytes 168664704 | solution.py:284
  485.4 48.9 %gather_fusion.7 = s32[6144]{0:T(1024)S(1)} fusion(s32[12,512]{1,0:T(8,128)S(1)} %broadcast.3929, s32[6144]{0:T(1024)S(1)} %reshape.4038), kind=kCustom, calls=%fused_computation.5.clone | custom fusion | bytes 98304 | tf_op jit(solution)/shard_map/cond/branch_1_fun/jit(take_along_axis)/gather | solution.py:65
  534.3 48.9 %gather_fusion.6 = s32[6144]{0:T(1024)S(1)} fusion(s32[12,512]{1,0:T(8,128)S(1)} %broadcast.3928, s32[6144]{0:T(1024)S(1)} %reshape.4038), kind=kCustom, calls=%fused_computation.4.clone | custom fusion | bytes 98304 | tf_op jit(solution)/shard_map/cond/branch_1_fun/jit(take_along_axis)/gather | solution.py:62
  590.6 60.4 %gather_fusion.10 = bf16[6144,64]{1,0:T(8,128)(2,1)} fusion(bf16[12,512,64]{2,1,0:T(8,128)(2,1)S(1)} %bitcast.1289, s32[6144]{0:T(1024)S(1)} %reshape.4050), kind=kCustom, calls=%fused_computation.19.clone | custom fusion | bytes 1622016 | tf_op jit(solution)/shard_map/cond/branch_1_fun/jit(take_along_axis)/gather | solution.py:46
  658.4 60.4 %gather_fusion.9 = bf16[6144,64]{1,0:T(8,128)(2,1)} fusion(bf16[12,512,64]{2,1,0:T(8,128)(2,1)S(1)} %bitcast.1301, s32[6144]{0:T(1024)S(1)} %reshape.4050), kind=kCustom, calls=%fused_computation.18.clone | custom fusion | bytes 1622016 | tf_op jit(solution)/shard_map/cond/branch_1_fun/jit(take_along_axis)/gather | solution.py:46
  726.2 60.4 %gather_fusion.8 = bf16[6144,64]{1,0:T(8,128)(2,1)} fusion(bf16[12,512,64]{2,1,0:T(8,128)(2,1)S(1)} %bitcast.1295, s32[6144]{0:T(1024)S(1)} %reshape.4050), kind=kCustom, calls=%fused_computation.17.clone | custom fusion | bytes 1622016 | tf_op jit(solution)/shard_map/cond/branch_1_fun/jit(take_along_axis)/gather | solution.py:46
  816.9 60.4 %gather_fusion.11 = bf16[6144,64]{1,0:T(8,128)(2,1)} fusion(bf16[12,512,64]{2,1,0:T(8,128)(2,1)S(1)} %bitcast.1283, s32[6144]{0:T(1024)S(1)} %reshape.4068), kind=kCustom, calls=%fused_computation.20.clone | custom fusion | bytes 1622016 | tf_op jit(solution)/shard_map/cond/branch_1_fun/jit(take_along_axis)/gather | solution.py:53
  1010.5 883.5 %collective-permute-done.2 = bf16[1,512,768]{2,1,0:T(8,128)(2,1)S(1)} collective-permute-done((bf16[1,512,768]{2,1,0:T(8,128)(2,1)}, bf16[1,512,768]{2,1,0:T(8,128)(2,1)S(1)}, u32[]{:S(2)}, u32[]{:S(2)}) %collective-permute-start.2) | collective-permute-done | bytes 786464 | tf_op jit(solution)/shard_map/ppermute | solution.py:17
  1894.1 487.0 %conditional.13 = (bf16[1,512,768]{2,1,0:T(8,128)(2,1)}, bf16[1,512,768]{1,2,0:T(8,128)(2,1)}, bf16[1,512,768]{1,2,0:T(8,128)(2,1)}, bf16[1,512,768]{1,2,0:T(8,1...) conditional(s32[]{:T(128)} %convert_element_type.706, ...), branch_computations={%region_52.56_spmd, %region_53.71_spmd} | conditional | flops 7899281408 | bytes 280228672 | solution.py:284
  1939.1 32.3 gather_fusion.31
  2089.0 48.9 %gather_fusion.28 = s32[6144]{0:T(1024)S(1)} fusion(s32[12,512]{1,0:T(8,128)S(1)} %broadcast.3935, s32[6144]{0:T(1024)S(1)} %reshape.4164), kind=kCustom, calls=%fused_computation.11.clone | custom fusion | bytes 98304 | tf_op jit(solution)/shard_map/cond/branch_1_fun/jit(take_along_axis)/gather | solution.py:65
  2138.0 48.9 %gather_fusion.27 = s32[6144]{0:T(1024)S(1)} fusion(s32[12,512]{1,0:T(8,128)S(1)} %broadcast.3934, s32[6144]{0:T(1024)S(1)} %reshape.4164), kind=kCustom, calls=%fused_computation.10.clone | custom fusion | bytes 98304 | tf_op jit(solution)/shard_map/cond/branch_1_fun/jit(take_along_axis)/gather | solution.py:62
  2211.6 60.4 %gather_fusion.35 = bf16[6144,64]{1,0:T(8,128)(2,1)} fusion(bf16[12,512,64]{2,1,0:T(8,128)(2,1)S(1)} %bitcast.1277, s32[6144]{0:T(1024)S(1)} %reshape.4200), kind=kCustom, calls=%fused_computation.41.clone | custom fusion | bytes 1622016 | tf_op jit(solution)/shard_map/cond/branch_1_fun/jit(take_along_axis)/gather | solution.py:53
  2274.5 60.4 %gather_fusion.34 = bf16[6144,64]{1,0:T(8,128)(2,1)} fusion(bf16[12,512,64]{2,1,0:T(8,128)(2,1)S(1)} %bitcast.1286, s32[6144]{0:T(1024)S(1)} %reshape.4200), kind=kCustom, calls=%fused_computation.40.clone | custom fusion | bytes 1622016 | tf_op jit(solution)/shard_map/cond/branch_1_fun/jit(take_along_axis)/gather | solution.py:53
  2433.2 489.8 %conditional.14 = (bf16[1,512,768]{2,1,0:T(8,128)(2,1)}, bf16[1,512,768]{1,2,0:T(8,128)(2,1)}, bf16[1,512,768]{1,2,0:T(8,128)(2,1)}, bf16[1,512,768]{1,2,0:T(8,1...) conditional(s32[]{:T(128)} %convert_element_type.709, ...), branch_computations={%region_68.72_spmd, %region_69.87_spmd} | conditional | flops 7899281408 | bytes 288215936 | solution.py:284
  2630.9 48.9 %gather_fusion.37 = s32[6144]{0:T(1024)S(1)} fusion(s32[12,512]{1,0:T(8,128)S(1)} %broadcast.3937, s32[6144]{0:T(1024)S(1)} %reshape.4218), kind=kCustom, calls=%fused_computation.13.clone | custom fusion | bytes 98304 | tf_op jit(solution)/shard_map/cond/branch_1_fun/jit(take_along_axis)/gather | solution.py:65
  2679.9 48.9 %gather_fusion.36 = s32[6144]{0:T(1024)S(1)} fusion(s32[12,512]{1,0:T(8,128)S(1)} %broadcast.3936, s32[6144]{0:T(1024)S(1)} %reshape.4218), kind=kCustom, calls=%fused_computation.12.clone | custom fusion | bytes 98304 | tf_op jit(solution)/shard_map/cond/branch_1_fun/jit(take_along_axis)/gather | solution.py:62
  2753.5 60.3 %gather_fusion.44 = bf16[6144,64]{1,0:T(8,128)(2,1)} fusion(bf16[12,512,64]{2,1,0:T(8,128)(2,1)S(1)} %bitcast.1278, s32[6144]{0:T(1024)S(1)} %reshape.4254), kind=kCustom, calls=%fused_computation.44.clone | custom fusion | bytes 1622016 | tf_op jit(solution)/shard_map/cond/branch_1_fun/jit(take_along_axis)/gather | solution.py:53
  2816.4 60.4 %gather_fusion.43 = bf16[6144,64]{1,0:T(8,128)(2,1)} fusion(bf16[12,512,64]{2,1,0:T(8,128)(2,1)S(1)} %bitcast.1287, s32[6144]{0:T(1024)S(1)} %reshape.4254), kind=kCustom, calls=%fused_computation.43.clone | custom fusion | bytes 1622016 | tf_op jit(solution)/shard_map/cond/branch_1_fun/jit(take_along_axis)/gather | solution.py:53
  2923.0 33.4 conditional.17
  3025.9 60.9 %all-reduce.9 = (f32[768]{0:T(1024)S(1)}, f32[768]{0:T(1024)S(1)}, f32[768]{0:T(1024)S(1)}, f32[768]{0:T(1024)S(1)}, f32[768]{0:T(1024)S(1)}, /*index=5*/f32[307...) all-reduce(f32[768]{0:T(1024)S(1)} %add_add_fusion.20, ...), channel_id=3, replica_groups=mesh['section'=2,'dp'=16] {'dp'}, use_global_device_ids=true, to_apply=%region_106.110.clone | all-reduce | flops 9220 | bytes 73760
  3095.7 64.3 %reduce-scatter.11.cloned.1.call-done = f32[48,768]{1,0:T(8,128)} async-done(((f32[768,768]{1,0:T(8,128)}), f32[48,768]{1,0:T(8,128)}) %reduce-scatter.11.cloned.1.call-update) | async-done | bytes 147472 | tf_op jit(solution)/shard_map/reduce_scatter | solution.py:292
  3160.0 66.7 %reduce-scatter.13.cloned.1.call-done = f32[48,768]{1,0:T(8,128)} async-done(((f32[768,768]{1,0:T(8,128)}), f32[48,768]{1,0:T(8,128)}) %reduce-scatter.13.cloned.1.call-update) | async-done | bytes 147472 | tf_op jit(solution)/shard_map/reduce_scatter | solution.py:294
  3226.8 115.8 %reduce-scatter.15.cloned.1.call-done = f32[48,3072]{1,0:T(8,128)} async-done(((f32[768,3072]{1,0:T(8,128)}), f32[48,3072]{1,0:T(8,128)}) %reduce-scatter.15.cloned.1.call-update) | async-done | bytes 589840 | tf_op jit(solution)/shard_map/reduce_scatter | solution.py:298
  3342.6 117.0 %reduce-scatter.17.cloned.1.call-done = f32[192,768]{1,0:T(8,128)} async-done(((f32[3072,768]{1,0:T(8,128)}), f32[192,768]{1,0:T(8,128)}) %reduce-scatter.17.cloned.1.call-update) | async-done | bytes 589840 | tf_op jit(solution)/shard_map/reduce_scatter | solution.py:300
  (713 shorter events, 1059.7 us)
Async XLA Ops:
  11.7 1882.4 %copy-start.87 = (f32[768]{0:T(1024)}, f32[768]{0:T(1024)S(1)}, u32[]{:S(2)}) copy-start(f32[768]{0:T(1024)S(1)} %get-tuple-element.2719) | copy-start | bytes 9220
  12.7 332.9 %sort.92.cloned.1.call-start = ((), (), s32[]{:S(2)}) async-start(), calls=%async_computation.12 | async-start | bytes 196640 | tf_op jit(solution)/shard_map/cond/branch_1_fun/jit(argsort)/sort | solution.py:147
  15.6 48.9 %copy-start.92 = (s32[1,12,512]{2,1,0:T(8,128)S(1)}, s32[1,12,512]{2,1,0:T(8,128)}, u32[]{:S(2)}) copy-start(s32[1,12,512]{2,1,0:T(8,128)} %get-tuple-element.2556) | copy-start | bytes 73732 | tf_op jit(solution)/shard_map/cond
  64.6 50.5 %copy-start.32 = (bf16[768,768]{1,0:T(8,128)(2,1)S(1)}, bf16[768,768]{1,0:T(8,128)(2,1)}, u32[]{:S(2)}) copy-start(bf16[768,768]{1,0:T(8,128)(2,1)} %get-tuple-element.1312) | copy-start | bytes 3538948 | tf_op jit(solution)/shard_map/cond
  115.1 318.9 %copy-start.24 = (bf16[1,512,768]{2,1,0:T(8,128)(2,1)}, bf16[1,512,768]{2,1,0:T(8,128)(2,1)S(1)}, u32[]{:S(2)}) copy-start(bf16[1,512,768]{2,1,0:T(8,128)(2,1)S(1)} %dynamic-slice_select_fusion) | copy-start | bytes 2359300 | tf_op jit(solution)/shard_map/cond
  412.1 21.8 slice-start.6
  452.5 31.4 collective-permute-start
  483.9 331.4 %sort.94.cloned.1.call-start = ((), (), s32[]{:S(2)}) async-start(), calls=%async_computation.13 | async-start | bytes 196640 | tf_op jit(solution)/shard_map/cond/branch_1_fun/jit(argsort)/sort | solution.py:147
  485.4 48.9 %copy-start.93 = (s32[1,12,512]{2,1,0:T(8,128)S(1)}, s32[1,12,512]{2,1,0:T(8,128)}, u32[]{:S(2)}) copy-start(s32[1,12,512]{2,1,0:T(8,128)} %get-tuple-element.2564) | copy-start | bytes 73732 | tf_op jit(solution)/shard_map/cond
  584.8 317.5 %copy-start.26 = (bf16[1,512,768]{2,1,0:T(8,128)(2,1)}, bf16[1,512,768]{2,1,0:T(8,128)(2,1)S(1)}, u32[]{:S(2)}) copy-start(bf16[1,512,768]{2,1,0:T(8,128)(2,1)S(1)} %dynamic-slice_select_fusion.1) | copy-start | bytes 2359300 | tf_op jit(solution)/shard_map/cond
  881.9 20.4 slice-start.8
  919.0 24.7 collective-permute-start.1
  973.2 920.9 %copy-start.95 = (f32[3,1,12,4,128,1]{4,3,2,5,1,0:T(4,128)}, f32[3,1,12,4,128,1]{4,3,2,5,1,0:T(4,128)S(1)}, u32[]{:S(2)}) copy-start(f32[3,1,12,4,128,1]{4,3,2,5,1,0:T(4,128)S(1)} %constant_dynamic-update-slice_fusion.9) | copy-start | bytes 221188
  1009.2 884.8 %collective-permute-start.2 = (bf16[1,512,768]{2,1,0:T(8,128)(2,1)}, bf16[1,512,768]{2,1,0:T(8,128)(2,1)S(1)}, u32[]{:S(2)}, u32[]{:S(2)}) collective-permute-start(bf16[1,512,768]{2,1,0:T(8,128)(2,1)} %get-tuple-element.1678), channel_id=1, source_target_pairs={{16,0},{17,1},{18,2},{19,3},{20,4},{21,5},{22,6},{23,7},{24,8},{25... | collective-permute-start | bytes 2359304 | tf_op jit(solution)/shard_map/ppermute | solution.py:17
  1894.1 315.9 %sort.100.cloned.1.call-start = ((), (), s32[]{:S(2)}) async-start(), calls=%async_computation.16 | async-start | bytes 196640 | tf_op jit(solution)/shard_map/cond/branch_1_fun/jit(argsort)/sort | solution.py:214
  2089.0 48.9 %copy-start.91 = (s32[1,12,512]{2,1,0:T(8,128)S(1)}, s32[1,12,512]{2,1,0:T(8,128)}, u32[]{:S(2)}) copy-start(s32[1,12,512]{2,1,0:T(8,128)} %get-tuple-element.2589) | copy-start | bytes 73732 | tf_op jit(solution)/shard_map/cond
  2381.1 48.6 %collective-permute-start.3 = (bf16[1,512,768]{2,1,0:T(8,128)(2,1)}, bf16[1,512,768]{2,1,0:T(8,128)(2,1)}, u32[]{:S(2)}, u32[]{:S(2)}) collective-permute-start(bf16[1,512,768]{2,1,0:T(8,128)(2,1)} %get-tuple-element.1679), channel_id=1, source_target_pairs={{16,0},{17,1},{18,2},{19,3},{20,4},{21,5},{22,6},{23,7},{24,8},{25... | collective-permute-start | bytes 2359304 | tf_op jit(solution)/shard_map/ppermute | solution.py:17
  2393.0 40.1 %copy-start.37 = (pred[1,512,768]{2,1,0:T(8,128)(4,1)S(1)}, pred[1,512,768]{2,1,0:T(8,128)(4,1)}, u32[]{:S(2)}) copy-start(pred[1,512,768]{2,1,0:T(8,128)(4,1)} %copy-done.36) | copy-start | bytes 1179652
  2393.0 40.1 %copy-start.88 = (f32[768]{0:T(1024)S(1)}, f32[768]{0:T(1024)}, u32[]{:S(2)}) copy-start(f32[768]{0:T(1024)} %copy-done.87) | copy-start | bytes 9220
  2393.0 40.1 %copy-start.104 = (s32[2,512]{1,0:T(2,128)S(1)}, s32[2,512]{1,0:T(2,128)}, u32[]{:S(2)}) copy-start(s32[2,512]{1,0:T(2,128)} %param.47) | copy-start | bytes 12292
  2393.0 40.1 %copy-start.108 = (s32[2,512]{1,0:T(2,128)S(1)}, s32[2,512]{1,0:T(2,128)}, u32[]{:S(2)}) copy-start(s32[2,512]{1,0:T(2,128)} %param.46) | copy-start | bytes 12292
  2433.2 318.7 %sort.102.cloned.1.call-start = ((), (), s32[]{:S(2)}) async-start(), calls=%async_computation.17 | async-start | bytes 196640 | tf_op jit(solution)/shard_map/cond/branch_1_fun/jit(argsort)/sort | solution.py:214
  2445.9 20.6 slice-start.4
  2588.4 33.2 copy-start.109
  2630.9 48.9 %copy-start.89 = (s32[1,12,512]{2,1,0:T(8,128)S(1)}, s32[1,12,512]{2,1,0:T(8,128)}, u32[]{:S(2)}) copy-start(s32[1,12,512]{2,1,0:T(8,128)} %get-tuple-element.2598) | copy-start | bytes 73732 | tf_op jit(solution)/shard_map/cond
  2923.0 172.8 %reduce-scatter.7.cloned.1.call-start = ((), (), s32[]{:S(2)}) async-start(), calls=%async_computation.6 | async-start | bytes 2506752 | tf_op jit(solution)/shard_map/reduce_scatter | solution.py:289
  2963.5 132.2 %reduce-scatter.9.cloned.1.call-start = ((), (), s32[]{:S(2)}) async-start(), calls=%async_computation.7 | async-start | bytes 2506752 | tf_op jit(solution)/shard_map/reduce_scatter | solution.py:291
  2969.5 190.6 %reduce-scatter.11.cloned.1.call-start = ((), (), s32[]{:S(2)}) async-start(), calls=%async_computation.8 | async-start | bytes 2506752 | tf_op jit(solution)/shard_map/reduce_scatter | solution.py:292
  2975.6 251.2 %reduce-scatter.13.cloned.1.call-start = ((), (), s32[]{:S(2)}) async-start(), calls=%async_computation.9 | async-start | bytes 2506752 | tf_op jit(solution)/shard_map/reduce_scatter | solution.py:294
  2981.7 360.9 %reduce-scatter.15.cloned.1.call-start = ((), (), s32[]{:S(2)}) async-start(), calls=%async_computation.10 | async-start | bytes 10027008 | tf_op jit(solution)/shard_map/reduce_scatter | solution.py:298
  2996.9 462.8 %reduce-scatter.17.cloned.1.call-start = ((), (), s32[]{:S(2)}) async-start(), calls=%async_computation.11 | async-start | bytes 10027008 | tf_op jit(solution)/shard_map/reduce_scatter | solution.py:300
  3019.7 73.6 %collective-permute-start.4 = (bf16[1024,384]{1,0:T(8,128)(2,1)}, bf16[1024,384]{1,0:T(8,128)(2,1)}, u32[]{:S(2)}, u32[]{:S(2)}) collective-permute-start(bf16[1024,384]{1,0:T(8,128)(2,1)} %slice_select_fusion.2), channel_id=1, source_target_pairs={{0,16},{16,0},{1,17},{17,1},{2,18},{18,2},{3,19},{19,3},{4,20},{20... | collective-permute-start | bytes 2359304 | tf_op jit(solution)/shard_map/ppermute | solution.py:23
  (106 other events, 566.9 us)
Sparse Core Ops, SparseCore 0:
  16.5 17.1 sort.104.cloned.1.call-done
  487.8 17.1 sort.106.cloned.1.call-done
  1898.5 17.5 sort.112.cloned.1.call-done
  2437.3 17.3 sort.114.cloned.1.call-done
  (4 shorter events, 0.1 us)
Sparse Core Ops, SparseCore 1:
  2963.6 63.3 reduce-scatter.6
  3031.7 62.2 reduce-scatter.8
  3098.2 61.8 reduce-scatter.10
  3164.9 61.9 reduce-scatter.12
  3231.5 111.1 reduce-scatter.14
  3347.8 111.7 reduce-scatter.16
where the time goes:
time: 3480 us; the launch traced here: 3470 us
  local copies, waits for them, and re-layouts  1730 us (50%)
  waiting for transfers between devices  1250 us (36%)
  matrix products  220 us (6%)
  other arithmetic  168 us (5%)
  blocking collectives  60.9 us (2%)
    ppermute x4, waiting for transfers between devices, shifted(): return lax.ppermute(block, axis, route)  884 us
    gather x32, local copies, waits for them, and re-layouts, arrange(): picked = jnp.take_along_axis(head_split, orders[..., None], axis=2)  645 us
    gather x20, local copies, waits for them, and re-layouts, restore(): back_order = jnp.take_along_axis(flat_field, inverse[..., None], axis=2)  443 us
    gather x12, local copies, waits for them, and re-layouts, cluster_mask(): jnp.take_along_axis(jnp.broadcast_to(segment[:, None, :], orders.shape),...  196 us
    gather x8, local copies, waits for them, and re-layouts, cluster_mask(): jnp.take_along_axis(jnp.broadcast_to(valid[:, None, :], orders.shape), or...  196 us
    reduce_scatter x1, waiting for transfers between devices, sum_end(): lax.psum_scatter(parts[11], 'dp', scatter_dimension=0, tiled=True)  117 us
    reduce_scatter x1, waiting for transfers between devices, sum_end(): lax.psum_scatter(parts[9], 'dp', scatter_dimension=0, tiled=True)  116 us
  transfers between devices with their start and end apart: 11, of which 5 were waited for; matrix products, arithmetic and copies ran while one was open for 4% of the time, Pallas kernels for 0%

commit v1 on v0

v1 whole, which is shorter than its diff:
```python
from functools import partial

import jax
import jax.numpy as jnp
from jax import lax
from jax.experimental import pallas as pl
from jax.experimental.pallas import tpu as pltpu
from jax.sharding import PartitionSpec as P

HEAD_DIM = 64
CLUSTER = 128
SEQ = 512
LANES = 128
MIB = 1024 * 1024

BF16 = jnp.bfloat16
F32 = jnp.float32
LOG2E = 1.4426950408889634
SCALE = HEAD_DIM**-0.5
SCORE_SCALE = SCALE * LOG2E

NN = ((1,), (0,))
NT = ((1,), (1,))
TN = ((0,), (0,))

ANY = pl.BlockSpec(memory_space=pl.ANY)
WHOLE = pl.BlockSpec(memory_space=pltpu.VMEM)


def mm(left, right, dims):
    return lax.dot_general(left, right, (dims, ((), ())), preferred_element_type=F32)


class Copies:
    def __init__(self, sems):
        self.sems = sems
        self.used = 0

    def start(self, source, target):
        copy = pltpu.make_async_copy(source, target, self.sems.at[self.used])
        copy.start()
        self.used += 1
        return copy


def vec(ref):
    return ref[0:1, :].astype(F32)


SAVED = ("x", "qkv", "ctx", "lse", "kid", "qid", "n1", "r1", "hid", "act", "gp", "n2", "r2")


def saved_shapes(width, inner):
    return dict(
        x=((SEQ, width), BF16),
        qkv=((SEQ, 3 * width), BF16),
        ctx=((SEQ, width), BF16),
        lse=((16, SEQ), F32),
        kid=((SEQ, LANES), F32),
        qid=((16, SEQ), F32),
        n1=((SEQ, width), BF16),
        r1=((SEQ, LANES), F32),
        hid=((SEQ, width), BF16),
        act=((SEQ, inner), BF16),
        gp=((SEQ, inner), BF16),
        n2=((SEQ, width), BF16),
        r2=((SEQ, LANES), F32),
    )


def token_ids(row, heads, perm_ref, seg_ref, valid_ref):
    token = lax.broadcasted_iota(jnp.int32, (SEQ, LANES), 0)
    lane = lax.broadcasted_iota(jnp.int32, (SEQ, LANES), 1)
    clusters = jnp.zeros((SEQ, LANES), F32)
    for h in range(heads):
        places = perm_ref[0, row, h : h + 1, :]
        mine = jnp.zeros((SEQ, LANES), F32)
        for c in range(1, SEQ // CLUSTER):
            part = places[:, c * CLUSTER : (c + 1) * CLUSTER]
            mine = jnp.where(token == part, float(c), mine)
        column = jnp.sum(mine, axis=1, keepdims=True)
        clusters = jnp.where(lane == h, column, clusters)
    seg_row = seg_ref[row : row + 1, :].astype(F32)
    valid_row = valid_ref[row : row + 1, :].astype(F32)
    at = lax.broadcasted_iota(jnp.int32, (LANES, SEQ), 0)
    both = jnp.where(at == 0, seg_row, jnp.where(at == 1, valid_row, 0.0)).T
    live = both[:, 1:2]
    qid = clusters * 4.0 + both[:, 0:1]
    kid = jnp.where(live > 0.5, qid, -1.0)
    return kid, qid.T[0:16, :], live


def allowed_pairs(kid_column, qid_row):
    key = lax.broadcasted_iota(jnp.int32, (SEQ, SEQ), 0)
    query = lax.broadcasted_iota(jnp.int32, (SEQ, SEQ), 1)
    return (kid_column == qid_row) | (key == query)


def low_lanes():
    return lax.broadcasted_iota(jnp.int32, (SEQ, LANES), 1) < HEAD_DIM


def attend_pair(j, width, qkv, kid, qid, lse, ctx):
    low = low_lanes()
    lanes = slice(j * LANES, (j + 1) * LANES)
    query = qkv[:, j * LANES : (j + 1) * LANES]
    key = qkv[:, width + j * LANES : width + (j + 1) * LANES]
    value = qkv[:, 2 * width + j * LANES : 2 * width + (j + 1) * LANES]
    mixed = []
    for half in (0, 1):
        h = 2 * j + half
        own = low if half == 0 else ~low
        own_query = jnp.where(own, query, jnp.zeros_like(query))
        value_ones = jnp.where(own, value, jnp.ones_like(value))
        ok = allowed_pairs(kid[:, h : h + 1], qid[h : h + 1, :])
        scores = jnp.where(ok, mm(key, own_query, NT) * SCORE_SCALE, -1e30)
        top = jnp.max(scores, axis=0, keepdims=True)
        weights = jnp.exp2(scores - top)
        total = jnp.sum(weights, axis=0, keepdims=True)
        lse[h : h + 1, :] = top + jnp.log2(total)
        mixed.append(mm(weights.astype(BF16), value_ones, TN))
    sums = [pltpu.roll(part, HEAD_DIM, 1) for part in mixed]
    ctx[:, lanes] = (
        jnp.where(low, mixed[0], mixed[1]) / jnp.where(low, sums[0], sums[1])
    ).astype(BF16)


def normed(total):
    centre = total - jnp.mean(total, axis=-1, keepdims=True)
    spread = jnp.mean(centre * centre, axis=-1, keepdims=True)
    rate = lax.rsqrt(spread + 1e-05)
    return centre * rate, rate


ROW_BLOCK = 64


def over_rows(step):
    def body(i, carry):
        step(pl.ds(pl.multiple_of(i * ROW_BLOCK, ROW_BLOCK), ROW_BLOCK))
        return carry

    lax.fori_loop(0, SEQ // ROW_BLOCK, body, 0)


def over_tiles(size, tile, step):
    def body(i, carry):
        step(pl.ds(pl.multiple_of(i * tile, tile), tile))
        return carry

    lax.fori_loop(0, size // tile, body, 0)


def fold8(block):
    return jnp.sum(block.reshape(-1, 8, block.shape[-1]), axis=0)


def forward_kernel(section, row, x_row, n_alias, heads, *refs):
    (
        x_hbm,
        perm_ref,
        seg_ref,
        valid_ref,
        wq_hbm,
        bq_ref,
        wk_hbm,
        wv_hbm,
        bv_ref,
        wo_hbm,
        bo_ref,
        g1_ref,
        s1_ref,
        wu_hbm,
        bu_ref,
        wd_hbm,
        bd_ref,
        g2_ref,
        s2_ref,
    ) = refs[:19]
    refs = refs[19 + n_alias :]
    out = dict(zip(SAVED, refs[: len(SAVED)]))
    y_hbm, stats_hbm = refs[len(SAVED) : len(SAVED) + 2]
    refs = refs[len(SAVED) + 2 :]
    here = dict(zip(SAVED, refs[: len(SAVED)]))
    wqkv, wo, wu, wd, wide, feed, y_ref, stats, live_ref, sems = refs[len(SAVED) :]
    width = wo.shape[0]
    inner = wu.shape[1]

    @pl.when(lax.axis_index("section") == section)
    def _():
        copies = Copies(sems)
        get_x = copies.start(x_hbm.at[pl.ds(x_row * SEQ, SEQ), :], here["x"])
        get_qkv = [
            copies.start(w.at[0], wqkv.at[:, pl.ds(i * width, width)])
            for i, w in enumerate((wq_hbm, wk_hbm, wv_hbm))
        ]
        get_o = copies.start(wo_hbm.at[0], wo)
        get_u = copies.start(wu_hbm.at[0], wu)
        get_d = copies.start(wd_hbm.at[0], wd)
        puts = []

        def save(name):
            puts.append(copies.start(here[name], out[name]))

        kid, qid, live = token_ids(row, heads, perm_ref, seg_ref, valid_ref)
        here["kid"][...] = kid
        here["qid"][...] = qid
        live_ref[...] = jnp.broadcast_to(live, (SEQ, LANES))
        here["lse"][...] = jnp.zeros((16, SEQ), F32)
        stats[...] = jnp.zeros(stats.shape, F32)
        save("kid")
        save("qid")
        get_x.wait()
        save("x")
        xs = here["x"]
        qkv = here["qkv"]
        for i, bias in enumerate((bq_ref, None, bv_ref)):
            get_qkv[i].wait()
            part = pl.ds(i * width, width)
            value = mm(xs[...], wqkv[:, i * width : (i + 1) * width], NN)
            if bias is not None:
                value = value + vec(bias)
            qkv[:, part] = value.astype(BF16)
        save("qkv")
        for j in range(heads // 2):
            attend_pair(j, width, qkv, here["kid"], here["qid"], here["lse"], here["ctx"])
        save("lse")
        save("ctx")
        get_o.wait()
        wide[...] = mm(here["ctx"][...], wo[...], NN)

        def first_norm(rows):
            branch = wide[rows, :] + vec(bo_ref)
            alive = live_ref[rows, 0:1]
            stats[0:8, :] += fold8(branch * branch * alive)
            unit, rate = normed(xs[rows, :].astype(F32) + branch)
            hidden = unit * vec(g1_ref) + vec(s1_ref)
            here["n1"][rows, :] = unit.astype(BF16)
            here["r1"][rows, :] = jnp.broadcast_to(rate, (ROW_BLOCK, LANES))
            here["hid"][rows, :] = hidden.astype(BF16)
            wide[rows, :] = hidden

        over_rows(first_norm)
        save("n1")
        save("r1")
        save("hid")
        get_u.wait()

        def up(part):
            upper = mm(here["hid"][...], wu[:, part], NN) + bu_ref[0:1, part].astype(F32)
            half = 0.5 + 0.5 * lax.erf(upper * 0.5**0.5)
            bell = jnp.exp2(upper * upper * (-0.5 * LOG2E)) * 0.3989422804014327
            here["act"][:, part] = (upper * half).astype(BF16)
            here["gp"][:, part] = (half + upper * bell).astype(BF16)

        over_tiles(inner, inner // 4, up)
        save("act")
        save("gp")
        get_d.wait()
        feed[...] = mm(here["act"][...], wd[...], NN)

        def second_norm(rows):
            ffn = feed[rows, :] + vec(bd_ref)
            alive = live_ref[rows, 0:1]
            stats[8:16, :] += fold8(ffn * ffn * alive)
            unit, rate = normed(wide[rows, :] + ffn)
            result = unit * vec(g2_ref) + vec(s2_ref)
            stats[16:24, :] += fold8(result * result * alive)
            here["n2"][rows, :] = unit.astype(BF16)
            here["r2"][rows, :] = jnp.broadcast_to(rate, (ROW_BLOCK, LANES))
            y_ref[rows, :] = result.astype(BF16)

        over_rows(second_norm)
        puts.append(copies.start(y_ref, y_hbm))
        puts.append(copies.start(stats, stats_hbm))
        save("n2")
        save("r2")
        for put in puts:
            put.wait()


def forward(section, row, x, x_row, ids, params, saved):
    width = x.shape[1]
    inner = params[9].shape[2]
    heads = ids[0].shape[2]
    shapes = saved_shapes(width, inner)
    out_shape = [jax.ShapeDtypeStruct(*shapes[name]) for name in SAVED]
    out_shape += [
        jax.ShapeDtypeStruct((SEQ, width), BF16),
        jax.ShapeDtypeStruct((24, width), F32),
    ]
    param_specs = [ANY if p.ndim == 3 else WHOLE for p in params]
    old = [] if saved is None else list(saved)
    n_in = 4 + len(params)
    result = pl.pallas_call(
        partial(forward_kernel, section, row, x_row, len(old), heads),
        out_shape=out_shape,
        in_specs=[ANY, WHOLE, WHOLE, WHOLE] + param_specs + [ANY] * len(old),
        out_specs=[ANY] * len(out_shape),
        input_output_aliases={n_in + i: i for i in range(len(old))},
        scratch_shapes=[pltpu.VMEM(*shapes[name]) for name in SAVED]
        + [
            pltpu.VMEM((width, 3 * width), BF16),
            pltpu.VMEM((width, width), BF16),
            pltpu.VMEM((width, inner), BF16),
            pltpu.VMEM((inner, width), BF16),
            pltpu.VMEM((SEQ, width), F32),
            pltpu.VMEM((SEQ, width), F32),
            pltpu.VMEM((SEQ, width), BF16),
            pltpu.VMEM((24, width), F32),
            pltpu.VMEM((SEQ, LANES), F32),
            pltpu.SemaphoreType.DMA((24,)),
        ],
        compiler_params=pltpu.CompilerParams(vmem_limit_bytes=56 * MIB),
        cost_estimate=pl.CostEstimate(
            flops=2 * SEQ * (4 * width * width + 2 * width * inner) * 2,
            bytes_accessed=30 * MIB,
            transcendentals=0,
        ),
        name="layer_forward",
    )(x, *ids, *params, *old)
    return tuple(result[: len(SAVED)]), result[-2], result[-1]


GRADS = ("dffn", "dup", "dbr", "dqkv", "sums")
FROM_FORWARD = ("qkv", "ctx", "lse", "kid", "qid", "n1", "r1", "gp", "n2", "r2")
SUM_ROWS = ("gain2", "shift2", "bdown", "gain1", "shift1", "bout", "bq", "bv", "bup")


def grad_shapes(width, inner):
    return dict(
        dffn=((SEQ, width), BF16),
        dup=((SEQ, inner), BF16),
        dbr=((SEQ, width), BF16),
        dqkv=((SEQ, 3 * width), BF16),
        sums=((8 * len(SUM_ROWS), inner), F32),
    )


def attend_pair_back(j, width, qkv, dctx, kid, qid, lse, delta, dqkv):
    low = low_lanes()
    lanes = [slice(i * width + j * LANES, i * width + (j + 1) * LANES) for i in range(3)]
    query, key, value = (qkv[:, part] for part in lanes)
    d_out = dctx[:, lanes[0]]
    d_query, d_key, d_value = [], [], []
    for half in (0, 1):
        h = 2 * j + half
        own = low if half == 0 else ~low
        own_query = jnp.where(own, query, jnp.zeros_like(query))
        own_out = jnp.where(own, d_out, jnp.zeros_like(d_out))
        ok = allowed_pairs(kid[:, h : h + 1], qid[h : h + 1, :])
        scores = mm(key, own_query, NT) * SCORE_SCALE - lse[h : h + 1, :]
        weights = jnp.exp2(jnp.where(ok, scores, -1e30))
        d_weights = mm(value, own_out, NT)
        d_scores = (weights * (d_weights - delta[h : h + 1, :])).astype(BF16)
        d_value.append(mm(weights.astype(BF16), own_out, NN))
        d_key.append(mm(d_scores, own_query, NN))
        d_query.append(mm(d_scores, key, TN))
    dqkv[:, lanes[0]] = (jnp.where(low, d_query[0], d_query[1]) * SCALE).astype(BF16)
    dqkv[:, lanes[1]] = ((d_key[0] + d_key[1]) * SCALE).astype(BF16)
    dqkv[:, lanes[2]] = (d_value[0] + d_value[1]).astype(BF16)


def norm_back(grad, unit, rate, gain):
    scaled = grad * gain
    mean = jnp.mean(scaled, axis=-1, keepdims=True)
    along = jnp.mean(scaled * unit, axis=-1, keepdims=True)
    return (scaled - mean - unit * along) * rate


def backward_kernel(section, g_row, n_alias, heads, *refs):
    g_hbm = refs[0]
    wq_hbm, wk_hbm, wv_hbm, wo_hbm, wu_hbm, wd_hbm, g1_ref, g2_ref = refs[1:9]
    given = dict(zip(FROM_FORWARD, refs[9 : 9 + len(FROM_FORWARD)]))
    refs = refs[9 + len(FROM_FORWARD) + n_alias :]
    out = dict(zip(GRADS, refs[: len(GRADS)]))
    dx_hbm = refs[len(GRADS)]
    refs = refs[len(GRADS) + 1 :]
    here = dict(zip(FROM_FORWARD, refs[: len(FROM_FORWARD)]))
    refs = refs[len(FROM_FORWARD) :]
    made = dict(zip(GRADS, refs[: len(GRADS)]))
    wqkv, wo, wu, wd, g_ref, wide, dctx, delta, dx_ref, sems = refs[len(GRADS) :]
    width = wo.shape[0]
    inner = wu.shape[1]
    sums = made["sums"]

    def add_sum(name, value):
        at = 8 * SUM_ROWS.index(name)
        sums[at : at + 8, 0:width] += fold8(value)

    @pl.when(lax.axis_index("section") == section)
    def _():
        copies = Copies(sems)
        get_g = copies.start(g_hbm.at[pl.ds(g_row * SEQ, SEQ), :], g_ref)
        got = {}
        for name in ("n2", "r2"):
            got[name] = copies.start(given[name], here[name])
        get_d = copies.start(wd_hbm.at[0], wd)
        got["gp"] = copies.start(given["gp"], here["gp"])
        get_u = copies.start(wu_hbm.at[0], wu)
        for name in ("n1", "r1"):
            got[name] = copies.start(given[name], here[name])
        get_o = copies.start(wo_hbm.at[0], wo)
        for name in ("ctx", "lse", "kid", "qid", "qkv"):
            got[name] = copies.start(given[name], here[name])
        get_qkv = [
            copies.start(w.at[0], wqkv.at[:, pl.ds(i * width, width)])
            for i, w in enumerate((wq_hbm, wk_hbm, wv_hbm))
        ]
        puts = []

        def save(name):
            puts.append(copies.start(made[name], out[name]))

        sums[...] = jnp.zeros(sums.shape, F32)
        get_g.wait()
        got["n2"].wait()
        got["r2"].wait()

        def second_back(rows):
            grad = g_ref[rows, :].astype(F32)
            unit = here["n2"][rows, :].astype(F32)
            add_sum("gain2", grad * unit)
            add_sum("shift2", grad)
            d_second = norm_back(grad, unit, here["r2"][rows, 0:1], vec(g2_ref))
            wide[rows, :] = d_second
            low = d_second.astype(BF16)
            made["dffn"][rows, :] = low
            add_sum("bdown", low.astype(F32))

        over_rows(second_back)
        save("dffn")
        get_d.wait()
        got["gp"].wait()

        def up_back(part):
            d_act = mm(made["dffn"][...], wd[part, :], NT)
            low = (d_act * here["gp"][:, part].astype(F32)).astype(BF16)
            made["dup"][:, part] = low
            at = 8 * SUM_ROWS.index("bup")
            sums[at : at + 8, part] += fold8(low.astype(F32))

        over_tiles(inner, inner // 4, up_back)
        save("dup")
        get_u.wait()
        wide[...] += mm(made["dup"][...], wu[...], NT)
        got["n1"].wait()
        got["r1"].wait()

        def first_back(rows):
            grad = wide[rows, :]
            unit = here["n1"][rows, :].astype(F32)
            add_sum("gain1", grad * unit)
            add_sum("shift1", grad)
            d_first = norm_back(grad, unit, here["r1"][rows, 0:1], vec(g1_ref))
            wide[rows, :] = d_first
            low = d_first.astype(BF16)
            made["dbr"][rows, :] = low
            add_sum("bout", low.astype(F32))

        over_rows(first_back)
        save("dbr")
        get_o.wait()
        dctx[...] = mm(made["dbr"][...], wo[...], NT).astype(BF16)
        got["ctx"].wait()
        product = dctx[...].astype(F32) * here["ctx"][...].astype(F32)
        high = product.astype(BF16)
        rest = (product - high.astype(F32)).astype(BF16)
        of_head = (
            lax.broadcasted_iota(jnp.int32, (16, width), 1) // HEAD_DIM
            == lax.broadcasted_iota(jnp.int32, (16, width), 0)
        )
        pick = jnp.where(of_head, 1.0, 0.0).astype(BF16)
        delta[...] = mm(pick, high, NT) + mm(pick, rest, NT)
        for name in ("lse", "kid", "qid", "qkv"):
            got[name].wait()
        for j in range(heads // 2):
            attend_pair_back(
                j,
                width,
                here["qkv"],
                dctx,
                here["kid"],
                here["qid"],
                here["lse"],
                delta,
                made["dqkv"],
            )
        save("dqkv")
        for get in get_qkv:
            get.wait()

        def bias_sums(rows):
            add_sum("bq", made["dqkv"][rows, 0:width].astype(F32))
            add_sum("bv", made["dqkv"][rows, 2 * width : 3 * width].astype(F32))

        over_rows(bias_sums)
        save("sums")
        dx_ref[...] = (wide[...] + mm(made["dqkv"][...], wqkv[...], NT)).astype(BF16)
        puts.append(copies.start(dx_ref, dx_hbm))
        for put in puts:
            put.wait()


def backward(section, g, g_row, params, saved, grads):
    width = g.shape[1]
    inner = params[9].shape[2]
    heads = width // HEAD_DIM
    kept = dict(zip(SAVED, saved))
    shapes = saved_shapes(width, inner)
    out = grad_shapes(width, inner)
    wq, _, wk, wv, _, wo, _, g1, _, wu, _, wd, _, g2, _ = params
    out_shape = [jax.ShapeDtypeStruct(*out[name]) for name in GRADS]
    out_shape.append(jax.ShapeDtypeStruct((SEQ, width), BF16))
    old = [] if grads is None else list(grads)
    n_in = 9 + len(FROM_FORWARD)
    result = pl.pallas_call(
        partial(backward_kernel, section, g_row, len(old), heads),
        out_shape=out_shape,
        in_specs=[ANY] * 7 + [WHOLE] * 2 + [ANY] * (len(FROM_FORWARD) + len(old)),
        out_specs=[ANY] * len(out_shape),
        input_output_aliases={n_in + i: i for i in range(len(old))},
        scratch_shapes=[pltpu.VMEM(*shapes[name]) for name in FROM_FORWARD]
        + [pltpu.VMEM(*out[name]) for name in GRADS]
        + [
            pltpu.VMEM((width, 3 * width), BF16),
            pltpu.VMEM((width, width), BF16),
            pltpu.VMEM((width, inner), BF16),
            pltpu.VMEM((inner, width), BF16),
            pltpu.VMEM((SEQ, width), BF16),
            pltpu.VMEM((SEQ, width), F32),
            pltpu.VMEM((SEQ, width), BF16),
            pltpu.VMEM((16, SEQ), F32),
            pltpu.VMEM((SEQ, width), BF16),
            pltpu.SemaphoreType.DMA((24,)),
        ],
        compiler_params=pltpu.CompilerParams(vmem_limit_bytes=56 * MIB),
        cost_estimate=pl.CostEstimate(
            flops=2 * SEQ * (4 * width * width + 2 * width * inner) * 2,
            bytes_accessed=40 * MIB,
            transcendentals=0,
        ),
        name="layer_backward",
    )(g, wq, wk, wv, wo, wu, wd, g1, g2, *(kept[name] for name in FROM_FORWARD), *old)
    return tuple(result[: len(GRADS)]), result[-1]


def outer_kernel(n_rows, tile, split_left, *refs):
    lefts = refs[:n_rows]
    rights = refs[n_rows : 2 * n_rows]
    out_hbm = refs[2 * n_rows]
    left, right, out, sems = refs[2 * n_rows + 1 :]
    copies = Copies(sems)
    gets = [
        copies.start(ref, buf.at[pl.ds(i * SEQ, SEQ), :])
        for i in range(n_rows)
        for ref, buf in ((lefts[i], left), (rights[i], right))
    ]
    for get in gets:
        get.wait()

    size = left.shape[1] if split_left else right.shape[1]

    def body(i, carry):
        part = pl.ds(pl.multiple_of(i * tile, tile), tile)
        if split_left:
            out[part, :] = mm(left[:, part], right[...], TN).astype(BF16)
        else:
            out[:, part] = mm(left[...], right[:, part], TN).astype(BF16)
        return carry

    lax.fori_loop(0, size // tile, body, 0)
    put = copies.start(out, out_hbm)
    put.wait()


def outer(lefts, rights, tile, split_left):
    n_rows = len(lefts)
    rows, columns = lefts[0].shape[1], rights[0].shape[1]
    return pl.pallas_call(
        partial(outer_kernel, n_rows, tile, split_left),
        out_shape=jax.ShapeDtypeStruct((rows, columns), BF16),
        in_specs=[ANY] * (2 * n_rows),
        out_specs=ANY,
        scratch_shapes=[
            pltpu.VMEM((n_rows * SEQ, rows), BF16),
            pltpu.VMEM((n_rows * SEQ, columns), BF16),
            pltpu.VMEM((rows, columns), BF16),
            pltpu.SemaphoreType.DMA((2 * n_rows + 1,)),
        ],
        compiler_params=pltpu.CompilerParams(vmem_limit_bytes=48 * MIB),
        cost_estimate=pl.CostEstimate(
            flops=2 * n_rows * SEQ * rows * columns,
            bytes_accessed=2 * (n_rows * SEQ * (rows + columns) + rows * columns),
            transcendentals=0,
        ),
        name="weight_gradient",
    )(*lefts, *rights)


def scatter_sum(partial_sum):
    count = lax.axis_size("dp")
    if count != 16:
        total = lax.psum_scatter(partial_sum, "dp", scatter_dimension=0, tiled=True)
        return total.astype(F32)
    me = lax.axis_index("dp")
    core, x, z = me % 2, (me // 2) % 2, me // 4
    rows, columns = partial_sum.shape
    block = rows // count

    def pick(array, index):
        return lax.dynamic_index_in_dim(array, index, 1, keepdims=False)

    def halve(array, own, stride):
        pairs = [(d, d ^ stride) for d in range(count)]
        arrived = lax.ppermute(pick(array, 1 - own), "dp", pairs)
        return (pick(array, own).astype(F32) + arrived.astype(F32)).astype(BF16)

    held = halve(partial_sum.reshape(8, 2, block, columns), core, 1)
    held = halve(held.reshape(4, 2, block, columns), x, 2)

    def at(index):
        return lax.dynamic_index_in_dim(held, jnp.clip(index, 0, 3), 0, keepdims=False)

    rising = falling = None
    for step in range(3):
        up_pairs = [(d, d + 4) for d in range(12) if d // 4 <= step]
        down_pairs = [(d, d - 4) for d in range(4, 16) if 3 - d // 4 <= step]
        up = at(3 + z - step)
        down = at(step - 3 + z)
        if rising is not None:
            up = (up.astype(F32) + rising.astype(F32)).astype(BF16)
            down = (down.astype(F32) + falling.astype(F32)).astype(BF16)
        rising = lax.ppermute(up, "dp", up_pairs)
        falling = lax.ppermute(down, "dp", down_pairs)
    return at(z).astype(F32) + rising.astype(F32) + falling.astype(F32)


def on_device(
    tokens,
    cotangent,
    segment_ids,
    valid_mask,
    cluster_perm,
    *params,
):
    section = lax.axis_index("section")
    width = tokens.shape[1]
    inner = params[9].shape[2]
    ids = (cluster_perm, segment_ids, valid_mask)

    def hop(array, source, target):
        return lax.ppermute(array, "section", [(source, target)])

    def then(first, array):
        return lax.optimization_barrier((array, first))[0]

    kept0, y0, stats00 = forward(0, 0, tokens, 0, ids, params, None)
    in0 = hop(y0, 0, 1)
    kept1, y1, stats01 = forward(0, 1, tokens, 1, ids, params, None)
    in1 = hop(y1, 0, 1)
    kept0, out0, stats10 = forward(1, 0, in0, 0, ids, params, kept0)
    grads0, dx0 = backward(1, cotangent, 0, params, kept0, None)
    g0 = hop(dx0, 1, 0)
    kept1, out1, stats11 = forward(1, 1, in1, 0, ids, params, kept1)
    grads1, dx1 = backward(1, cotangent, 1, params, kept1, None)
    g1 = hop(dx1, 1, 0)
    grads0, dx0 = backward(0, g0, 0, params, kept0, grads0)
    grads1, dx1 = backward(0, g1, 0, params, kept1, grads1)

    a, b = dict(zip(SAVED, kept0)), dict(zip(SAVED, kept1))
    c, d = dict(zip(GRADS, grads0)), dict(zip(GRADS, grads1))

    def both(left, right, tile, split_left):
        return outer((a[left], b[left]), (c[right], d[right]), tile, split_left)

    w_down = scatter_sum(both("act", "dffn", width, True))
    w_up = scatter_sum(both("hid", "dup", width, False))
    w_out = scatter_sum(both("ctx", "dbr", width, False))
    w_qkv = scatter_sum(both("x", "dqkv", width, False))

    sums = (c["sums"] + d["sums"]).reshape(len(SUM_ROWS), 8, inner).sum(axis=1)
    first = section == 0
    stats = jnp.where(first, stats00 + stats01, stats10 + stats11)
    stats = stats.reshape(3, 8 * width).sum(axis=1)
    count = jnp.sum(valid_mask.astype(F32))
    small = jnp.concatenate(
        [sums[:8, :width].reshape(-1), sums[8], stats, jnp.broadcast_to(count, (1,))]
    )
    small = lax.psum(small, "dp")
    shares = lax.axis_size("dp")
    me = lax.axis_index("dp")

    def small_part(name):
        i = SUM_ROWS.index(name)
        size = inner if name == "bup" else width
        own = size // shares
        return lax.dynamic_slice_in_dim(small, i * width + me * own, own, 0)[None]

    base = 8 * width + inner
    root_means = jnp.sqrt(small[base : base + 3] / (small[base + 3] * width))[None, :]

    half = width // 2
    outputs = jnp.concatenate([out0, out1])
    input_grads = jnp.concatenate([dx0, dx1])
    outgoing = jnp.where(first, input_grads[:, half:], outputs[:, :half])
    arrived = lax.ppermute(outgoing, "section", [(0, 1), (1, 0)])
    block_part = jnp.where(first, arrived, outputs[:, half:])
    grad_part = jnp.where(first, input_grads[:, :half], arrived)
    return (
        block_part,
        grad_part,
        w_qkv[None, :, :width],
        small_part("bq"),
        w_qkv[None, :, width : 2 * width],
        w_qkv[None, :, 2 * width :],
        small_part("bv"),
        w_out[None],
        small_part("bout"),
        small_part("gain1"),
        small_part("shift1"),
        w_up[None],
        small_part("bup"),
        w_down[None],
        small_part("bdown"),
        small_part("gain2"),
        small_part("shift2"),
        root_means,
    )


def solution(mesh):
    by_layer = P("section", None)
    matrix = P("section", None, None)
    share = P("section", "dp")
    matrix_share = P("section", "dp", None)
    return jax.shard_map(
        on_device,
        mesh=mesh,
        in_specs=(
            P("dp", None),
            P("dp", None),
            P("dp", None),
            P("dp", None),
            P("section", "dp", None, None),
            matrix,
            by_layer,
            matrix,
            matrix,
            by_layer,
            matrix,
            by_layer,
            by_layer,
            by_layer,
            matrix,
            by_layer,
            matrix,
            by_layer,
            by_layer,
            by_layer,
        ),
        out_specs=(
            P("dp", "section"),
            P("dp", "section"),
            matrix_share,
            share,
            matrix_share,
            matrix_share,
            share,
            matrix_share,
            share,
            share,
            share,
            matrix_share,
            share,
            matrix_share,
            share,
            share,
            share,
            P("section", None),
        ),
        check_vma=False,
    )
```

time: 3480 us -> 483 us (0.14)
  the two profiles are of different devices: /device:TPU:0 before, /device:TPU:20 now
where the time goes in v1:
time: 483 us; the launch traced here: 474 us
  Pallas kernels  181 us (37%)
  waiting for transfers between devices  132 us (27%)
  starting transfers between devices  79.5 us (16%)
  blocking collectives  45 us (9%)
  local copies, waits for them, and re-layouts  18.4 us (4%)
  other arithmetic  15.4 us (3%)
    pallas_call x4, Pallas kernels, backward(): pl.pallas_call(partial(backward_kernel, section, g_row, len(old), heads),...  79.7 us
    pallas_call x4, Pallas kernels, forward(): pl.pallas_call(partial(forward_kernel, section, row, x_row, len(old), hea...  70.4 us
    ppermute x8, waiting for transfers between devices, halve(): arrived = lax.ppermute(pick(array, 1 - own), 'dp', pairs)  62.1 us
    psum x1, blocking collectives, on_device(): small = lax.psum(small, 'dp')  45 us
    ppermute x12, waiting for transfers between devices, scatter_sum(): falling = lax.ppermute(down, 'dp', down_pairs)  32.4 us
    pallas_call x4, Pallas kernels, outer(): pl.pallas_call(partial(outer_kernel, n_rows, tile, split_left), out_shape...  30.9 us
    ppermute x4, waiting for transfers between devices, hop(): return lax.ppermute(array, 'section', [(source, target)])  30.3 us
    ppermute x12, starting transfers between devices, scatter_sum(): falling = lax.ppermute(down, 'dp', down_pairs)  26.2 us
  transfers between devices with their start and end apart: 37, of which 16 were waited for; matrix products, arithmetic and copies ran while one was open for 5% of the time, Pallas kernels for 34%

profile of v1, /device:TPU:20, one launch (start us, length us, event | category | flops | bytes accessed | tf_op | source)
XLA Modules:
  0.0 473.7 jit_solution(15216160490355637547)
XLA Ops:
  2.1 8.9 %layer_forward.6 = (bf16[512,768]{1,0:T(8,128)(2,1)}, bf16[512,2304]{1,0:T(8,128)(2,1)}, bf16[512,768]{1,0:T(8,128)(2,1)}, f32[16,512]{1,0:T(8,128)}, f32[512,12...) custom-call(bf16[1024,768]{1,0:T(8,128)(2,1)} %refs_0_.6, ...), custom_call_target="tpu_custom_call" | custom-call | flops 14495514624 | bytes 31457280 | tf_op jit(solution)/shard_map/layer_forward/pallas_call | solution.py:295
  12.3 9.4 %layer_forward.4 = (bf16[512,768]{1,0:T(8,128)(2,1)}, bf16[512,2304]{1,0:T(8,128)(2,1)}, bf16[512,768]{1,0:T(8,128)(2,1)}, f32[16,512]{1,0:T(8,128)}, f32[512,12...) custom-call(bf16[1024,768]{1,0:T(8,128)(2,1)} %refs_0_.6, ...), custom_call_target="tpu_custom_call" | custom-call | flops 14495514624 | bytes 31457280 | tf_op jit(solution)/shard_map/layer_forward/pallas_call | solution.py:295
  23.7 24.0 %collective-permute-done.2.refs_0_ = bf16[512,768]{1,0:T(8,128)(2,1)S(1)} collective-permute-done((bf16[512,768]{1,0:T(8,128)(2,1)}, bf16[512,768]{1,0:T(8,128)(2,1)S(1)}, u32[]{:S(2)}, u32[]{:S(2)}) %collective-permute-start.2) | collective-permute-done | bytes 786464 | tf_op jit(solution)/shard_map/ppermute | solution.py:653
  48.6 26.0 %layer_forward.7 = (bf16[512,768]{1,0:T(8,128)(2,1)}, bf16[512,2304]{1,0:T(8,128)(2,1)}, bf16[512,768]{1,0:T(8,128)(2,1)}, f32[16,512]{1,0:T(8,128)}, f32[512,12...) custom-call(bf16[512,768]{1,0:T(8,128)(2,1)} %copy-done.26, ...), custom_call_target="tpu_custom_call", output_to_operand_aliasing={{0}: (19, {}), {1}: (20, {}), {2}: (21, {}), {3}: (22, {}),... | custom-call | flops 14495514624 | bytes 31457280 | tf_op jit(solution)/shard_map/layer_forward/pallas_call | solution.py:295
  74.7 30.8 %layer_backward.6 = (bf16[512,768]{1,0:T(8,128)(2,1)}, bf16[512,3072]{1,0:T(8,128)(2,1)}, bf16[512,768]{1,0:T(8,128)(2,1)}, bf16[512,2304]{1,0:T(8,128)(2,1)}, f...) custom-call(bf16[1024,768]{1,0:T(8,128)(2,1)} %refs_0_.7, bf16[1,768,768]{2,1,0:T(8,128)(2,1)} %refs_1_.11, ...), custom_call_target="tpu_custom_call" | custom-call | flops 14495514624 | bytes 41943040 | tf_op jit(solution)/shard_map/layer_backward/pallas_call | solution.py:517
  107.8 26.1 %layer_forward.5 = (bf16[512,768]{1,0:T(8,128)(2,1)}, bf16[512,2304]{1,0:T(8,128)(2,1)}, bf16[512,768]{1,0:T(8,128)(2,1)}, f32[16,512]{1,0:T(8,128)}, f32[512,12...) custom-call(bf16[512,768]{1,0:T(8,128)(2,1)} %copy-done.25, ...), custom_call_target="tpu_custom_call", output_to_operand_aliasing={{0}: (19, {}), {1}: (20, {}), {2}: (21, {}), {3}: (22, {}),... | custom-call | flops 14495514624 | bytes 31457280 | tf_op jit(solution)/shard_map/layer_forward/pallas_call | solution.py:295
  133.9 31.1 %layer_backward.4 = (bf16[512,768]{1,0:T(8,128)(2,1)}, bf16[512,3072]{1,0:T(8,128)(2,1)}, bf16[512,768]{1,0:T(8,128)(2,1)}, bf16[512,2304]{1,0:T(8,128)(2,1)}, f...) custom-call(bf16[1024,768]{1,0:T(8,128)(2,1)} %refs_0_.7, bf16[1,768,768]{2,1,0:T(8,128)(2,1)} %refs_1_.11, ...), custom_call_target="tpu_custom_call" | custom-call | flops 14495514624 | bytes 41943040 | tf_op jit(solution)/shard_map/layer_backward/pallas_call | solution.py:517
  169.6 7.5 %layer_backward.7 = (bf16[512,768]{1,0:T(8,128)(2,1)}, bf16[512,3072]{1,0:T(8,128)(2,1)}, bf16[512,768]{1,0:T(8,128)(2,1)}, bf16[512,2304]{1,0:T(8,128)(2,1)}, f...) custom-call(bf16[512,768]{1,0:T(8,128)(2,1)} %copy-done.27, ...), custom_call_target="tpu_custom_call", output_to_operand_aliasing={{0}: (19, {}), {1}: (20, {}), {2}: (21, {}), {3}: (22, {}),... | custom-call | flops 14495514624 | bytes 41943040 | tf_op jit(solution)/shard_map/layer_backward/pallas_call | solution.py:517
  177.1 6.3 %collective-permute-done.1.refs_0_ = bf16[512,768]{1,0:T(8,128)(2,1)S(1)} collective-permute-done((bf16[512,768]{1,0:T(8,128)(2,1)}, bf16[512,768]{1,0:T(8,128)(2,1)S(1)}, u32[]{:S(2)}, u32[]{:S(2)}) %collective-permute-start.1) | collective-permute-done | bytes 786464 | tf_op jit(solution)/shard_map/ppermute | solution.py:653
  184.3 10.2 %layer_backward.5 = (bf16[512,768]{1,0:T(8,128)(2,1)}, bf16[512,3072]{1,0:T(8,128)(2,1)}, bf16[512,768]{1,0:T(8,128)(2,1)}, bf16[512,2304]{1,0:T(8,128)(2,1)}, f...) custom-call(bf16[512,768]{1,0:T(8,128)(2,1)} %copy-done.28, ...), custom_call_target="tpu_custom_call", output_to_operand_aliasing={{0}: (19, {}), {1}: (20, {}), {2}: (21, {}), {3}: (22, {}),... | custom-call | flops 14495514624 | bytes 41943040 | tf_op jit(solution)/shard_map/layer_backward/pallas_call | solution.py:517
  196.8 45.0 %psum.7 = f32[9220]{0:T(1024)S(1)} all-reduce(f32[9220]{0:T(1024)S(1)} %concatenate.11), channel_id=1, replica_groups=mesh['section'=2,'dp'=16] {'dp'}, use_global_device_ids=true, to_apply=%region_4.5 | all-reduce | flops 9220 | bytes 73760 | tf_op jit(solution)/shard_map/psum | solution.py:690
  249.7 22.6 %collective-permute-start.4 = (bf16[1024,384]{1,0:T(8,128)(2,1)}, bf16[1024,384]{1,0:T(8,128)(2,1)}, u32[]{:S(2)}, u32[]{:S(2)}) collective-permute-start(bf16[1024,384]{1,0:T(8,128)(2,1)} %slice_select_fusion.2), channel_id=1, source_target_pairs={{0,16},{16,0},{1,17},{17,1},{2,18},{18,2},{3,19},{19,3},{4,20},{20... | collective-permute-start | bytes 2359304 | tf_op jit(solution)/shard_map/ppermute | solution.py:707
  272.3 8.3 %weight_gradient.4 = bf16[768,2304]{1,0:T(8,128)(2,1)} custom-call(bf16[512,768]{1,0:T(8,128)(2,1)S(1)} %copy-done.7, bf16[512,768]{1,0:T(8,128)(2,1)S(1)} %copy-done.8, bf16[512,2304]{1,0:T(8,128)(2,1)S(1)} %copy-done.4, bf16[512,2304]{1,0:T(8,128)(2,1)} %get-tuple-element.169.refs_3_), custom_call_target="tpu_custom_call" | custom-call | flops 3623878656 | bytes 9830400 | tf_op jit(solution)/shard_map/weight_gradient/pallas_call | solution.py:580
  283.0 10.4 %weight_gradient.7 = bf16[3072,768]{1,0:T(8,128)(2,1)} custom-call(bf16[512,3072]{1,0:T(8,128)(2,1)S(1)} %copy-done.5, bf16[512,3072]{1,0:T(8,128)(2,1)} %get-tuple-element.183.refs_1_, bf16[512,768]{1,0:T(8,128)(2,1)S(1)} %copy-done.12, bf16[512,768]{1,0:T(8,128)(2,1)S(1)} %copy-done.11), custom_call_target="tpu_custom_call" | custom-call | flops 4831838208 | bytes 12582912 | tf_op jit(solution)/shard_map/weight_gradient/pallas_call | solution.py:580
  293.5 10.2 %weight_gradient.6 = bf16[768,3072]{1,0:T(8,128)(2,1)} custom-call(bf16[512,768]{1,0:T(8,128)(2,1)S(1)} %copy-done.9, bf16[512,768]{1,0:T(8,128)(2,1)S(1)} %copy-done.10, bf16[512,3072]{1,0:T(8,128)(2,1)S(1)} %copy-done.6, bf16[512,3072]{1,0:T(8,128)(2,1)} %get-tuple-element.181.refs_3_), custom_call_target="tpu_custom_call" | custom-call | flops 4831838208 | bytes 12582912 | tf_op jit(solution)/shard_map/weight_gradient/pallas_call | solution.py:580
  305.0 5.3 %collective-permute-start.14 = (bf16[4,48,768]{2,1,0:T(8,128)(2,1)S(1)}, bf16[4,48,768]{2,1,0:T(8,128)(2,1)S(1)}, u32[]{:S(2)}, u32[]{:S(2)}) collective-permute-start(bf16[4,48,768]{2,1,0:T(8,128)(2,1)S(1)} %dynamic-slice_bitcast_fusion.11), channel_id=1, source_target_pairs={{0,2},{1,3},{2,0},{3,1},{4,6},{5,7},{6,4},{7,5},{8,10},{9,11},{10,... | collective-permute-start | bytes 884744 | tf_op jit(solution)/shard_map/ppermute | solution.py:616
  314.2 3.4 collective-permute-done.14
  323.1 8.3 %collective-permute-done.18 = bf16[48,768]{1,0:T(8,128)(2,1)S(1)} collective-permute-done((bf16[48,768]{1,0:T(8,128)(2,1)S(1)}, bf16[48,768]{1,0:T(8,128)(2,1)S(1)}, u32[]{:S(2)}, u32[]{:S(2)}) %collective-permute-start.18) | collective-permute-done | bytes 73760 | tf_op jit(solution)/shard_map/ppermute | solution.py:635
  331.4 7.2 %collective-permute-done.16 = bf16[48,768]{1,0:T(8,128)(2,1)S(1)} collective-permute-done((bf16[48,768]{1,0:T(8,128)(2,1)S(1)}, bf16[48,768]{1,0:T(8,128)(2,1)S(1)}, u32[]{:S(2)}, u32[]{:S(2)}) %collective-permute-start.16) | collective-permute-done | bytes 73760 | tf_op jit(solution)/shard_map/ppermute | solution.py:634
  338.6 3.9 collective-permute-start.19
  342.6 2.7 slice_select_fusion
  347.2 3.9 collective-permute-start.20
  355.9 18.4 %collective-permute-done.6 = bf16[4,48,2304]{2,1,0:T(8,128)(2,1)S(1)} collective-permute-done((bf16[4,48,2304]{2,1,0:T(8,128)(2,1)S(1)}, bf16[4,48,2304]{2,1,0:T(8,128)(2,1)S(1)}, u32[]{:S(2)}, u32[]{:S(2)}) %collective-permute-start.6) | collective-permute-done | bytes 884768 | tf_op jit(solution)/shard_map/ppermute | solution.py:616
  378.6 20.9 %collective-permute-done.30 = bf16[4,192,768]{2,1,0:T(8,128)(2,1)S(1)} collective-permute-done((bf16[4,192,768]{2,1,0:T(8,128)(2,1)S(1)}, bf16[4,192,768]{2,1,0:T(8,128)(2,1)S(1)}, u32[]{:S(2)}, u32[]{:S(2)}) %collective-permute-start.30) | collective-permute-done | bytes 1179680 | tf_op jit(solution)/shard_map/ppermute | solution.py:616
  400.8 19.3 %collective-permute-done.22 = bf16[4,48,3072]{2,1,0:T(8,128)(2,1)S(1)} collective-permute-done((bf16[4,48,3072]{2,1,0:T(8,128)(2,1)S(1)}, bf16[4,48,3072]{2,1,0:T(8,128)(2,1)S(1)}, u32[]{:S(2)}, u32[]{:S(2)}) %collective-permute-start.22) | collective-permute-done | bytes 1179680 | tf_op jit(solution)/shard_map/ppermute | solution.py:616
  423.6 3.6 collective-permute-start.11
  431.4 2.5 collective-permute-done.11
  435.2 5.0 %collective-permute-done.34 = bf16[192,768]{1,0:T(8,128)(2,1)S(1)} collective-permute-done((bf16[192,768]{1,0:T(8,128)(2,1)S(1)}, bf16[192,768]{1,0:T(8,128)(2,1)S(1)}, u32[]{:S(2)}, u32[]{:S(2)}) %collective-permute-start.34) | collective-permute-done | bytes 294944 | tf_op jit(solution)/shard_map/ppermute | solution.py:635
  448.6 2.6 collective-permute-done.12
  455.2 2.4 collective-permute-done.35
  459.6 4.3 collective-permute-done.27
  469.3 3.2 collective-permute-done.28
  (175 shorter events, 77.3 us)
Async XLA Ops:
  11.0 36.7 %collective-permute-start.2 = (bf16[512,768]{1,0:T(8,128)(2,1)}, bf16[512,768]{1,0:T(8,128)(2,1)S(1)}, u32[]{:S(2)}, u32[]{:S(2)}) collective-permute-start(bf16[512,768]{1,0:T(8,128)(2,1)} %get-tuple-element.133), channel_id=1, source_target_pairs={{0,16},{1,17},{2,18},{3,19},{4,20},{5,21},{6,22},{7,23},{8,24},{9,... | collective-permute-start | bytes 2359304 | tf_op jit(solution)/shard_map/ppermute | solution.py:653
  21.6 85.2 %collective-permute-start = (bf16[512,768]{1,0:T(8,128)(2,1)}, bf16[512,768]{1,0:T(8,128)(2,1)S(1)}, u32[]{:S(2)}, u32[]{:S(2)}) collective-permute-start(bf16[512,768]{1,0:T(8,128)(2,1)} %get-tuple-element.102), channel_id=1, source_target_pairs={{0,16},{1,17},{2,18},{3,19},{4,20},{5,21},{6,22},{7,23},{8,24},{9,... | collective-permute-start | bytes 2359304 | tf_op jit(solution)/shard_map/ppermute | solution.py:653
  105.5 63.1 %collective-permute-start.3 = (bf16[512,768]{1,0:T(8,128)(2,1)}, bf16[512,768]{1,0:T(8,128)(2,1)S(1)}, u32[]{:S(2)}, u32[]{:S(2)}) collective-permute-start(bf16[512,768]{1,0:T(8,128)(2,1)} %get-tuple-element.157), channel_id=1, source_target_pairs={{16,0},{17,1},{18,2},{19,3},{20,4},{21,5},{22,6},{23,7},{24,8},{25... | collective-permute-start | bytes 2359304 | tf_op jit(solution)/shard_map/ppermute | solution.py:653
  165.3 18.1 %collective-permute-start.1 = (bf16[512,768]{1,0:T(8,128)(2,1)}, bf16[512,768]{1,0:T(8,128)(2,1)S(1)}, u32[]{:S(2)}, u32[]{:S(2)}) collective-permute-start(bf16[512,768]{1,0:T(8,128)(2,1)} %get-tuple-element.126), channel_id=1, source_target_pairs={{16,0},{17,1},{18,2},{19,3},{20,4},{21,5},{22,6},{23,7},{24,8},{25... | collective-permute-start | bytes 2359304 | tf_op jit(solution)/shard_map/ppermute | solution.py:653
  246.3 57.4 %collective-permute-start.13 = (bf16[8,48,768]{2,1,0:T(8,128)(2,1)}, bf16[8,48,768]{2,1,0:T(8,128)(2,1)}, u32[]{:S(2)}, u32[]{:S(2)}) collective-permute-start(bf16[8,48,768]{2,1,0:T(8,128)(2,1)} %dynamic-slice_bitcast_fusion.6), channel_id=1, source_target_pairs={{0,1},{1,0},{2,3},{3,2},{4,5},{5,4},{6,7},{7,6},{8,9},{9,8},{10,11... | collective-permute-start | bytes 1769480 | tf_op jit(solution)/shard_map/ppermute | solution.py:616
  249.7 92.9 %collective-permute-start.4 = (bf16[1024,384]{1,0:T(8,128)(2,1)}, bf16[1024,384]{1,0:T(8,128)(2,1)}, u32[]{:S(2)}, u32[]{:S(2)}) collective-permute-start(bf16[1024,384]{1,0:T(8,128)(2,1)} %slice_select_fusion.2), channel_id=1, source_target_pairs={{0,16},{16,0},{1,17},{17,1},{2,18},{18,2},{3,19},{19,3},{4,20},{20... | collective-permute-start | bytes 2359304 | tf_op jit(solution)/shard_map/ppermute | solution.py:707
  282.4 68.8 %collective-permute-start.5 = (bf16[8,48,2304]{2,1,0:T(8,128)(2,1)S(1)}, bf16[8,48,2304]{2,1,0:T(8,128)(2,1)S(1)}, u32[]{:S(2)}, u32[]{:S(2)}) collective-permute-start(bf16[8,48,2304]{2,1,0:T(8,128)(2,1)S(1)} %dynamic-slice_bitcast_fusion.2), channel_id=1, source_target_pairs={{0,1},{1,0},{2,3},{3,2},{4,5},{5,4},{6,7},{7,6},{8,9},{9,8},{10,11... | collective-permute-start | bytes 5308424 | tf_op jit(solution)/shard_map/ppermute | solution.py:616
  305.0 12.7 %collective-permute-start.14 = (bf16[4,48,768]{2,1,0:T(8,128)(2,1)S(1)}, bf16[4,48,768]{2,1,0:T(8,128)(2,1)S(1)}, u32[]{:S(2)}, u32[]{:S(2)}) collective-permute-start(bf16[4,48,768]{2,1,0:T(8,128)(2,1)S(1)} %dynamic-slice_bitcast_fusion.11), channel_id=1, source_target_pairs={{0,2},{1,3},{2,0},{3,1},{4,6},{5,7},{6,4},{7,5},{8,10},{9,11},{10,... | collective-permute-start | bytes 884744 | tf_op jit(solution)/shard_map/ppermute | solution.py:616
  313.5 38.5 %collective-permute-start.29 = (bf16[8,192,768]{2,1,0:T(8,128)(2,1)S(1)}, bf16[8,192,768]{2,1,0:T(8,128)(2,1)S(1)}, u32[]{:S(2)}, u32[]{:S(2)}) collective-permute-start(bf16[8,192,768]{2,1,0:T(8,128)(2,1)S(1)} %dynamic-slice_bitcast_fusion), channel_id=1, source_target_pairs={{0,1},{1,0},{2,3},{3,2},{4,5},{5,4},{6,7},{7,6},{8,9},{9,8},{10,11... | collective-permute-start | bytes 7077896 | tf_op jit(solution)/shard_map/ppermute | solution.py:616
  319.6 11.8 %collective-permute-start.18 = (bf16[48,768]{1,0:T(8,128)(2,1)S(1)}, bf16[48,768]{1,0:T(8,128)(2,1)S(1)}, u32[]{:S(2)}, u32[]{:S(2)}) collective-permute-start(bf16[48,768]{1,0:T(8,128)(2,1)S(1)} %get-tuple-element.206), channel_id=1, source_target_pairs={{12,8},{13,9},{14,10},{15,11},{28,24},{29,25},{30,26},{31,27}} | collective-permute-start | bytes 221192 | tf_op jit(solution)/shard_map/ppermute | solution.py:635
  321.0 17.6 %collective-permute-start.16 = (bf16[48,768]{1,0:T(8,128)(2,1)S(1)}, bf16[48,768]{1,0:T(8,128)(2,1)S(1)}, u32[]{:S(2)}, u32[]{:S(2)}) collective-permute-start(bf16[48,768]{1,0:T(8,128)(2,1)S(1)} %fusion.27), channel_id=1, source_target_pairs={{0,4},{1,5},{2,6},{3,7},{4,8},{5,9},{6,10},{7,11},{16,20},{17,21},... | collective-permute-start | bytes 221192 | tf_op jit(solution)/shard_map/ppermute | solution.py:634
  331.4 23.1 %collective-permute-start.21 = (bf16[8,48,3072]{2,1,0:T(8,128)(2,1)S(1)}, bf16[8,48,3072]{2,1,0:T(8,128)(2,1)S(1)}, u32[]{:S(2)}, u32[]{:S(2)}) collective-permute-start(bf16[8,48,3072]{2,1,0:T(8,128)(2,1)S(1)} %dynamic-slice_bitcast_fusion.1), channel_id=1, source_target_pairs={{0,1},{1,0},{2,3},{3,2},{4,5},{5,4},{6,7},{7,6},{8,9},{9,8},{10,11... | collective-permute-start | bytes 7077896 | tf_op jit(solution)/shard_map/ppermute | solution.py:616
  345.2 30.0 %collective-permute-start.17 = (bf16[48,768]{1,0:T(8,128)(2,1)S(1)}, bf16[48,768]{1,0:T(8,128)(2,1)S(1)}, u32[]{:S(2)}, u32[]{:S(2)}) collective-permute-start(bf16[48,768]{1,0:T(8,128)(2,1)S(1)} %get-tuple-element.203), channel_id=1, source_target_pairs={{0,4},{1,5},{2,6},{3,7},{4,8},{5,9},{6,10},{7,11},{8,12},{9,13},{1... | collective-permute-start | bytes 221192 | tf_op jit(solution)/shard_map/ppermute | solution.py:634
  347.2 28.1 %collective-permute-start.20 = (bf16[48,768]{1,0:T(8,128)(2,1)S(1)}, bf16[48,768]{1,0:T(8,128)(2,1)S(1)}, u32[]{:S(2)}, u32[]{:S(2)}) collective-permute-start(bf16[48,768]{1,0:T(8,128)(2,1)S(1)} %fusion.26), channel_id=1, source_target_pairs={{4,0},{5,1},{6,2},{7,3},{8,4},{9,5},{10,6},{11,7},{12,8},{13,9},{1... | collective-permute-start | bytes 221192 | tf_op jit(solution)/shard_map/ppermute | solution.py:635
  351.6 22.6 %collective-permute-start.6 = (bf16[4,48,2304]{2,1,0:T(8,128)(2,1)S(1)}, bf16[4,48,2304]{2,1,0:T(8,128)(2,1)S(1)}, u32[]{:S(2)}, u32[]{:S(2)}) collective-permute-start(bf16[4,48,2304]{2,1,0:T(8,128)(2,1)S(1)} %dynamic-slice_bitcast_fusion.5), channel_id=1, source_target_pairs={{0,2},{1,3},{2,0},{3,1},{4,6},{5,7},{6,4},{7,5},{8,10},{9,11},{10,... | collective-permute-start | bytes 2654216 | tf_op jit(solution)/shard_map/ppermute | solution.py:616
  352.7 46.9 %collective-permute-start.30 = (bf16[4,192,768]{2,1,0:T(8,128)(2,1)S(1)}, bf16[4,192,768]{2,1,0:T(8,128)(2,1)S(1)}, u32[]{:S(2)}, u32[]{:S(2)}) collective-permute-start(bf16[4,192,768]{2,1,0:T(8,128)(2,1)S(1)} %dynamic-slice_bitcast_fusion.3), channel_id=1, source_target_pairs={{0,2},{1,3},{2,0},{3,1},{4,6},{5,7},{6,4},{7,5},{8,10},{9,11},{10,... | collective-permute-start | bytes 3538952 | tf_op jit(solution)/shard_map/ppermute | solution.py:616
  355.5 64.6 %collective-permute-start.22 = (bf16[4,48,3072]{2,1,0:T(8,128)(2,1)S(1)}, bf16[4,48,3072]{2,1,0:T(8,128)(2,1)S(1)}, u32[]{:S(2)}, u32[]{:S(2)}) collective-permute-start(bf16[4,48,3072]{2,1,0:T(8,128)(2,1)S(1)} %dynamic-slice_bitcast_fusion.4), channel_id=1, source_target_pairs={{0,2},{1,3},{2,0},{3,1},{4,6},{5,7},{6,4},{7,5},{8,10},{9,11},{10,... | collective-permute-start | bytes 3538952 | tf_op jit(solution)/shard_map/ppermute | solution.py:616
  376.0 45.3 %collective-permute-start.10 = (bf16[48,2304]{1,0:T(8,128)(2,1)S(1)}, bf16[48,2304]{1,0:T(8,128)(2,1)S(1)}, u32[]{:S(2)}, u32[]{:S(2)}) collective-permute-start(bf16[48,2304]{1,0:T(8,128)(2,1)S(1)} %get-tuple-element.197), channel_id=1, source_target_pairs={{12,8},{13,9},{14,10},{15,11},{28,24},{29,25},{30,26},{31,27}} | collective-permute-start | bytes 663560 | tf_op jit(solution)/shard_map/ppermute | solution.py:635
  377.3 43.9 %collective-permute-start.8 = (bf16[48,2304]{1,0:T(8,128)(2,1)S(1)}, bf16[48,2304]{1,0:T(8,128)(2,1)S(1)}, u32[]{:S(2)}, u32[]{:S(2)}) collective-permute-start(bf16[48,2304]{1,0:T(8,128)(2,1)S(1)} %fusion.22), channel_id=1, source_target_pairs={{0,4},{1,5},{2,6},{3,7},{4,8},{5,9},{6,10},{7,11},{16,20},{17,21},... | collective-permute-start | bytes 663560 | tf_op jit(solution)/shard_map/ppermute | solution.py:634
  399.9 28.7 %collective-permute-start.31 = (bf16[192,768]{1,0:T(8,128)(2,1)S(1)}, bf16[192,768]{1,0:T(8,128)(2,1)S(1)}, u32[]{:S(2)}, u32[]{:S(2)}) collective-permute-start(bf16[192,768]{1,0:T(8,128)(2,1)S(1)} %get-tuple-element.188), channel_id=1, source_target_pairs={{0,4},{1,5},{2,6},{3,7},{16,20},{17,21},{18,22},{19,23}} | collective-permute-start | bytes 884744 | tf_op jit(solution)/shard_map/ppermute | solution.py:634
  421.4 27.2 %collective-permute-start.9 = (bf16[48,2304]{1,0:T(8,128)(2,1)S(1)}, bf16[48,2304]{1,0:T(8,128)(2,1)S(1)}, u32[]{:S(2)}, u32[]{:S(2)}) collective-permute-start(bf16[48,2304]{1,0:T(8,128)(2,1)S(1)} %get-tuple-element.194), channel_id=1, source_target_pairs={{0,4},{1,5},{2,6},{3,7},{4,8},{5,9},{6,10},{7,11},{8,12},{9,13},{1... | collective-permute-start | bytes 663560 | tf_op jit(solution)/shard_map/ppermute | solution.py:634
  423.6 10.3 %collective-permute-start.11 = (bf16[48,2304]{1,0:T(8,128)(2,1)S(1)}, bf16[48,2304]{1,0:T(8,128)(2,1)S(1)}, u32[]{:S(2)}, u32[]{:S(2)}) collective-permute-start(bf16[48,2304]{1,0:T(8,128)(2,1)S(1)} %get-tuple-element.195), channel_id=1, source_target_pairs={{8,4},{9,5},{10,6},{11,7},{12,8},{13,9},{14,10},{15,11},{24,20},{2... | collective-permute-start | bytes 663560 | tf_op jit(solution)/shard_map/ppermute | solution.py:635
  427.3 12.9 %collective-permute-start.34 = (bf16[192,768]{1,0:T(8,128)(2,1)S(1)}, bf16[192,768]{1,0:T(8,128)(2,1)S(1)}, u32[]{:S(2)}, u32[]{:S(2)}) collective-permute-start(bf16[192,768]{1,0:T(8,128)(2,1)S(1)} %get-tuple-element.189), channel_id=1, source_target_pairs={{12,8},{13,9},{14,10},{15,11},{28,24},{29,25},{30,26},{31,27}} | collective-permute-start | bytes 884744 | tf_op jit(solution)/shard_map/ppermute | solution.py:635
  428.6 17.9 %collective-permute-start.26 = (bf16[48,3072]{1,0:T(8,128)(2,1)S(1)}, bf16[48,3072]{1,0:T(8,128)(2,1)S(1)}, u32[]{:S(2)}, u32[]{:S(2)}) collective-permute-start(bf16[48,3072]{1,0:T(8,128)(2,1)S(1)} %get-tuple-element.193), channel_id=1, source_target_pairs={{12,8},{13,9},{14,10},{15,11},{28,24},{29,25},{30,26},{31,27}} | collective-permute-start | bytes 884744 | tf_op jit(solution)/shard_map/ppermute | solution.py:635
  430.0 12.1 %collective-permute-start.32 = (bf16[192,768]{1,0:T(8,128)(2,1)S(1)}, bf16[192,768]{1,0:T(8,128)(2,1)S(1)}, u32[]{:S(2)}, u32[]{:S(2)}) collective-permute-start(bf16[192,768]{1,0:T(8,128)(2,1)S(1)} %fusion.9), channel_id=1, source_target_pairs={{0,4},{1,5},{2,6},{3,7},{4,8},{5,9},{6,10},{7,11},{16,20},{17,21},... | collective-permute-start | bytes 884744 | tf_op jit(solution)/shard_map/ppermute | solution.py:634
  433.9 12.6 %collective-permute-start.24 = (bf16[48,3072]{1,0:T(8,128)(2,1)S(1)}, bf16[48,3072]{1,0:T(8,128)(2,1)S(1)}, u32[]{:S(2)}, u32[]{:S(2)}) collective-permute-start(bf16[48,3072]{1,0:T(8,128)(2,1)S(1)} %fusion.15), channel_id=1, source_target_pairs={{0,4},{1,5},{2,6},{3,7},{4,8},{5,9},{6,10},{7,11},{16,20},{17,21},... | collective-permute-start | bytes 884744 | tf_op jit(solution)/shard_map/ppermute | solution.py:634
  440.2 11.1 %collective-permute-start.12 = (bf16[48,2304]{1,0:T(8,128)(2,1)S(1)}, bf16[48,2304]{1,0:T(8,128)(2,1)S(1)}, u32[]{:S(2)}, u32[]{:S(2)}) collective-permute-start(bf16[48,2304]{1,0:T(8,128)(2,1)S(1)} %fusion.21), channel_id=1, source_target_pairs={{4,0},{5,1},{6,2},{7,3},{8,4},{9,5},{10,6},{11,7},{12,8},{13,9},{1... | collective-permute-start | bytes 663560 | tf_op jit(solution)/shard_map/ppermute | solution.py:635
  442.3 15.3 %collective-permute-start.35 = (bf16[192,768]{1,0:T(8,128)(2,1)S(1)}, bf16[192,768]{1,0:T(8,128)(2,1)S(1)}, u32[]{:S(2)}, u32[]{:S(2)}) collective-permute-start(bf16[192,768]{1,0:T(8,128)(2,1)S(1)} %get-tuple-element.187), channel_id=1, source_target_pairs={{8,4},{9,5},{10,6},{11,7},{12,8},{13,9},{14,10},{15,11},{24,20},{2... | collective-permute-start | bytes 884744 | tf_op jit(solution)/shard_map/ppermute | solution.py:635
  446.7 17.2 %collective-permute-start.27 = (bf16[48,3072]{1,0:T(8,128)(2,1)S(1)}, bf16[48,3072]{1,0:T(8,128)(2,1)S(1)}, u32[]{:S(2)}, u32[]{:S(2)}) collective-permute-start(bf16[48,3072]{1,0:T(8,128)(2,1)S(1)} %get-tuple-element.191), channel_id=1, source_target_pairs={{8,4},{9,5},{10,6},{11,7},{12,8},{13,9},{14,10},{15,11},{24,20},{2... | collective-permute-start | bytes 884744 | tf_op jit(solution)/shard_map/ppermute | solution.py:635
  451.3 15.3 %collective-permute-start.33 = (bf16[192,768]{1,0:T(8,128)(2,1)S(1)}, bf16[192,768]{1,0:T(8,128)(2,1)S(1)}, u32[]{:S(2)}, u32[]{:S(2)}) collective-permute-start(bf16[192,768]{1,0:T(8,128)(2,1)S(1)} %get-tuple-element.186), channel_id=1, source_target_pairs={{0,4},{1,5},{2,6},{3,7},{4,8},{5,9},{6,10},{7,11},{8,12},{9,13},{1... | collective-permute-start | bytes 884744 | tf_op jit(solution)/shard_map/ppermute | solution.py:634
  453.3 16.1 %collective-permute-start.25 = (bf16[48,3072]{1,0:T(8,128)(2,1)S(1)}, bf16[48,3072]{1,0:T(8,128)(2,1)S(1)}, u32[]{:S(2)}, u32[]{:S(2)}) collective-permute-start(bf16[48,3072]{1,0:T(8,128)(2,1)S(1)} %get-tuple-element.190), channel_id=1, source_target_pairs={{0,4},{1,5},{2,6},{3,7},{4,8},{5,9},{6,10},{7,11},{8,12},{9,13},{1... | collective-permute-start | bytes 884744 | tf_op jit(solution)/shard_map/ppermute | solution.py:634
  457.7 10.8 %collective-permute-start.36 = (bf16[192,768]{1,0:T(8,128)(2,1)S(1)}, bf16[192,768]{1,0:T(8,128)(2,1)S(1)}, u32[]{:S(2)}, u32[]{:S(2)}) collective-permute-start(bf16[192,768]{1,0:T(8,128)(2,1)S(1)} %fusion.8), channel_id=1, source_target_pairs={{4,0},{5,1},{6,2},{7,3},{8,4},{9,5},{10,6},{11,7},{12,8},{13,9},{1... | collective-permute-start | bytes 884744 | tf_op jit(solution)/shard_map/ppermute | solution.py:635
  (36 other events, 567.7 us)

commit v2 on v1

v2 whole, which is shorter than its diff:
```python
from functools import partial

import jax
import jax.numpy as jnp
from jax import lax
from jax.experimental import pallas as pl
from jax.experimental.pallas import tpu as pltpu
from jax.sharding import PartitionSpec as P

HEAD_DIM = 64
CLUSTER = 128
SEQ = 512
LANES = 128
MIB = 1024 * 1024

BF16 = jnp.bfloat16
F32 = jnp.float32
LOG2E = 1.4426950408889634
SCALE = HEAD_DIM**-0.5
SCORE_SCALE = SCALE * LOG2E

NN = ((1,), (0,))
NT = ((1,), (1,))
TN = ((0,), (0,))

ANY = pl.BlockSpec(memory_space=pltpu.HBM)
SHORT = pl.CostEstimate(flops=1, bytes_accessed=1, transcendentals=0)
WHOLE = pl.BlockSpec(memory_space=pltpu.VMEM)


def mm(left, right, dims):
    return lax.dot_general(left, right, (dims, ((), ())), preferred_element_type=F32)


class Copies:
    def __init__(self, sems):
        self.sems = sems
        self.used = 0

    def start(self, source, target):
        copy = pltpu.make_async_copy(source, target, self.sems.at[self.used])
        copy.start()
        self.used += 1
        return copy


def vec(ref):
    return ref[0:1, :].astype(F32)


SAVED = ("x", "qkv", "ctx", "lse", "kid", "qid", "n1", "r1", "hid", "act", "gp", "n2", "r2")


def saved_shapes(width, inner):
    return dict(
        x=((SEQ, width), BF16),
        qkv=((SEQ, 3 * width), BF16),
        ctx=((SEQ, width), BF16),
        lse=((16, SEQ), F32),
        kid=((SEQ, width), F32),
        qid=((16, SEQ), F32),
        n1=((SEQ, width), BF16),
        r1=((SEQ, LANES), F32),
        hid=((SEQ, width), BF16),
        act=((SEQ, inner), BF16),
        gp=((SEQ, inner), BF16),
        n2=((SEQ, width), BF16),
        r2=((SEQ, LANES), F32),
    )


def token_ids(row, heads, perm_ref, seg_ref, valid_ref, kid_ref, qid_ref):
    token = lax.broadcasted_iota(jnp.int32, (SEQ, LANES), 0)
    lane = lax.broadcasted_iota(jnp.int32, (SEQ, LANES), 1)
    seg_row = seg_ref[row : row + 1, :].astype(F32)
    valid_row = valid_ref[row : row + 1, :].astype(F32)
    at = lax.broadcasted_iota(jnp.int32, (LANES, SEQ), 0)
    both = jnp.where(at == 0, seg_row, jnp.where(at == 1, valid_row, 0.0)).T
    segment, live = both[:, 0:1], both[:, 1:2]

    def column(h):
        places = perm_ref[0, row, pl.ds(h, 1), :]
        mine = jnp.zeros((SEQ, LANES), F32)
        for c in range(1, SEQ // CLUSTER):
            part = places[:, c * CLUSTER : (c + 1) * CLUSTER]
            mine = jnp.where(token == part, float(c), mine)
        return jnp.sum(mine, axis=1, keepdims=True) * 4.0 + segment

    def pair(j, ids):
        left, right = column(2 * j), column(2 * j + 1)
        own = jnp.where(lane < HEAD_DIM, left, right)
        kid_ref[:, lanes_at(j * LANES)] = jnp.where(live > 0.5, own, -1.0)
        ids = jnp.where(lane == 2 * j, left, ids)
        return jnp.where(lane == 2 * j + 1, right, ids)

    qid = lax.fori_loop(0, heads // 2, pair, jnp.zeros((SEQ, LANES), F32))
    qid_ref[...] = qid.T[0:16, :]
    return live


def allowed_pairs(kid_column, qid_row):
    key = lax.broadcasted_iota(jnp.int32, (SEQ, SEQ), 0)
    query = lax.broadcasted_iota(jnp.int32, (SEQ, SEQ), 1)
    return (kid_column == qid_row) | (key == query)


def low_lanes():
    return lax.broadcasted_iota(jnp.int32, (SEQ, LANES), 1) < HEAD_DIM


def lanes_at(start):
    return pl.ds(pl.multiple_of(start, LANES), LANES)


def attend_pair(j, width, qkv, kid, qid, lse, ctx):
    low = low_lanes()
    lanes = lanes_at(j * LANES)
    query = qkv[:, lanes]
    key = qkv[:, lanes_at(width + j * LANES)]
    value = qkv[:, lanes_at(2 * width + j * LANES)]
    kid_pair = kid[:, lanes]
    mixed = []
    for half in (0, 1):
        h = pl.ds(2 * j + half, 1)
        own = low if half == 0 else ~low
        own_query = jnp.where(own, query, jnp.zeros_like(query))
        value_ones = jnp.where(own, value, jnp.ones_like(value))
        kid_column = kid_pair[:, half * HEAD_DIM : half * HEAD_DIM + 1]
        ok = allowed_pairs(kid_column, qid[h, :])
        scores = jnp.where(ok, mm(key, own_query, NT) * SCORE_SCALE, -1e30)
        top = jnp.max(scores, axis=0, keepdims=True)
        weights = jnp.exp2(scores - top)
        total = jnp.sum(weights, axis=0, keepdims=True)
        lse[h, :] = top + jnp.log2(total)
        mixed.append(mm(weights.astype(BF16), value_ones, TN))
    sums = [pltpu.roll(part, HEAD_DIM, 1) for part in mixed]
    ctx[:, lanes] = (
        jnp.where(low, mixed[0], mixed[1]) / jnp.where(low, sums[0], sums[1])
    ).astype(BF16)


def normed(total):
    centre = total - jnp.mean(total, axis=-1, keepdims=True)
    spread = jnp.mean(centre * centre, axis=-1, keepdims=True)
    rate = lax.rsqrt(spread + 1e-05)
    return centre * rate, rate


ROW_BLOCK = 64


def over_rows(step):
    def body(i, carry):
        step(pl.ds(pl.multiple_of(i * ROW_BLOCK, ROW_BLOCK), ROW_BLOCK))
        return carry

    lax.fori_loop(0, SEQ // ROW_BLOCK, body, 0)


def over_tiles(size, tile, step):
    def body(i, carry):
        step(pl.ds(pl.multiple_of(i * tile, tile), tile))
        return carry

    lax.fori_loop(0, size // tile, body, 0)


def fold8(block):
    return jnp.sum(block.reshape(-1, 8, block.shape[-1]), axis=0)


def forward_kernel(section, row, x_row, n_alias, heads, *refs):
    (
        x_hbm,
        perm_ref,
        seg_ref,
        valid_ref,
        wq_hbm,
        bq_ref,
        wk_hbm,
        wv_hbm,
        bv_ref,
        wo_hbm,
        bo_ref,
        g1_ref,
        s1_ref,
        wu_hbm,
        bu_ref,
        wd_hbm,
        bd_ref,
        g2_ref,
        s2_ref,
    ) = refs[:19]
    refs = refs[19 + n_alias :]
    out = dict(zip(SAVED, refs[: len(SAVED)]))
    y_hbm, stats_hbm = refs[len(SAVED) : len(SAVED) + 2]
    refs = refs[len(SAVED) + 2 :]
    here = dict(zip(SAVED, refs[: len(SAVED)]))
    wqkv, wo, wu, wd, wide, feed, y_ref, stats, live_ref, bias, sems = refs[len(SAVED) :]
    width = wo.shape[0]
    inner = wu.shape[1]

    @pl.when(lax.axis_index("section") == section)
    def _():
        copies = Copies(sems)
        get_x = copies.start(x_hbm.at[pl.ds(x_row * SEQ, SEQ), :], here["x"])
        get_qkv = [
            copies.start(w.at[0], wqkv.at[:, pl.ds(i * width, width)])
            for i, w in enumerate((wq_hbm, wk_hbm, wv_hbm))
        ]
        get_o = copies.start(wo_hbm.at[0], wo)
        get_u = copies.start(wu_hbm.at[0], wu)
        get_d = copies.start(wd_hbm.at[0], wd)
        puts = []

        def save(name):
            puts.append(copies.start(here[name], out[name]))

        live = token_ids(row, heads, perm_ref, seg_ref, valid_ref, here["kid"], here["qid"])
        live_ref[...] = jnp.broadcast_to(live, (SEQ, LANES))
        here["lse"][...] = jnp.zeros((16, SEQ), F32)
        stats[...] = jnp.zeros(stats.shape, F32)
        save("kid")
        save("qid")
        get_x.wait()
        save("x")
        xs = here["x"]
        qkv = here["qkv"]
        bias[0:1, :] = vec(bq_ref)
        bias[1:2, :] = jnp.zeros((1, width), F32)
        bias[2:3, :] = vec(bv_ref)
        for get in get_qkv:
            get.wait()

        def to_qkv(i, carry):
            part = pl.ds(pl.multiple_of(i * width, LANES), width)
            qkv[:, part] = (mm(xs[...], wqkv[:, part], NN) + bias[pl.ds(i, 1), :]).astype(BF16)
            return carry

        lax.fori_loop(0, 3, to_qkv, 0)
        save("qkv")

        def attend(j, carry):
            attend_pair(j, width, qkv, here["kid"], here["qid"], here["lse"], here["ctx"])
            return carry

        lax.fori_loop(0, heads // 2, attend, 0)
        save("lse")
        save("ctx")
        get_o.wait()
        wide[...] = mm(here["ctx"][...], wo[...], NN)

        def first_norm(rows):
            branch = wide[rows, :] + vec(bo_ref)
            alive = live_ref[rows, 0:1]
            stats[0:8, :] += fold8(branch * branch * alive)
            unit, rate = normed(xs[rows, :].astype(F32) + branch)
            hidden = unit * vec(g1_ref) + vec(s1_ref)
            here["n1"][rows, :] = unit.astype(BF16)
            here["r1"][rows, :] = jnp.broadcast_to(rate, (ROW_BLOCK, LANES))
            here["hid"][rows, :] = hidden.astype(BF16)
            wide[rows, :] = hidden

        over_rows(first_norm)
        save("n1")
        save("r1")
        save("hid")
        get_u.wait()

        def up(part):
            upper = mm(here["hid"][...], wu[:, part], NN) + bu_ref[0:1, part].astype(F32)
            half = 0.5 + 0.5 * lax.erf(upper * 0.5**0.5)
            bell = jnp.exp2(upper * upper * (-0.5 * LOG2E)) * 0.3989422804014327
            here["act"][:, part] = (upper * half).astype(BF16)
            here["gp"][:, part] = (half + upper * bell).astype(BF16)

        over_tiles(inner, inner // 4, up)
        save("act")
        save("gp")
        get_d.wait()
        feed[...] = mm(here["act"][...], wd[...], NN)

        def second_norm(rows):
            ffn = feed[rows, :] + vec(bd_ref)
            alive = live_ref[rows, 0:1]
            stats[8:16, :] += fold8(ffn * ffn * alive)
            unit, rate = normed(wide[rows, :] + ffn)
            result = unit * vec(g2_ref) + vec(s2_ref)
            stats[16:24, :] += fold8(result * result * alive)
            here["n2"][rows, :] = unit.astype(BF16)
            here["r2"][rows, :] = jnp.broadcast_to(rate, (ROW_BLOCK, LANES))
            y_ref[rows, :] = result.astype(BF16)

        over_rows(second_norm)
        puts.append(copies.start(y_ref, y_hbm))
        puts.append(copies.start(stats, stats_hbm))
        save("n2")
        save("r2")
        for put in puts:
            put.wait()


def forward(section, row, x, x_row, ids, params, saved):
    width = x.shape[1]
    inner = params[9].shape[2]
    heads = ids[0].shape[2]
    shapes = saved_shapes(width, inner)
    out_shape = [jax.ShapeDtypeStruct(*shapes[name]) for name in SAVED]
    out_shape += [
        jax.ShapeDtypeStruct((SEQ, width), BF16),
        jax.ShapeDtypeStruct((24, width), F32),
    ]
    param_specs = [ANY if p.ndim == 3 else WHOLE for p in params]
    old = [] if saved is None else list(saved)
    n_in = 4 + len(params)
    result = pl.pallas_call(
        partial(forward_kernel, section, row, x_row, len(old), heads),
        out_shape=out_shape,
        in_specs=[ANY, WHOLE, WHOLE, WHOLE] + param_specs + [ANY] * len(old),
        out_specs=[ANY] * len(out_shape),
        input_output_aliases={n_in + i: i for i in range(len(old))},
        scratch_shapes=[pltpu.VMEM(*shapes[name]) for name in SAVED]
        + [
            pltpu.VMEM((width, 3 * width), BF16),
            pltpu.VMEM((width, width), BF16),
            pltpu.VMEM((width, inner), BF16),
            pltpu.VMEM((inner, width), BF16),
            pltpu.VMEM((SEQ, width), F32),
            pltpu.VMEM((SEQ, width), F32),
            pltpu.VMEM((SEQ, width), BF16),
            pltpu.VMEM((24, width), F32),
            pltpu.VMEM((SEQ, LANES), F32),
            pltpu.VMEM((8, width), F32),
            pltpu.SemaphoreType.DMA((24,)),
        ],
        compiler_params=pltpu.CompilerParams(vmem_limit_bytes=58 * MIB),
        cost_estimate=SHORT,
        name="layer_forward",
    )(x, *ids, *params, *old)
    return tuple(result[: len(SAVED)]), result[-2], result[-1]


MATRICES = ("wq", "wk", "wv", "wo", "wu", "wd")
PARTS = dict(
    ffn=(("g", "n2", "r2", "wd", "gp"), ("dffn", "dup", "wide", "sums_a")),
    mid=(("dup", "wide", "wu", "n1", "r1", "wo", "ctx"), ("dbr", "wide", "dctx", "delta", "sums_b")),
    att=(("dctx", "delta", "lse", "kid", "qid", "qkv"), ("dqkv", "sums_c")),
    dx=(("dqkv", "wide", "wq", "wk", "wv"), ("dx",)),
)
GRADS = ("dffn", "dup", "sums_a", "dbr", "sums_b", "dqkv", "sums_c")
BETWEEN = ("wide", "dctx", "delta")
SUM_ROWS = dict(
    sums_a=("gain2", "shift2", "bdown", "bup"),
    sums_b=("gain1", "shift1", "bout"),
    sums_c=("bq", "bv"),
)


def backward_shapes(width, inner):
    shapes = dict(saved_shapes(width, inner))
    shapes.update(
        g=((SEQ, width), BF16),
        dffn=((SEQ, width), BF16),
        dup=((SEQ, inner), BF16),
        dbr=((SEQ, width), BF16),
        dqkv=((SEQ, 3 * width), BF16),
        sums_a=((32, inner), F32),
        sums_b=((24, width), F32),
        sums_c=((16, width), F32),
        wide=((SEQ, width), F32),
        dctx=((SEQ, width), BF16),
        delta=((16, SEQ), F32),
        dx=((SEQ, width), BF16),
        wo=((width, width), BF16),
        wu=((width, inner), BF16),
        wd=((inner, width), BF16),
    )
    return shapes


def attend_pair_back(j, width, qkv, dctx, kid, qid, lse, delta, dqkv):
    low = low_lanes()
    lanes = [lanes_at(i * width + j * LANES) for i in range(3)]
    query, key, value = (qkv[:, part] for part in lanes)
    d_out = dctx[:, lanes[0]]
    kid_pair = kid[:, lanes[0]]
    d_query, d_key, d_value = [], [], []
    for half in (0, 1):
        h = pl.ds(2 * j + half, 1)
        own = low if half == 0 else ~low
        own_query = jnp.where(own, query, jnp.zeros_like(query))
        own_out = jnp.where(own, d_out, jnp.zeros_like(d_out))
        kid_column = kid_pair[:, half * HEAD_DIM : half * HEAD_DIM + 1]
        ok = allowed_pairs(kid_column, qid[h, :])
        scores = mm(key, own_query, NT) * SCORE_SCALE - lse[h, :]
        weights = jnp.exp2(jnp.where(ok, scores, -1e30))
        d_weights = mm(value, own_out, NT)
        d_scores = (weights * (d_weights - delta[h, :])).astype(BF16)
        d_value.append(mm(weights.astype(BF16), own_out, NN))
        d_key.append(mm(d_scores, own_query, NN))
        d_query.append(mm(d_scores, key, TN))
    dqkv[:, lanes[0]] = (jnp.where(low, d_query[0], d_query[1]) * SCALE).astype(BF16)
    dqkv[:, lanes[1]] = ((d_key[0] + d_key[1]) * SCALE).astype(BF16)
    dqkv[:, lanes[2]] = (d_value[0] + d_value[1]).astype(BF16)


def norm_back(grad, unit, rate, gain):
    scaled = grad * gain
    mean = jnp.mean(scaled, axis=-1, keepdims=True)
    along = jnp.mean(scaled * unit, axis=-1, keepdims=True)
    return (scaled - mean - unit * along) * rate


def needs_and_gives(parts):
    needs, gives = [], []
    for part in parts:
        for name in PARTS[part][0]:
            if name not in needs and name not in gives:
                needs.append(name)
        for name in PARTS[part][1]:
            if name not in gives:
                gives.append(name)
    if len(parts) == len(PARTS):
        gives = [name for name in gives if name not in BETWEEN]
    return needs, gives


def backward_kernel(section, g_row, parts, pairs, n_alias, names, *refs):
    needs, gives, held = names
    given = dict(zip(needs, refs))
    gain1_ref, gain2_ref = refs[len(needs) : len(needs) + 2]
    refs = refs[len(needs) + 2 + n_alias :]
    out = dict(zip(gives, refs))
    refs = refs[len(gives) :]
    at = dict(zip(held, refs))
    sems = refs[-1]
    width = gain1_ref.shape[1]

    @pl.when(lax.axis_index("section") == section)
    def _():
        copies = Copies(sems)
        got = {}
        for name in needs:
            source = given[name]
            if name in MATRICES:
                source = source.at[0]
            if name == "g":
                source = source.at[pl.ds(g_row * SEQ, SEQ), :]
            if name in ("wq", "wk", "wv"):
                third = MATRICES.index(name)
                target = at["wqkv"].at[:, pl.ds(third * width, width)]
            else:
                target = at[name]
            got[name] = copies.start(source, target)
        puts = []

        def ready(*wanted):
            for name in wanted:
                if name in got:
                    got.pop(name).wait()

        def save(*made):
            for name in made:
                if name not in out:
                    continue
                if name == "dqkv" and len(parts) == 1:
                    for i in range(3):
                        lanes = pl.ds(i * width + pairs[0] * LANES, (pairs[1] - pairs[0]) * LANES)
                        puts.append(copies.start(at[name].at[:, lanes], out[name].at[:, lanes]))
                else:
                    puts.append(copies.start(at[name], out[name]))

        def add_sum(group, name, value):
            first = 8 * SUM_ROWS[group].index(name)
            at[group][first : first + 8, 0:width] += fold8(value)

        for group in SUM_ROWS:
            if group in at:
                at[group][...] = jnp.zeros(at[group].shape, F32)

        if "ffn" in parts:
            ready("g", "n2", "r2")

            def second_back(rows):
                grad = at["g"][rows, :].astype(F32)
                unit = at["n2"][rows, :].astype(F32)
                add_sum("sums_a", "gain2", grad * unit)
                add_sum("sums_a", "shift2", grad)
                d_second = norm_back(grad, unit, at["r2"][rows, 0:1], vec(gain2_ref))
                at["wide"][rows, :] = d_second
                low = d_second.astype(BF16)
                at["dffn"][rows, :] = low
                add_sum("sums_a", "bdown", low.astype(F32))

            over_rows(second_back)
            save("dffn")
            ready("wd", "gp")

            def up_back(part):
                d_act = mm(at["dffn"][...], at["wd"][part, :], NT)
                low = (d_act * at["gp"][:, part].astype(F32)).astype(BF16)
                at["dup"][:, part] = low
                at["sums_a"][24:32, part] += fold8(low.astype(F32))

            inner = at["dup"].shape[1]
            over_tiles(inner, inner // 4, up_back)
            save("dup", "sums_a")
            if "mid" not in parts:
                save("wide")

        if "mid" in parts:
            ready("dup", "wide", "wu")
            at["wide"][...] += mm(at["dup"][...], at["wu"][...], NT)
            ready("n1", "r1")

            def first_back(rows):
                grad = at["wide"][rows, :]
                unit = at["n1"][rows, :].astype(F32)
                add_sum("sums_b", "gain1", grad * unit)
                add_sum("sums_b", "shift1", grad)
                d_first = norm_back(grad, unit, at["r1"][rows, 0:1], vec(gain1_ref))
                at["wide"][rows, :] = d_first
                low = d_first.astype(BF16)
                at["dbr"][rows, :] = low
                add_sum("sums_b", "bout", low.astype(F32))

            over_rows(first_back)
            save("dbr", "wide", "sums_b")
            ready("wo")
            at["dctx"][...] = mm(at["dbr"][...], at["wo"][...], NT).astype(BF16)
            ready("ctx")
            product = at["dctx"][...].astype(F32) * at["ctx"][...].astype(F32)
            high = product.astype(BF16)
            rest = (product - high.astype(F32)).astype(BF16)
            of_head = (
                lax.broadcasted_iota(jnp.int32, (16, width), 1) // HEAD_DIM
                == lax.broadcasted_iota(jnp.int32, (16, width), 0)
            )
            pick = jnp.where(of_head, 1.0, 0.0).astype(BF16)
            at["delta"][...] = mm(pick, high, NT) + mm(pick, rest, NT)
            save("dctx", "delta")

        if "att" in parts:
            ready(*PARTS["att"][0])

            def attend_back(j, carry):
                attend_pair_back(
                    j,
                    width,
                    at["qkv"],
                    at["dctx"],
                    at["kid"],
                    at["qid"],
                    at["lse"],
                    at["delta"],
                    at["dqkv"],
                )
                for i, name in ((0, "bq"), (2, "bv")):
                    made = at["dqkv"][:, lanes_at(i * width + j * LANES)]
                    first = 8 * SUM_ROWS["sums_c"].index(name)
                    at["sums_c"][first : first + 8, lanes_at(j * LANES)] = fold8(made.astype(F32))
                return carry

            lax.fori_loop(pairs[0], pairs[1], attend_back, 0)
            save("dqkv", "sums_c")

        if "dx" in parts:
            ready(*PARTS["dx"][0])
            at["dx"][...] = (at["wide"][...] + mm(at["dqkv"][...], at["wqkv"][...], NT)).astype(
                BF16
            )
            save("dx")
        for put in puts:
            put.wait()


def backward(section, parts, g_row, known, gains, old, pairs=None):
    width, inner = known["wu"].shape[1:]
    shapes = backward_shapes(width, inner)
    if pairs is None:
        pairs = (0, width // LANES)
    needs, gives = needs_and_gives(parts)
    held = [name for name in needs if name not in ("wq", "wk", "wv")]
    made = [name for part in parts for name in PARTS[part][1]]
    held += [name for name in dict.fromkeys(made) if name not in held]
    scratch = [pltpu.VMEM(*shapes[name]) for name in held]
    if "dx" in parts:
        held.append("wqkv")
        scratch.append(pltpu.VMEM((width, 3 * width), BF16))
    reused = [name for name in gives if name in old]
    n_in = len(needs) + 2
    aliases = {n_in + i: gives.index(name) for i, name in enumerate(reused)}
    result = pl.pallas_call(
        partial(backward_kernel, section, g_row, parts, pairs, len(reused), (needs, gives, held)),
        out_shape=[jax.ShapeDtypeStruct(*shapes[name]) for name in gives],
        in_specs=[ANY] * len(needs) + [WHOLE] * 2 + [ANY] * len(reused),
        out_specs=[ANY] * len(gives),
        input_output_aliases=aliases,
        scratch_shapes=scratch + [pltpu.SemaphoreType.DMA((36,))],
        compiler_params=pltpu.CompilerParams(vmem_limit_bytes=58 * MIB),
        cost_estimate=SHORT,
        name="backward_" + "_".join(parts),
    )(*(known[name] for name in needs), *gains, *(old[name] for name in reused))
    return dict(zip(gives, result))


def outer_kernel(n_rows, tile, split_left, pairs, *refs):
    lefts = refs[:n_rows]
    rights = refs[n_rows : 2 * n_rows]
    outs = refs[2 * n_rows : -4]
    left, right, out, sems = refs[-4:]
    copies = Copies(sems)
    gets = [
        copies.start(ref, buf.at[pl.ds(i * SEQ, SEQ), :])
        for i in range(n_rows)
        for ref, buf in ((lefts[i], left), (rights[i], right))
    ]
    for get in gets:
        get.wait()

    size = left.shape[1] if split_left else right.shape[1]

    def body(i, carry):
        part = pl.ds(pl.multiple_of(i * tile, tile), tile)
        if split_left:
            out[part, :] = mm(left[:, part], right[...], TN).astype(BF16)
        else:
            out[:, part] = mm(left[...], right[:, part], TN).astype(BF16)
        return carry

    lax.fori_loop(0, size // tile, body, 0)
    if pairs == 0:
        puts = [copies.start(out, outs[0])]
    else:
        core = lax.axis_index("dp") % 2
        block = out.shape[0] // (2 * pairs)
        puts = []
        for i in range(pairs):
            for target, which in zip(outs, (core, 1 - core)):
                rows = pl.ds(pl.multiple_of((2 * i + which) * block, 16), block)
                puts.append(copies.start(out.at[rows, :], target.at[i]))
    for put in puts:
        put.wait()


def outer(lefts, rights, tile, split_left):
    n_rows = len(lefts)
    rows, columns = lefts[0].shape[1], rights[0].shape[1]
    count = lax.axis_size("dp")
    if count == 16:
        pairs = 8
        out_shape = [jax.ShapeDtypeStruct((pairs, rows // count, columns), BF16)] * 2
    else:
        pairs = 0
        out_shape = [jax.ShapeDtypeStruct((rows, columns), BF16)]
    return pl.pallas_call(
        partial(outer_kernel, n_rows, tile, split_left, pairs),
        out_shape=out_shape,
        in_specs=[ANY] * (2 * n_rows),
        out_specs=[ANY] * len(out_shape),
        scratch_shapes=[
            pltpu.VMEM((n_rows * SEQ, rows), BF16),
            pltpu.VMEM((n_rows * SEQ, columns), BF16),
            pltpu.VMEM((rows, columns), BF16),
            pltpu.SemaphoreType.DMA((2 * n_rows + 16,)),
        ],
        compiler_params=pltpu.CompilerParams(vmem_limit_bytes=58 * MIB),
        cost_estimate=SHORT,
        name="weight_gradient",
    )(*lefts, *rights)


def swap(array, stride):
    count = lax.axis_size("dp")
    return lax.ppermute(array, "dp", [(d, d ^ stride) for d in range(count)])


def place(stride):
    return (lax.axis_index("dp") // stride) % 2


def add(left, right):
    return (left.astype(F32) + right.astype(F32)).astype(BF16)


class ScatterSum:
    def __init__(self, blocks, order):
        self.shape = blocks[0].shape[1:]
        self.blocks = blocks
        self.order = (1,) + order
        self.axes = [8, 4, 2]
        self.done = 0
        self.arrived = blocks[0]
        self.plain = lax.axis_size("dp") != 16

    def pick(self, array, stride, index):
        at = self.axes.index(stride)
        split = array.reshape((2**at, 2, 2 ** (len(self.axes) - at - 1)) + self.shape)
        taken = lax.dynamic_index_in_dim(split, index, 1, keepdims=False)
        return taken.reshape((-1,) + self.shape)

    def advance(self):
        before = self.arrived
        if self.plain or self.done == 4:
            return before
        stride = self.order[self.done]
        self.done += 1
        if stride == 1:
            self.kept, send = self.blocks
        else:
            own = place(stride)
            send, self.kept = (
                add(self.pick(self.kept, stride, side), self.pick(before, stride, side))
                for side in (1 - own, own)
            )
            self.axes.remove(stride)
        self.arrived = swap(send, stride)
        return before

    def finish(self):
        if self.plain:
            total = lax.psum_scatter(self.blocks[0], "dp", scatter_dimension=0, tiled=True)
            return total.astype(F32)
        while self.done < 4:
            self.advance()
        return (self.kept.astype(F32) + self.arrived.astype(F32)).reshape(self.shape)


def small_sum(values):
    count = lax.axis_size("dp")
    if count != 16:
        return lax.psum(values, "dp")
    for stride in (1, 2, 4, 8):
        values = values + swap(values, stride)
    return values


X_FIRST = (2, 4, 8)
Z_FIRST = (4, 2, 8)


def on_device(
    tokens,
    cotangent,
    segment_ids,
    valid_mask,
    cluster_perm,
    *params,
):
    section = lax.axis_index("section")
    width = tokens.shape[1]
    inner = params[9].shape[2]
    ids = (cluster_perm, segment_ids, valid_mask)
    wq, _, wk, wv, _, wo, _, gain1, _, wu, _, wd, _, gain2, _ = params
    matrices = dict(wq=wq, wk=wk, wv=wv, wo=wo, wu=wu, wd=wd)
    gains = (gain1, gain2)

    def hop(array, source, target):
        return lax.ppermute(array, "section", [(source, target)])

    def after(array, first):
        return lax.optimization_barrier((array, first))[0]

    whole = tuple(PARTS)
    kept0, y0, stats00 = forward(0, 0, tokens, 0, ids, params, None)
    in0 = hop(y0, 0, 1)
    kept1, y1, stats01 = forward(0, 1, tokens, 1, ids, params, None)
    in1 = hop(y1, 0, 1)
    kept0, out0, stats10 = forward(1, 0, in0, 0, ids, params, kept0)
    known = dict(zip(SAVED, kept0), g=cotangent, **matrices)
    first = backward(1, whole, 0, known, gains, {})
    in1 = after(in1, first["dx"])
    g0 = hop(first["dx"], 1, 0)
    kept1, out1, stats11 = forward(1, 1, in1, 0, ids, params, kept1)
    known = dict(zip(SAVED, kept1), g=cotangent, **matrices)
    second = backward(1, whole, 1, known, gains, {})
    g0 = after(g0, second["dx"])
    g1 = hop(second["dx"], 1, 0)
    known = dict(zip(SAVED, kept0), g=g0, **matrices)
    first = backward(0, whole, 0, known, gains, first)
    g1 = after(g1, first["dx"])
    known = dict(zip(SAVED, kept1), g=g1, **matrices)

    def step(parts, pairs=None):
        made = backward(0, parts, 0, known, gains, second, pairs)
        known.update(made)
        second.update({name: made[name] for name in made if name in second})

    row0, row1 = dict(zip(SAVED, kept0)), dict(zip(SAVED, kept1))

    def both(left, right, tile, split_left):
        return outer((row0[left], row1[left]), (first[right], second[right]), tile, split_left)

    step(("ffn",))
    down = both("act", "dffn", width, True)
    down_sum = ScatterSum(down, X_FIRST)
    down_sum.advance()
    second["dup"] = after(second["dup"], down[0])
    up = both("hid", "dup", width, False)
    up_sum = ScatterSum(up, Z_FIRST)
    up_sum.advance()
    known["wide"] = after(known["wide"], (up[0], down_sum.advance()))
    step(("mid",))
    known["dctx"] = after(known["dctx"], up_sum.advance())
    out = both("ctx", "dbr", width, False)
    out_sum = ScatterSum(out, X_FIRST)
    out_sum.advance()
    known["dctx"] = after(known["dctx"], out[0])
    half_pairs = width // LANES // 2
    step(("att",), (0, half_pairs))
    early = second.pop("sums_c")
    known["dctx"] = after(known["dctx"], (out_sum.arrived, known["dqkv"]))
    step(("att",), (half_pairs, 2 * half_pairs))
    qkv = both("x", "dqkv", width, False)
    qkv_sum = ScatterSum(qkv, X_FIRST)
    qkv_sum.advance()
    waited = (qkv[0], down_sum.advance(), up_sum.advance())
    known["wide"] = after(known["wide"], waited)
    step(("dx",))
    out_sum.arrived = after(out_sum.arrived, second["dx"])

    w_down = down_sum.finish()
    w_up = up_sum.finish()
    w_out = out_sum.finish()
    w_qkv = qkv_sum.finish()
    dx0, dx1 = first["dx"], second["dx"]
    is_first = section == 0

    late = jnp.where(
        (lax.broadcasted_iota(jnp.int32, (1, width), 1) >= half_pairs * LANES) & is_first,
        known["sums_c"],
        early,
    )
    sum_a = (first["sums_a"] + second["sums_a"]).reshape(4, 8, inner).sum(axis=1)
    sum_b = (first["sums_b"] + second["sums_b"]).reshape(3, 8, width).sum(axis=1)
    sum_c = (first["sums_c"] + late).reshape(2, 8, width).sum(axis=1)
    stats = jnp.where(is_first, stats00 + stats01, stats10 + stats11)
    stats = stats.reshape(3, 8 * width).sum(axis=1)
    count = jnp.sum(valid_mask.astype(F32))
    pieces = [sum_a[:3, :width].reshape(-1), sum_b.reshape(-1), sum_c.reshape(-1), sum_a[3]]
    base = 8 * width + inner
    spare = -(base + 4) % (8 * LANES)
    tail = jnp.concatenate([stats, jnp.broadcast_to(count, (1,)), jnp.zeros((spare,), F32)])
    small = jnp.concatenate(pieces + [tail]).reshape(-1, LANES)
    small = after(small, dx1)
    small = small_sum(small).reshape(-1)
    shares = lax.axis_size("dp")
    me = lax.axis_index("dp")
    order = ("gain2", "shift2", "bdown", "gain1", "shift1", "bout", "bq", "bv", "bup")

    def small_part(name):
        size = inner if name == "bup" else width
        own = size // shares
        start = order.index(name) * width + me * own
        return lax.dynamic_slice_in_dim(small, start, own, 0)[None]

    root_means = jnp.sqrt(small[base : base + 3] / (small[base + 3] * width))[None, :]

    half = width // 2
    dx0, out0, out1 = (after(array, dx1) for array in (dx0, out0, out1))
    outgoing = jnp.concatenate(
        [
            jnp.where(is_first, grad[:, half:], made[:, :half])
            for grad, made in ((dx0, out0), (dx1, out1))
        ]
    )
    arrived = lax.ppermute(outgoing, "section", [(0, 1), (1, 0)])
    block_own = jnp.concatenate([out0[:, half:], out1[:, half:]])
    grad_own = jnp.concatenate([dx0[:, :half], dx1[:, :half]])
    block_part = jnp.where(is_first, arrived, block_own)
    grad_part = jnp.where(is_first, grad_own, arrived)
    return (
        block_part,
        grad_part,
        w_qkv[None, :, :width],
        small_part("bq"),
        w_qkv[None, :, width : 2 * width],
        w_qkv[None, :, 2 * width :],
        small_part("bv"),
        w_out[None],
        small_part("bout"),
        small_part("gain1"),
        small_part("shift1"),
        w_up[None],
        small_part("bup"),
        w_down[None],
        small_part("bdown"),
        small_part("gain2"),
        small_part("shift2"),
        root_means,
    )


def solution(mesh):
    by_layer = P("section", None)
    matrix = P("section", None, None)
    share = P("section", "dp")
    matrix_share = P("section", "dp", None)
    return jax.shard_map(
        on_device,
        mesh=mesh,
        in_specs=(
            P("dp", None),
            P("dp", None),
            P("dp", None),
            P("dp", None),
            P("section", "dp", None, None),
            matrix,
            by_layer,
            matrix,
            matrix,
            by_layer,
            matrix,
            by_layer,
            by_layer,
            by_layer,
            matrix,
            by_layer,
            matrix,
            by_layer,
            by_layer,
            by_layer,
        ),
        out_specs=(
            P("dp", "section"),
            P("dp", "section"),
            matrix_share,
            share,
            matrix_share,
            matrix_share,
            share,
            matrix_share,
            share,
            share,
            share,
            matrix_share,
            share,
            matrix_share,
            share,
            share,
            share,
            P("section", None),
        ),
        check_vma=False,
    )
```

time: 483 us -> 407 us (0.84)
  the two profiles are of different devices: /device:TPU:20 before, /device:TPU:31 now
where the time goes in v2:
time: 407 us; the launch traced here: 401 us
  Pallas kernels  167 us (41%)
  waiting for transfers between devices  142 us (35%)
  starting transfers between devices  58.9 us (14%)
  other arithmetic  20.8 us (5%)
  local copies, waits for them, and re-layouts  9.89 us (2%)
    ppermute x20, waiting for transfers between devices, swap(): return lax.ppermute(array, 'dp', [(d, d ^ stride) for d in range(count)])  85.1 us
    pallas_call x8, Pallas kernels, backward(): pl.pallas_call(partial(backward_kernel, section, g_row, parts, pairs, len...  69.1 us
    pallas_call x4, Pallas kernels, forward(): pl.pallas_call(partial(forward_kernel, section, row, x_row, len(old), hea...  61.4 us
    ppermute x4, waiting for transfers between devices, hop(): return lax.ppermute(array, 'section', [(source, target)])  56.6 us
    ppermute x1, starting transfers between devices, on_device(): arrived = lax.ppermute(outgoing, 'section', [(0, 1), (1, 0)])  41 us
    pallas_call x4, Pallas kernels, outer(): pl.pallas_call(partial(outer_kernel, n_rows, tile, split_left, pairs), ou...  36.5 us
    convert_element_type x12, other arithmetic, add(): return (left.astype(F32) + right.astype(F32)).astype(BF16)  14.7 us
    ppermute x20, starting transfers between devices, swap(): return lax.ppermute(array, 'dp', [(d, d ^ stride) for d in range(count)])  12.6 us
  transfers between devices with their start and end apart: 25, of which 15 were waited for; matrix products, arithmetic and copies ran while one was open for 6% of the time, Pallas kernels for 35%

profile of v2, /device:TPU:31, one launch (start us, length us, event | category | flops | bytes accessed | tf_op | source)
XLA Modules:
  0.0 401.0 jit_solution(15823061210501395814)
XLA Ops:
  4.6 1.8 layer_forward.6
  7.6 42.5 %collective-permute-done.refs_0_ = bf16[512,768]{1,0:T(8,128)(2,1)S(1)} collective-permute-done((bf16[512,768]{1,0:T(8,128)(2,1)}, bf16[512,768]{1,0:T(8,128)(2,1)S(1)}, u32[]{:S(2)}, u32[]{:S(2)}) %collective-permute-start) | collective-permute-done | bytes 786464 | tf_op jit(solution)/shard_map/ppermute | solution.py:759
  51.0 29.2 %layer_forward.5 = (bf16[512,768]{1,0:T(8,128)(2,1)}, bf16[512,2304]{1,0:T(8,128)(2,1)}, bf16[512,768]{1,0:T(8,128)(2,1)}, f32[16,512]{1,0:T(8,128)}, f32[512,76...) custom-call(bf16[512,768]{1,0:T(8,128)(2,1)} %copy-done.12, ...), custom_call_target="tpu_custom_call", output_to_operand_aliasing={{0}: (19, {}), {1}: (20, {}), {2}: (21, {}), {3}: (22, {}),... | custom-call | flops 1 | bytes 1 | tf_op jit(solution)/shard_map/layer_forward/pallas_call | solution.py:316
  80.2 31.1 %backward_ffn_mid_att_dx.3 = (bf16[512,768]{1,0:T(8,128)(2,1)}, bf16[512,3072]{1,0:T(8,128)(2,1)}, f32[32,3072]{1,0:T(8,128)}, bf16[512,768]{1,0:T(8,128)(2,1)},...) custom-call(bf16[1024,768]{1,0:T(8,128)(2,1)} %refs_0_.7, ...), custom_call_target="tpu_custom_call" | custom-call | flops 1 | bytes 1 | tf_op jit(solution)/shard_map/backward_ffn_mid_att_dx/pallas_call | solution.py:593
  113.5 29.2 %layer_forward.7 = (bf16[512,768]{1,0:T(8,128)(2,1)}, bf16[512,2304]{1,0:T(8,128)(2,1)}, bf16[512,768]{1,0:T(8,128)(2,1)}, f32[16,512]{1,0:T(8,128)}, f32[512,76...) custom-call(bf16[512,768]{1,0:T(8,128)(2,1)} %copy-done.11, ...), custom_call_target="tpu_custom_call", output_to_operand_aliasing={{0}: (19, {}), {1}: (20, {}), {2}: (21, {}), {3}: (22, {}),... | custom-call | flops 1 | bytes 1 | tf_op jit(solution)/shard_map/layer_forward/pallas_call | solution.py:316
  142.7 31.3 %backward_ffn_mid_att_dx.4 = (bf16[512,768]{1,0:T(8,128)(2,1)}, bf16[512,3072]{1,0:T(8,128)(2,1)}, f32[32,3072]{1,0:T(8,128)}, bf16[512,768]{1,0:T(8,128)(2,1)},...) custom-call(bf16[1024,768]{1,0:T(8,128)(2,1)} %refs_0_.7, ...), custom_call_target="tpu_custom_call" | custom-call | flops 1 | bytes 1 | tf_op jit(solution)/shard_map/backward_ffn_mid_att_dx/pallas_call | solution.py:593
  177.5 14.1 %collective-permute-done.3.refs_0_ = bf16[512,768]{1,0:T(8,128)(2,1)S(1)} collective-permute-done((bf16[512,768]{1,0:T(8,128)(2,1)}, bf16[512,768]{1,0:T(8,128)(2,1)S(1)}, u32[]{:S(2)}, u32[]{:S(2)}) %collective-permute-start.3) | collective-permute-done | bytes 786464 | tf_op jit(solution)/shard_map/ppermute | solution.py:759
  193.7 11.3 %weight_gradient.4 = (bf16[8,192,768]{2,1,0:T(8,128)(2,1)}, bf16[8,192,768]{2,1,0:T(8,128)(2,1)}) custom-call(bf16[512,3072]{1,0:T(8,128)(2,1)} %get-tuple-element.206.refs_0_, bf16[512,3072]{1,0:T(8,128)(2,1)} %get-tuple-element.207.refs_1_, bf16[512,768]{1,0:T(8,128)(2,1)} %get-tuple-element.208.refs_2_, bf16[512,768]{1,0:T(8,128)(2,1)} %get-tuple-element.209.refs_3_), custom_call_target="tpu_custom_call" | custom-call | flops 1 | bytes 1 | tf_op jit(solution)/shard_map/weight_gradient/pallas_call | solution.py:656
  205.0 11.5 %weight_gradient.5 = (bf16[8,48,3072]{2,1,0:T(8,128)(2,1)}, bf16[8,48,3072]{2,1,0:T(8,128)(2,1)}) custom-call(bf16[512,768]{1,0:T(8,128)(2,1)} %get-tuple-element.203.refs_0_, bf16[512,768]{1,0:T(8,128)(2,1)} %get-tuple-element.204.refs_1_, bf16[512,3072]{1,0:T(8,128)(2,1)} %get-tuple-element.205.refs_2_, bf16[512,3072]{1,0:T(8,128)(2,1)} %get-tuple-element.211.refs_3_.refs_0_), custom_call_target="tpu_custom_call" | custom-call | flops 1 | bytes 1 | tf_op jit(solution)/shard_map/weight_gradient/pallas_call | solution.py:656
  216.5 1.9 collective-permute-start.5
  218.5 7.0 %collective-permute-done.5 = bf16[8,48,3072]{2,1,0:T(8,128)(2,1)} collective-permute-done((bf16[8,48,3072]{2,1,0:T(8,128)(2,1)}, bf16[8,48,3072]{2,1,0:T(8,128)(2,1)}, u32[]{:S(2)}, u32[]{:S(2)}) %collective-permute-start.5) | collective-permute-done | bytes 2359328 | tf_op jit(solution)/shard_map/ppermute | solution.py:675
  225.5 4.5 %add_convert_fusion.1 = (bf16[2,1,2,48,3072]{4,3,2,1,0:T(8,128)(2,1)S(1)}, bf16[2,1,2,48,3072]{4,3,2,1,0:T(8,128)(2,1)}) fusion(bf16[2,2,2,48,3072]{4,3,2,1,0:T(8,128)(2,1)} %bitcast.4, s32[]{:T(128)S(6)} %select_n.200, bf16[2,2,2,48,3072]{4,3,2,1,0:T(8,128)(2,1)} %bitcast.97, s32[]{:T(128)S(6)} %select_n.194), kind=kLoop, calls=%fused_computation.1 | loop fusion | flops 4718592 | bytes 7077896 | tf_op jit(solution)/shard_map/convert_element_type | solution.py:683
  231.6 3.2 add_convert_fusion
  236.2 4.5 %weight_gradient.6 = (bf16[8,48,768]{2,1,0:T(8,128)(2,1)}, bf16[8,48,768]{2,1,0:T(8,128)(2,1)}) custom-call(bf16[512,768]{1,0:T(8,128)(2,1)} %get-tuple-element.156.refs_9_.refs_0_, bf16[512,768]{1,0:T(8,128)(2,1)} %get-tuple-element.182.refs_9_.refs_6_.refs_1_, bf16[512,768]{1,0:T(8,128)(2,1)} %get-tuple-element.220.refs_2_, ...), custom_call_target="tpu_custom_call" | custom-call | flops 1 | bytes 1 | tf_op jit(solution)/shard_map/weight_gradient/pallas_call | solution.py:656
  245.4 9.2 %weight_gradient.7 = (bf16[8,48,2304]{2,1,0:T(8,128)(2,1)}, bf16[8,48,2304]{2,1,0:T(8,128)(2,1)}) custom-call(bf16[512,768]{1,0:T(8,128)(2,1)} %get-tuple-element.232.refs_0_, bf16[512,768]{1,0:T(8,128)(2,1)} %get-tuple-element.233.refs_1_, bf16[512,2304]{1,0:T(8,128)(2,1)} %get-tuple-element.234.refs_2_, bf16[512,2304]{1,0:T(8,128)(2,1)} %get-tuple-element.230.refs_3_.refs_0_), custom_call_target="tpu_custom_call" | custom-call | flops 1 | bytes 1 | tf_op jit(solution)/shard_map/weight_gradient/pallas_call | solution.py:656
  255.5 2.1 collective-permute-done.8
  257.5 4.5 %collective-permute-done.7 = bf16[4,192,768]{2,1,0:T(8,128)(2,1)} collective-permute-done((bf16[4,192,768]{2,1,0:T(8,128)(2,1)}, bf16[4,192,768]{2,1,0:T(8,128)(2,1)}, u32[]{:S(2)}, u32[]{:S(2)}) %collective-permute-start.7) | collective-permute-done | bytes 1179680 | tf_op jit(solution)/shard_map/ppermute | solution.py:675
  263.0 1.6 collective-permute-start.14
  264.6 1.5 add_convert_fusion.7
  267.5 1.7 add_convert_fusion.9
  272.7 18.4 %collective-permute-done.15 = f32[80,128]{1,0:T(8,128)S(1)} collective-permute-done((f32[80,128]{1,0:T(8,128)S(1)}, f32[80,128]{1,0:T(8,128)S(1)}, u32[]{:S(2)}, u32[]{:S(2)}) %collective-permute-start.15) | collective-permute-done | bytes 40992 | tf_op jit(solution)/shard_map/ppermute | solution.py:675
  291.5 2.5 collective-permute-done.16
  294.1 3.9 collective-permute-done.17
  298.1 41.0 %collective-permute-start.9 = (bf16[1024,384]{1,0:T(8,128)(2,1)S(1)}, bf16[1024,384]{1,0:T(8,128)(2,1)S(1)}, u32[]{:S(2)}, u32[]{:S(2)}) collective-permute-start(bf16[1024,384]{1,0:T(8,128)(2,1)S(1)} %pad_maximum_fusion), channel_id=1, source_target_pairs={{0,16},{16,0},{1,17},{17,1},{2,18},{18,2},{3,19},{19,3},{4,20},{20... | collective-permute-start | bytes 2359304 | tf_op jit(solution)/shard_map/ppermute | solution.py:867
  342.3 2.5 collective-permute-done.19
  344.9 1.9 add_convert_fusion.5
  348.1 1.6 collective-permute-done.20
  351.3 1.7 collective-permute-start.22
  355.0 8.2 %collective-permute-done.11 = bf16[4,48,2304]{2,1,0:T(8,128)(2,1)S(1)} collective-permute-done((bf16[4,48,2304]{2,1,0:T(8,128)(2,1)S(1)}, bf16[4,48,2304]{2,1,0:T(8,128)(2,1)S(1)}, u32[]{:S(2)}, u32[]{:S(2)}) %collective-permute-start.11) | collective-permute-done | bytes 884768 | tf_op jit(solution)/shard_map/ppermute | solution.py:675
  363.5 10.7 %collective-permute-done.22 = bf16[1,48,3072]{2,1,0:T(8,128)(2,1)S(1)} collective-permute-done((bf16[1,48,3072]{2,1,0:T(8,128)(2,1)S(1)}, bf16[1,48,3072]{2,1,0:T(8,128)(2,1)S(1)}, u32[]{:S(2)}, u32[]{:S(2)}) %collective-permute-start.22) | collective-permute-done | bytes 294944 | tf_op jit(solution)/shard_map/ppermute | solution.py:675
  375.1 12.6 %collective-permute-done.12 = bf16[2,48,2304]{2,1,0:T(8,128)(2,1)S(1)} collective-permute-done((bf16[2,48,2304]{2,1,0:T(8,128)(2,1)S(1)}, bf16[2,48,2304]{2,1,0:T(8,128)(2,1)S(1)}, u32[]{:S(2)}, u32[]{:S(2)}) %collective-permute-start.12) | collective-permute-done | bytes 442400 | tf_op jit(solution)/shard_map/ppermute | solution.py:675
  388.8 11.0 %collective-permute-done.13 = bf16[1,48,2304]{2,1,0:T(8,128)(2,1)S(1)} collective-permute-done((bf16[1,48,2304]{2,1,0:T(8,128)(2,1)S(1)}, bf16[1,48,2304]{2,1,0:T(8,128)(2,1)S(1)}, u32[]{:S(2)}, u32[]{:S(2)}) %collective-permute-start.13) | collective-permute-done | bytes 221216 | tf_op jit(solution)/shard_map/ppermute | solution.py:675
  (127 shorter events, 38.9 us)
Async XLA Ops:
  3.3 46.9 %collective-permute-start = (bf16[512,768]{1,0:T(8,128)(2,1)}, bf16[512,768]{1,0:T(8,128)(2,1)S(1)}, u32[]{:S(2)}, u32[]{:S(2)}) collective-permute-start(bf16[512,768]{1,0:T(8,128)(2,1)} %get-tuple-element.137), channel_id=1, source_target_pairs={{0,16},{1,17},{2,18},{3,19},{4,20},{5,21},{6,22},{7,23},{8,24},{9,... | collective-permute-start | bytes 2359304 | tf_op jit(solution)/shard_map/ppermute | solution.py:759
  6.3 106.3 %collective-permute-start.2 = (bf16[512,768]{1,0:T(8,128)(2,1)}, bf16[512,768]{1,0:T(8,128)(2,1)S(1)}, u32[]{:S(2)}, u32[]{:S(2)}) collective-permute-start(bf16[512,768]{1,0:T(8,128)(2,1)} %get-tuple-element.162), channel_id=1, source_target_pairs={{0,16},{1,17},{2,18},{3,19},{4,20},{5,21},{6,22},{7,23},{8,24},{9,... | collective-permute-start | bytes 2359304 | tf_op jit(solution)/shard_map/ppermute | solution.py:759
  111.3 64.2 %collective-permute-start.1 = (bf16[512,768]{1,0:T(8,128)(2,1)}, bf16[512,768]{1,0:T(8,128)(2,1)S(1)}, u32[]{:S(2)}, u32[]{:S(2)}) collective-permute-start(bf16[512,768]{1,0:T(8,128)(2,1)} %get-tuple-element.161.refs_26_), channel_id=1, source_target_pairs={{16,0},{17,1},{18,2},{19,3},{20,4},{21,5},{22,6},{23,7},{24,8},{25... | collective-permute-start | bytes 2359304 | tf_op jit(solution)/shard_map/ppermute | solution.py:759
  174.1 17.5 %collective-permute-start.3 = (bf16[512,768]{1,0:T(8,128)(2,1)}, bf16[512,768]{1,0:T(8,128)(2,1)S(1)}, u32[]{:S(2)}, u32[]{:S(2)}) collective-permute-start(bf16[512,768]{1,0:T(8,128)(2,1)} %get-tuple-element.187.refs_7_), channel_id=1, source_target_pairs={{16,0},{17,1},{18,2},{19,3},{20,4},{21,5},{22,6},{23,7},{24,8},{25... | collective-permute-start | bytes 2359304 | tf_op jit(solution)/shard_map/ppermute | solution.py:759
  216.5 9.0 %collective-permute-start.5 = (bf16[8,48,3072]{2,1,0:T(8,128)(2,1)}, bf16[8,48,3072]{2,1,0:T(8,128)(2,1)}, u32[]{:S(2)}, u32[]{:S(2)}) collective-permute-start(bf16[8,48,3072]{2,1,0:T(8,128)(2,1)} %get-tuple-element.218), channel_id=1, source_target_pairs={{0,1},{1,0},{2,3},{3,2},{4,5},{5,4},{6,7},{7,6},{8,9},{9,8},{10,11... | collective-permute-start | bytes 7077896 | tf_op jit(solution)/shard_map/ppermute | solution.py:675
  218.4 11.8 %collective-permute-start.4 = (bf16[8,192,768]{2,1,0:T(8,128)(2,1)}, bf16[8,192,768]{2,1,0:T(8,128)(2,1)S(1)}, u32[]{:S(2)}, u32[]{:S(2)}) collective-permute-start(bf16[8,192,768]{2,1,0:T(8,128)(2,1)} %get-tuple-element.213), channel_id=1, source_target_pairs={{0,1},{1,0},{2,3},{3,2},{4,5},{5,4},{6,7},{7,6},{8,9},{9,8},{10,11... | collective-permute-start | bytes 7077896 | tf_op jit(solution)/shard_map/ppermute | solution.py:675
  230.0 27.5 %collective-permute-start.8 = (bf16[4,48,3072]{2,1,0:T(8,128)(2,1)}, bf16[4,48,3072]{2,1,0:T(8,128)(2,1)}, u32[]{:S(2)}, u32[]{:S(2)}) collective-permute-start(bf16[4,48,3072]{2,1,0:T(8,128)(2,1)} %bitcast.5), channel_id=1, source_target_pairs={{0,4},{1,5},{2,6},{3,7},{4,0},{5,1},{6,2},{7,3},{8,12},{9,13},{10,... | collective-permute-start | bytes 3538952 | tf_op jit(solution)/shard_map/ppermute | solution.py:675
  234.8 27.2 %collective-permute-start.7 = (bf16[4,192,768]{2,1,0:T(8,128)(2,1)}, bf16[4,192,768]{2,1,0:T(8,128)(2,1)}, u32[]{:S(2)}, u32[]{:S(2)}) collective-permute-start(bf16[4,192,768]{2,1,0:T(8,128)(2,1)} %get-tuple-element.257), channel_id=1, source_target_pairs={{0,2},{1,3},{2,0},{3,1},{4,6},{5,7},{6,4},{7,5},{8,10},{9,11},{10,... | collective-permute-start | bytes 3538952 | tf_op jit(solution)/shard_map/ppermute | solution.py:675
  236.2 6.5 %copy-start.5 = (f32[32,3072]{1,0:T(8,128)S(1)}, f32[32,3072]{1,0:T(8,128)}, u32[]{:S(2)}) copy-start(f32[32,3072]{1,0:T(8,128)} %get-tuple-element.243) | copy-start | bytes 1179652
  240.8 3.3 collective-permute-start.6
  245.4 9.2 %copy-start.16 = (f32[16,768]{1,0:T(8,128)S(1)}, f32[16,768]{1,0:T(8,128)}, u32[]{:S(2)}) copy-start(f32[16,768]{1,0:T(8,128)} %get-tuple-element.249) | copy-start | bytes 147460
  245.4 9.2 %copy-start.17 = (f32[16,768]{1,0:T(8,128)S(1)}, f32[16,768]{1,0:T(8,128)}, u32[]{:S(2)}) copy-start(f32[16,768]{1,0:T(8,128)} %get-tuple-element.247) | copy-start | bytes 147460
  245.4 9.2 %copy-start.23 = (f32[16,768]{1,0:T(8,128)S(1)}, f32[16,768]{1,0:T(8,128)}, u32[]{:S(2)}) copy-start(f32[16,768]{1,0:T(8,128)} %get-tuple-element.248) | copy-start | bytes 147460
  254.6 90.3 %collective-permute-start.10 = (bf16[8,48,2304]{2,1,0:T(8,128)(2,1)}, bf16[8,48,2304]{2,1,0:T(8,128)(2,1)}, u32[]{:S(2)}, u32[]{:S(2)}) collective-permute-start(bf16[8,48,2304]{2,1,0:T(8,128)(2,1)} %get-tuple-element.242), channel_id=1, source_target_pairs={{0,1},{1,0},{2,3},{3,2},{4,5},{5,4},{6,7},{7,6},{8,9},{9,8},{10,11... | collective-permute-start | bytes 5308424 | tf_op jit(solution)/shard_map/ppermute | solution.py:675
  263.0 9.0 %collective-permute-start.14 = (f32[80,128]{1,0:T(8,128)S(1)}, f32[80,128]{1,0:T(8,128)S(1)}, u32[]{:S(2)}, u32[]{:S(2)}) collective-permute-start(f32[80,128]{1,0:T(8,128)S(1)} %bitcast.103), channel_id=1, source_target_pairs={{0,1},{1,0},{2,3},{3,2},{4,5},{5,4},{6,7},{7,6},{8,9},{9,8},{10,11... | collective-permute-start | bytes 122888 | tf_op jit(solution)/shard_map/ppermute | solution.py:675
  266.2 84.2 %collective-permute-start.23 = (bf16[2,192,768]{2,1,0:T(8,128)(2,1)S(1)}, bf16[2,192,768]{2,1,0:T(8,128)(2,1)S(1)}, u32[]{:S(2)}, u32[]{:S(2)}) collective-permute-start(bf16[2,192,768]{2,1,0:T(8,128)(2,1)S(1)} %get-tuple-element.263), channel_id=1, source_target_pairs={{0,4},{1,5},{2,6},{3,7},{4,0},{5,1},{6,2},{7,3},{8,12},{9,13},{10,... | collective-permute-start | bytes 1769480 | tf_op jit(solution)/shard_map/ppermute | solution.py:675
  269.3 82.0 %collective-permute-start.21 = (bf16[2,48,3072]{2,1,0:T(8,128)(2,1)S(1)}, bf16[2,48,3072]{2,1,0:T(8,128)(2,1)S(1)}, u32[]{:S(2)}, u32[]{:S(2)}) collective-permute-start(bf16[2,48,3072]{2,1,0:T(8,128)(2,1)S(1)} %get-tuple-element.265), channel_id=1, source_target_pairs={{0,2},{1,3},{2,0},{3,1},{4,6},{5,7},{6,4},{7,5},{8,10},{9,11},{10,... | collective-permute-start | bytes 1769480 | tf_op jit(solution)/shard_map/ppermute | solution.py:675
  270.9 20.4 %copy-start.1 = (bf16[512,768]{1,0:T(8,128)(2,1)S(1)}, bf16[512,768]{1,0:T(8,128)(2,1)}, u32[]{:S(2)}) copy-start(bf16[512,768]{1,0:T(8,128)(2,1)} %get-tuple-element.237) | copy-start | bytes 2359300
  270.9 20.4 %copy-start.8 = (bf16[512,768]{1,0:T(8,128)(2,1)S(1)}, bf16[512,768]{1,0:T(8,128)(2,1)}, u32[]{:S(2)}) copy-start(bf16[512,768]{1,0:T(8,128)(2,1)} %get-tuple-element.239) | copy-start | bytes 2359300
  270.9 69.4 %collective-permute-start.18 = (bf16[4,48,768]{2,1,0:T(8,128)(2,1)S(1)}, bf16[4,48,768]{2,1,0:T(8,128)(2,1)S(1)}, u32[]{:S(2)}, u32[]{:S(2)}) collective-permute-start(bf16[4,48,768]{2,1,0:T(8,128)(2,1)S(1)} %get-tuple-element.269), channel_id=1, source_target_pairs={{0,2},{1,3},{2,0},{3,1},{4,6},{5,7},{6,4},{7,5},{8,10},{9,11},{10,... | collective-permute-start | bytes 884744 | tf_op jit(solution)/shard_map/ppermute | solution.py:675
  272.1 19.0 %collective-permute-start.15 = (f32[80,128]{1,0:T(8,128)S(1)}, f32[80,128]{1,0:T(8,128)S(1)}, u32[]{:S(2)}, u32[]{:S(2)}) collective-permute-start(f32[80,128]{1,0:T(8,128)S(1)} %add.334), channel_id=1, source_target_pairs={{0,2},{1,3},{2,0},{3,1},{4,6},{5,7},{6,4},{7,5},{8,10},{9,11},{10,... | collective-permute-start | bytes 122888 | tf_op jit(solution)/shard_map/ppermute | solution.py:675
  291.1 2.9 collective-permute-start.16
  291.5 53.4 %copy-start.4 = (bf16[8,48,2304]{2,1,0:T(8,128)(2,1)S(1)}, bf16[8,48,2304]{2,1,0:T(8,128)(2,1)}, u32[]{:S(2)}) copy-start(bf16[8,48,2304]{2,1,0:T(8,128)(2,1)} %get-tuple-element.235) | copy-start | bytes 5308420
  294.0 4.1 %collective-permute-start.17 = (f32[80,128]{1,0:T(8,128)S(1)}, f32[80,128]{1,0:T(8,128)S(1)}, u32[]{:S(2)}, u32[]{:S(2)}) collective-permute-start(f32[80,128]{1,0:T(8,128)S(1)} %add.336), channel_id=1, source_target_pairs={{0,8},{1,9},{2,10},{3,11},{4,12},{5,13},{6,14},{7,15},{8,0},{9,1},... | collective-permute-start | bytes 122888 | tf_op jit(solution)/shard_map/ppermute | solution.py:675
  298.1 55.4 %collective-permute-start.9 = (bf16[1024,384]{1,0:T(8,128)(2,1)S(1)}, bf16[1024,384]{1,0:T(8,128)(2,1)S(1)}, u32[]{:S(2)}, u32[]{:S(2)}) collective-permute-start(bf16[1024,384]{1,0:T(8,128)(2,1)S(1)} %pad_maximum_fusion), channel_id=1, source_target_pairs={{0,16},{16,0},{1,17},{17,1},{2,18},{18,2},{3,19},{19,3},{4,20},{20... | collective-permute-start | bytes 2359304 | tf_op jit(solution)/shard_map/ppermute | solution.py:867
  340.4 4.4 %collective-permute-start.19 = (bf16[2,48,768]{2,1,0:T(8,128)(2,1)S(1)}, bf16[2,48,768]{2,1,0:T(8,128)(2,1)S(1)}, u32[]{:S(2)}, u32[]{:S(2)}) collective-permute-start(bf16[2,48,768]{2,1,0:T(8,128)(2,1)S(1)} %get-tuple-element.279), channel_id=1, source_target_pairs={{0,4},{1,5},{2,6},{3,7},{4,0},{5,1},{6,2},{7,3},{8,12},{9,13},{10,... | collective-permute-start | bytes 442376 | tf_op jit(solution)/shard_map/ppermute | solution.py:675
  344.8 4.8 %collective-permute-start.20 = (bf16[1,48,768]{2,1,0:T(8,128)(2,1)S(1)}, bf16[1,48,768]{2,1,0:T(8,128)(2,1)S(1)}, u32[]{:S(2)}, u32[]{:S(2)}) collective-permute-start(bf16[1,48,768]{2,1,0:T(8,128)(2,1)S(1)} %fusion.13), channel_id=1, source_target_pairs={{0,8},{1,9},{2,10},{3,11},{4,12},{5,13},{6,14},{7,15},{8,0},{9,1},... | collective-permute-start | bytes 221192 | tf_op jit(solution)/shard_map/ppermute | solution.py:675
  346.8 16.4 %collective-permute-start.11 = (bf16[4,48,2304]{2,1,0:T(8,128)(2,1)S(1)}, bf16[4,48,2304]{2,1,0:T(8,128)(2,1)S(1)}, u32[]{:S(2)}, u32[]{:S(2)}) collective-permute-start(bf16[4,48,2304]{2,1,0:T(8,128)(2,1)S(1)} %get-tuple-element.261), channel_id=1, source_target_pairs={{0,2},{1,3},{2,0},{3,1},{4,6},{5,7},{6,4},{7,5},{8,10},{9,11},{10,... | collective-permute-start | bytes 2654216 | tf_op jit(solution)/shard_map/ppermute | solution.py:675
  350.4 37.4 %collective-permute-start.24 = (bf16[1,192,768]{2,1,0:T(8,128)(2,1)S(1)}, bf16[1,192,768]{2,1,0:T(8,128)(2,1)S(1)}, u32[]{:S(2)}, u32[]{:S(2)}) collective-permute-start(bf16[1,192,768]{2,1,0:T(8,128)(2,1)S(1)} %fusion.4), channel_id=1, source_target_pairs={{0,8},{1,9},{2,10},{3,11},{4,12},{5,13},{6,14},{7,15},{8,0},{9,1},... | collective-permute-start | bytes 884744 | tf_op jit(solution)/shard_map/ppermute | solution.py:675
  351.3 22.9 %collective-permute-start.22 = (bf16[1,48,3072]{2,1,0:T(8,128)(2,1)S(1)}, bf16[1,48,3072]{2,1,0:T(8,128)(2,1)S(1)}, u32[]{:S(2)}, u32[]{:S(2)}) collective-permute-start(bf16[1,48,3072]{2,1,0:T(8,128)(2,1)S(1)} %fusion.6), channel_id=1, source_target_pairs={{0,8},{1,9},{2,10},{3,11},{4,12},{5,13},{6,14},{7,15},{8,0},{9,1},... | collective-permute-start | bytes 884744 | tf_op jit(solution)/shard_map/ppermute | solution.py:675
  363.4 24.3 %collective-permute-start.12 = (bf16[2,48,2304]{2,1,0:T(8,128)(2,1)S(1)}, bf16[2,48,2304]{2,1,0:T(8,128)(2,1)S(1)}, u32[]{:S(2)}, u32[]{:S(2)}) collective-permute-start(bf16[2,48,2304]{2,1,0:T(8,128)(2,1)S(1)} %get-tuple-element.267), channel_id=1, source_target_pairs={{0,4},{1,5},{2,6},{3,7},{4,0},{5,1},{6,2},{7,3},{8,12},{9,13},{10,... | collective-permute-start | bytes 1327112 | tf_op jit(solution)/shard_map/ppermute | solution.py:675
  387.8 12.0 %collective-permute-start.13 = (bf16[1,48,2304]{2,1,0:T(8,128)(2,1)S(1)}, bf16[1,48,2304]{2,1,0:T(8,128)(2,1)S(1)}, u32[]{:S(2)}, u32[]{:S(2)}) collective-permute-start(bf16[1,48,2304]{2,1,0:T(8,128)(2,1)S(1)} %fusion.9), channel_id=1, source_target_pairs={{0,8},{1,9},{2,10},{3,11},{4,12},{5,13},{6,14},{7,15},{8,0},{9,1},... | collective-permute-start | bytes 663560 | tf_op jit(solution)/shard_map/ppermute | solution.py:675
  (17 other events, 58.9 us)

commit v3 on v0

v3 whole, which is shorter than its diff:
```python
from functools import partial

import jax
import jax.numpy as jnp
from jax import lax
from jax.experimental import pallas as pl
from jax.experimental.pallas import tpu as pltpu
from jax.sharding import PartitionSpec as P

HEAD_DIM = 64
CLUSTER = 128
SEQ = 512
LANES = 128
ROW_BLOCK = 128
PAIR_UNROLL = 2
MIB = 1024 * 1024

BF16 = jnp.bfloat16
F32 = jnp.float32
LOG2E = 1.4426950408889634
SCALE = HEAD_DIM**-0.5
SCORE_SCALE = SCALE * LOG2E

NN = ((1,), (0,))
NT = ((1,), (1,))
TN = ((0,), (0,))

ROWS = "dp"
LAYER = "section"
ANY = pl.BlockSpec(memory_space=pltpu.HBM)
WHOLE = pl.BlockSpec(memory_space=pltpu.VMEM)
SHORT = pl.CostEstimate(flops=1, bytes_accessed=1, transcendentals=0)

X, QKV, CTX, LSE, KID, QID, N1, R1, HID, ACT, GP, N2, R2 = range(13)
G, DFFN, DUP, DBR, DQKV, SUMS_A, SUMS_B, SUMS_C, WIDE, DCTX, DELTA, DX, FEED, LIVE = range(13, 27)
BIAS, WQKV, Y, STATS, WO, WU, WD, REST = range(27, 35)
SAVED = (X, QKV, CTX, LSE, KID, QID, N1, R1, HID, ACT, GP, N2, R2)
GRADS = (DFFN, DUP, DBR, DQKV, SUMS_A, SUMS_B, SUMS_C)
GAIN2, SHIFT2, B_DOWN, B_UP = 0, 8, 16, 24
GAIN1, SHIFT1, B_OUT = 0, 8, 16
B_QUERY, B_VALUE = 0, 8


def shapes_of(width, inner):
    token, token32, narrow = ((SEQ, width), BF16), ((SEQ, width), F32), ((SEQ, LANES), F32)
    heads = ((16, SEQ), F32)
    shapes = {name: token for name in (X, CTX, N1, HID, N2, G, DFFN, DBR, DCTX, DX, Y)}
    shapes.update({name: token32 for name in (KID, WIDE, FEED)})
    shapes.update({name: narrow for name in (R1, R2, LIVE)})
    shapes.update({name: heads for name in (LSE, QID, DELTA)})
    shapes.update({name: ((SEQ, inner), BF16) for name in (ACT, GP, DUP)})
    shapes.update({name: ((SEQ, 3 * width), BF16) for name in (QKV, DQKV)})
    shapes.update({SUMS_A: ((32, inner), F32), SUMS_B: ((24, width), F32)})
    shapes.update({SUMS_C: ((16, width), F32), STATS: ((24, width), F32), BIAS: ((8, width), F32)})
    shapes.update({WQKV: ((width, 3 * width), BF16), WO: ((width, width), BF16)})
    shapes.update({WU: ((width, inner), BF16), WD: ((inner, width), BF16)})
    shapes[REST] = ((width, 4 * width), BF16)
    return shapes


def mm(left, right, dims):
    return lax.dot_general(left, right, (dims, ((), ())), preferred_element_type=F32)


def vec(ref):
    return ref[0:1, :].astype(F32)


def lanes_at(start, size=LANES):
    return pl.ds(pl.multiple_of(start, LANES), size)


def fold8(block):
    return jnp.sum(block.reshape(-1, 8, block.shape[-1]), axis=0)


def over_rows(step):
    def body(i, carry):
        step(pl.ds(pl.multiple_of(i * ROW_BLOCK, ROW_BLOCK), ROW_BLOCK))
        return carry

    lax.fori_loop(0, SEQ // ROW_BLOCK, body, 0)


def over_tiles(size, tile, step):
    def body(i, carry):
        step(pl.ds(pl.multiple_of(i * tile, tile), tile))
        return carry

    lax.fori_loop(0, size // tile, body, 0)


class Copies:
    def __init__(self, at, sems):
        self.at, self.sems = at, sems
        self.used = 0
        self.loads = {}
        self.stores = []

    def plan(self, source, target):
        self.used += 1
        return pltpu.make_async_copy(source, target, self.sems.at[self.used - 1])

    def load(self, name, source, target=None, now=True):
        target = self.at[name] if target is None else target
        copy = self.plan(source, target)
        self.loads.setdefault(name, []).append(copy)
        if now:
            copy.start()

    def go(self):
        for copies in self.loads.values():
            for copy in copies:
                copy.start()

    def ready(self, *names):
        for name in names:
            for copy in self.loads.pop(name, ()):
                copy.wait()

    def store(self, source, target, now=True):
        copy = self.plan(source, target)
        self.stores.append(copy)
        if now:
            copy.start()
        return copy

    def finish(self):
        for copy in self.stores:
            copy.wait()


def load_qkv(copies, weights, width):
    for i, weight in enumerate(weights):
        copies.load(WQKV, weight.at[0], copies.at[WQKV].at[:, pl.ds(i * width, width)])


def call(body, name, inputs, old, outs, scratch, n_sems):
    arrays = [array for array, _ in inputs]
    n_in = len(arrays)
    return pl.pallas_call(
        partial(body, n_in, len(old), len(outs)),
        out_shape=[jax.ShapeDtypeStruct(*shape) for shape in outs],
        in_specs=[spec for _, spec in inputs] + [ANY] * len(old),
        out_specs=[ANY] * len(outs),
        input_output_aliases={n_in + i: place for i, place in enumerate(old)},
        scratch_shapes=[pltpu.VMEM(*shape) for shape in scratch]
        + [pltpu.SemaphoreType.DMA((n_sems,))],
        compiler_params=pltpu.CompilerParams(vmem_limit_bytes=58 * MIB),
        cost_estimate=SHORT,
        name=name,
    )(*arrays, *old.values())


def split_refs(n_in, n_old, n_out, refs):
    return refs[:n_in], refs[n_in + n_old : n_in + n_old + n_out], refs[n_in + n_old + n_out :]


def low_lanes():
    return lax.broadcasted_iota(jnp.int32, (SEQ, LANES), 1) < HEAD_DIM


def masked(scores, kid_column, qid_row):
    shape = (CLUSTER, CLUSTER)
    same = lax.broadcasted_iota(jnp.int32, shape, 0) == lax.broadcasted_iota(jnp.int32, shape, 1)
    count = SEQ // CLUSTER
    parts = [slice(i * CLUSTER, (i + 1) * CLUSTER) for i in range(count)]
    rows = []
    for i in range(count):
        tiles = []
        for j in range(count):
            ok = kid_column[parts[i]] == qid_row[:, parts[j]]
            if i == j:
                ok = ok | same
            tiles.append(jnp.where(ok, scores[parts[i], parts[j]], -1e30))
        rows.append(jnp.concatenate(tiles, axis=1))
    return jnp.concatenate(rows, axis=0)


def attend_pair(j, width, at):
    low = low_lanes()
    lanes = lanes_at(j * LANES)
    query = at[QKV][:, lanes]
    key = at[QKV][:, lanes_at(width + j * LANES)]
    value = at[QKV][:, lanes_at(2 * width + j * LANES)]
    kid_pair = at[KID][:, lanes]
    mixed, tops = [], []
    for half in (0, 1):
        own = low if half == 0 else ~low
        own_query = jnp.where(own, query, jnp.zeros_like(query))
        value_ones = jnp.where(own, value, jnp.ones_like(value))
        kid_column = kid_pair[:, half * HEAD_DIM : half * HEAD_DIM + 1]
        scores = mm(key, own_query, NT) * SCORE_SCALE
        scores = masked(scores, kid_column, at[QID][pl.ds(2 * j + half, 1), :])
        top = jnp.max(scores, axis=0, keepdims=True)
        tops.append(top)
        mixed.append(mm(jnp.exp2(scores - top).astype(BF16), value_ones, TN))
    sums = [pltpu.roll(part, HEAD_DIM, 1) for part in mixed]
    total = jnp.where(low, sums[0], sums[1])
    at[CTX][:, lanes] = (jnp.where(low, mixed[0], mixed[1]) / total).astype(BF16)
    turned = total.T
    for half in (0, 1):
        row = turned[half * HEAD_DIM : half * HEAD_DIM + 1, :]
        at[LSE][pl.ds(2 * j + half, 1), :] = tops[half] + jnp.log2(row)


def attend_pair_back(j, width, at, target, base):
    low = low_lanes()
    lanes = [lanes_at(i * width + j * LANES) for i in range(3)]
    query, key, value = (at[QKV][:, part] for part in lanes)
    d_out = at[DCTX][:, lanes[0]]
    kid_pair = at[KID][:, lanes[0]]
    d_query, d_key, d_value = [], [], []
    for half in (0, 1):
        h = pl.ds(2 * j + half, 1)
        own = low if half == 0 else ~low
        own_query = jnp.where(own, query, jnp.zeros_like(query))
        own_out = jnp.where(own, d_out, jnp.zeros_like(d_out))
        kid_column = kid_pair[:, half * HEAD_DIM : half * HEAD_DIM + 1]
        scores = mm(key, own_query, NT) * SCORE_SCALE - at[LSE][h, :]
        weights = jnp.exp2(masked(scores, kid_column, at[QID][h, :]))
        d_weights = mm(value, own_out, NT)
        d_scores = (weights * (d_weights - at[DELTA][h, :])).astype(BF16)
        d_value.append(mm(weights.astype(BF16), own_out, NN))
        d_key.append(mm(d_scores, own_query, NN))
        d_query.append(mm(d_scores, key, TN))
    made = (
        jnp.where(low, d_query[0], d_query[1]) * SCALE,
        (d_key[0] + d_key[1]) * SCALE,
        d_value[0] + d_value[1],
    )
    rows = pl.ds(base, SEQ)
    for i, place in ((0, B_QUERY), (1, None), (2, B_VALUE)):
        rounded = made[i].astype(BF16)
        target[rows, lanes[i]] = rounded
        if place is not None:
            at[SUMS_C][place : place + 8, lanes[0]] = fold8(rounded.astype(F32))


def over_pairs(width, step):
    def body(j, carry):
        step(j)
        return carry

    lax.fori_loop(0, width // LANES, body, 0, unroll=PAIR_UNROLL)


def token_ids(row, heads, perm_ref, seg_ref, valid_ref, kid_ref, qid_ref):
    token = lax.broadcasted_iota(jnp.int32, (SEQ, LANES), 0)
    lane = lax.broadcasted_iota(jnp.int32, (SEQ, LANES), 1)
    seg_row = seg_ref[row : row + 1, :].astype(F32)
    valid_row = valid_ref[row : row + 1, :].astype(F32)
    at = lax.broadcasted_iota(jnp.int32, (LANES, SEQ), 0)
    both = jnp.where(at == 0, seg_row, jnp.where(at == 1, valid_row, 0.0)).T
    segment, live = both[:, 0:1], both[:, 1:2]

    def column(h):
        places = perm_ref[0, row, pl.ds(h, 1), :]
        mine = jnp.zeros((SEQ, LANES), F32)
        for c in range(1, SEQ // CLUSTER):
            part = places[:, c * CLUSTER : (c + 1) * CLUSTER]
            mine = jnp.where(token == part, float(c), mine)
        return jnp.sum(mine, axis=1, keepdims=True) * 4.0 + segment

    def pair(j, ids):
        left, right = column(2 * j), column(2 * j + 1)
        own = jnp.where(lane < HEAD_DIM, left, right)
        kid_ref[:, lanes_at(j * LANES)] = jnp.where(live > 0.5, own, -1.0)
        ids = jnp.where(lane == 2 * j, left, ids)
        return jnp.where(lane == 2 * j + 1, right, ids)

    qid = lax.fori_loop(0, heads // 2, pair, jnp.zeros((SEQ, LANES), F32))
    qid_ref[...] = qid.T[0:16, :]
    return live


def normed(total):
    centre = total - jnp.mean(total, axis=-1, keepdims=True)
    spread = jnp.mean(centre * centre, axis=-1, keepdims=True)
    rate = lax.rsqrt(spread + 1e-05)
    return centre * rate, rate


FORWARD_HELD = SAVED + (WQKV, WO, WU, WD, WIDE, FEED, Y, STATS, LIVE, BIAS)


def forward_kernel(section, row, x_row, heads, n_in, n_old, n_out, *refs):
    ins, outs, refs = split_refs(n_in, n_old, n_out, refs)
    x_hbm, perm_ref, seg_ref, valid_ref = ins[:4]
    wq, bq, wk, wv, bv, wo, bo, g1, s1, wu, bu, wd, bd, g2, s2 = ins[4:]
    out = dict(zip(SAVED + (Y, STATS), outs))
    at = dict(zip(FORWARD_HELD, refs))
    width, inner = at[WU].shape

    @pl.when(lax.axis_index(LAYER) == section)
    def _():
        copies = Copies(at, refs[-1])

        def save(*names):
            for name in names:
                copies.store(at[name], out[name])

        copies.load(X, x_hbm.at[pl.ds(x_row * SEQ, SEQ), :])
        first = copies.used
        load_qkv(copies, (wq, wk, wv), width)
        live = token_ids(row, heads, perm_ref, seg_ref, valid_ref, at[KID], at[QID])
        at[LIVE][...] = jnp.broadcast_to(live, (SEQ, LANES))
        at[LSE][...] = jnp.zeros((16, SEQ), F32)
        at[STATS][...] = jnp.zeros((24, width), F32)
        at[BIAS][0:1, :] = vec(bq)
        at[BIAS][1:2, :] = jnp.zeros((1, width), F32)
        at[BIAS][2:3, :] = vec(bv)
        copies.ready(X)

        def to_qkv(i, carry):
            part = pl.ds(pl.multiple_of(i * width, LANES), width)
            weight = at[WQKV].at[:, part]
            pltpu.make_async_copy(weight, weight, copies.sems.at[first + i]).wait()
            made = mm(at[X][...], at[WQKV][:, part], NN) + at[BIAS][pl.ds(i, 1), :]
            at[QKV][:, part] = made.astype(BF16)
            return carry

        lax.fori_loop(0, 3, to_qkv, 0)
        copies.load(WO, wo.at[0])
        copies.load(WU, wu.at[0])
        copies.load(WD, wd.at[0])
        save(KID, QID, X, QKV)
        over_pairs(width, lambda j: attend_pair(j, width, at))
        save(LSE, CTX)
        copies.ready(WO)
        at[WIDE][...] = mm(at[CTX][...], at[WO][...], NN)

        def first_norm(rows):
            branch = at[WIDE][rows, :] + vec(bo)
            alive = at[LIVE][rows, 0:1]
            at[STATS][0:8, :] += fold8(branch * branch * alive)
            unit, rate = normed(at[X][rows, :].astype(F32) + branch)
            hidden = unit * vec(g1) + vec(s1)
            at[N1][rows, :] = unit.astype(BF16)
            at[R1][rows, :] = jnp.broadcast_to(rate, (ROW_BLOCK, LANES))
            at[HID][rows, :] = hidden.astype(BF16)
            at[WIDE][rows, :] = hidden

        over_rows(first_norm)
        save(N1, R1, HID)
        copies.ready(WU)

        def up(part):
            upper = mm(at[HID][...], at[WU][:, part], NN) + bu[0:1, part].astype(F32)
            half = 0.5 + 0.5 * lax.erf(upper * 0.5**0.5)
            bell = jnp.exp2(upper * upper * (-0.5 * LOG2E)) * 0.3989422804014327
            at[ACT][:, part] = (upper * half).astype(BF16)
            at[GP][:, part] = (half + upper * bell).astype(BF16)

        over_tiles(inner, inner // 4, up)
        save(ACT, GP)
        copies.ready(WD)
        at[FEED][...] = mm(at[ACT][...], at[WD][...], NN)

        def second_norm(rows):
            ffn = at[FEED][rows, :] + vec(bd)
            alive = at[LIVE][rows, 0:1]
            at[STATS][8:16, :] += fold8(ffn * ffn * alive)
            unit, rate = normed(at[WIDE][rows, :] + ffn)
            result = unit * vec(g2) + vec(s2)
            at[STATS][16:24, :] += fold8(result * result * alive)
            at[N2][rows, :] = unit.astype(BF16)
            at[R2][rows, :] = jnp.broadcast_to(rate, (ROW_BLOCK, LANES))
            at[Y][rows, :] = result.astype(BF16)

        over_rows(second_norm)
        save(Y, STATS, N2, R2)
        copies.finish()


def forward(section, row, x, x_row, ids, params, kept):
    width, inner = params[9].shape[1:]
    shapes = shapes_of(width, inner)
    inputs = [(x, ANY)] + [(array, WHOLE) for array in ids]
    inputs += [(array, ANY if array.ndim == 3 else WHOLE) for array in params]
    made = call(
        partial(forward_kernel, section, row, x_row, width // HEAD_DIM),
        "forward",
        inputs,
        {} if kept is None else {i: kept[name] for i, name in enumerate(SAVED)},
        [shapes[name] for name in SAVED + (Y, STATS)],
        [shapes[name] for name in FORWARD_HELD],
        32,
    )
    return dict(zip(SAVED, made)), made[-2], made[-1]


def norm_back(grad, unit, rate, gain):
    scaled = grad * gain
    mean = jnp.mean(scaled, axis=-1, keepdims=True)
    along = jnp.mean(scaled * unit, axis=-1, keepdims=True)
    return (scaled - mean - unit * along) * rate


def add_sum(ref, place, value):
    ref[place : place + 8, 0 : value.shape[-1]] += fold8(value)


def second_norm_back(at, gain2, target, base):
    def step(rows):
        grad = at[G][rows, :].astype(F32)
        unit = at[N2][rows, :].astype(F32)
        add_sum(at[SUMS_A], GAIN2, grad * unit)
        add_sum(at[SUMS_A], SHIFT2, grad)
        d_second = norm_back(grad, unit, at[R2][rows, 0:1], vec(gain2))
        at[WIDE][rows, :] = d_second
        low = d_second.astype(BF16)
        target[pl.ds(pl.multiple_of(rows.start + base, ROW_BLOCK), ROW_BLOCK), :] = low
        add_sum(at[SUMS_A], B_DOWN, low.astype(F32))

    over_rows(step)


def up_back(at, dffn, part):
    d_act = mm(dffn, at[WD][part, :], NT)
    low = (d_act * at[GP][:, part].astype(F32)).astype(BF16)
    at[SUMS_A][B_UP : B_UP + 8, part] += fold8(low.astype(F32))
    return low


def first_norm_back(at, gain1, target, base):
    def step(rows):
        grad = at[WIDE][rows, :]
        unit = at[N1][rows, :].astype(F32)
        add_sum(at[SUMS_B], GAIN1, grad * unit)
        add_sum(at[SUMS_B], SHIFT1, grad)
        d_first = norm_back(grad, unit, at[R1][rows, 0:1], vec(gain1))
        at[WIDE][rows, :] = d_first
        low = d_first.astype(BF16)
        target[pl.ds(pl.multiple_of(rows.start + base, ROW_BLOCK), ROW_BLOCK), :] = low
        add_sum(at[SUMS_B], B_OUT, low.astype(F32))

    over_rows(step)


def context_back(at, dbr, context):
    width = dbr.shape[1]
    d_context = mm(dbr, at[WO][...], NT).astype(BF16)
    at[DCTX][...] = d_context
    product = d_context.astype(F32) * context.astype(F32)
    high = product.astype(BF16)
    rest = (product - high.astype(F32)).astype(BF16)
    of_head = (
        lax.broadcasted_iota(jnp.int32, (16, width), 1) // HEAD_DIM
        == lax.broadcasted_iota(jnp.int32, (16, width), 0)
    )
    pick = jnp.where(of_head, 1.0, 0.0).astype(BF16)
    at[DELTA][...] = mm(pick, high, NT) + mm(pick, rest, NT)


BACK_READ = (N2, R2, GP, N1, R1, CTX, LSE, KID, QID, QKV)
SHARE_READ = (ACT, HID, X)
BACK_HELD = (G,) + BACK_READ + GRADS + (WIDE, DCTX, DELTA, DX, WQKV, WO, WU, WD)


def backward_kernel(section, g_row, n_in, n_old, n_out, *refs):
    ins, outs, refs = split_refs(n_in, n_old, n_out, refs)
    g_hbm, gain1, gain2, wq, wk, wv, wo, wu, wd = ins[:9]
    given = dict(zip(BACK_READ + SHARE_READ, ins[9:]))
    with_shares = section == 0
    out = dict(zip(GRADS + (DX,), outs))
    at = dict(zip(BACK_HELD + (SHARE_READ if with_shares else ()), refs))
    width, inner = at[WU].shape
    shared = Copies(at, refs[-1])
    shared.used = 40
    if with_shares:
        for name in SHARE_READ:
            shared.load(name, given[name], now=False)

        @pl.when(lax.axis_index(LAYER) != section)
        def _():
            others = Copies(at, refs[-1])
            others.used = 50
            for name in (DFFN, DUP, DBR, DQKV):
                others.load(name, out[name])
            others.load(CTX, given[CTX])
            shared.go()
            others.ready(DFFN, DUP, DBR, DQKV, CTX)

    @pl.when(lax.axis_index(LAYER) == section)
    def _():
        copies = Copies(at, refs[-1])

        def get(*names):
            for name in names:
                copies.load(name, given[name])

        def save(*names):
            for name in names:
                copies.store(at[name], out[name])

        copies.load(G, g_hbm.at[pl.ds(g_row * SEQ, SEQ), :])
        get(N2, R2)
        for name in (SUMS_A, SUMS_B):
            at[name][...] = jnp.zeros(at[name].shape, F32)
        copies.ready(G, N2, R2)
        copies.load(WD, wd.at[0])
        get(GP)
        second_norm_back(at, gain2, at[DFFN], 0)
        save(DFFN)
        copies.ready(WD, GP)
        copies.load(WU, wu.at[0])
        get(N1, R1)
        copies.load(WO, wo.at[0])
        get(CTX)

        def up(part):
            at[DUP][:, part] = up_back(at, at[DFFN][...], part)

        over_tiles(inner, inner // 4, up)
        save(DUP, SUMS_A)
        copies.ready(WU)
        get(QKV, KID, QID, LSE)
        load_qkv(copies, (wq, wk, wv), width)
        at[WIDE][...] += mm(at[DUP][...], at[WU][...], NT)
        copies.ready(N1, R1)
        first_norm_back(at, gain1, at[DBR], 0)
        save(DBR, SUMS_B)
        copies.ready(WO, CTX)
        context_back(at, at[DBR][...], at[CTX][...])
        copies.ready(QKV, KID, QID, LSE)
        if with_shares:
            shared.go()
        over_pairs(width, lambda j: attend_pair_back(j, width, at, at[DQKV], 0))
        save(DQKV, SUMS_C)
        copies.ready(WQKV)
        at[DX][...] = (at[WIDE][...] + mm(at[DQKV][...], at[WQKV][...], NT)).astype(BF16)
        save(DX)
        copies.finish()

    if not with_shares:
        return
    down, up, rest = at[WD], at[WU], refs[-2]
    shared.ready(*SHARE_READ)

    def to_down(part):
        down[part, :] = mm(at[ACT][:, part], at[DFFN][...], TN).astype(BF16)

    over_tiles(inner, width, to_down)
    shared.store(down, outs[-3])

    def to_up(part):
        up[:, part] = mm(at[HID][...], at[DUP][:, part], TN).astype(BF16)

    over_tiles(inner, width, to_up)
    shared.store(up, outs[-2])
    rest[:, 0:width] = mm(at[CTX][...], at[DBR][...], TN).astype(BF16)

    def to_rest(i, carry):
        made = mm(at[X][...], at[DQKV][:, lanes_at(i * width - width, width)], TN)
        rest[:, lanes_at(i * width, width)] = made.astype(BF16)
        return carry

    lax.fori_loop(1, 4, to_rest, 0)
    shared.store(rest, outs[-1])
    shared.finish()


def backward(section, g, g_row, params, kept, old):
    wq, _, wk, wv, _, wo, _, gain1, _, wu, _, wd, _, gain2, _ = params
    shapes = shapes_of(*wu.shape[1:])
    inputs = [(g, ANY), (gain1, WHOLE), (gain2, WHOLE)]
    inputs += [(array, ANY) for array in (wq, wk, wv, wo, wu, wd)]
    inputs += [(kept[name], ANY) for name in BACK_READ]
    outs, held = list(GRADS + (DX,)), list(BACK_HELD)
    if section == 0:
        inputs += [(kept[name], ANY) for name in SHARE_READ]
        outs += [WD, WU, REST]
        held += SHARE_READ + (REST,)
    made = call(
        partial(backward_kernel, section, g_row),
        "backward",
        inputs,
        {} if old is None else {i: old[name] for i, name in enumerate(GRADS)},
        [shapes[name] for name in outs],
        [shapes[name] for name in held],
        56,
    )
    return dict(zip(GRADS, made)), made[len(GRADS) :]


N_TILES = 4


def gradient_shapes(rows, columns):
    count = lax.axis_size(ROWS)
    if count == 16:
        return ((8, 2, rows // count, columns), BF16), [((8, rows // count, columns), BF16)] * 2
    return ((rows, columns), BF16), [((rows, columns), BF16)]


class GradientOut:
    def __init__(self, ref, targets, sems, first_sem, by_rows):
        self.ref, self.targets, self.sems, self.first_sem = ref, targets, sems, first_sem
        self.by_rows = by_rows
        self.plain = len(targets) == 1
        if self.plain:
            self.rows, self.columns = ref.shape
        else:
            self.rows, self.columns = ref.shape[0] * 2 * ref.shape[2], ref.shape[3]
        self.tile = (self.rows if by_rows else self.columns) // N_TILES

    def moves(self, i):
        start = i * self.tile
        if self.plain:
            at = (
                (pl.ds(start, self.tile), slice(None))
                if self.by_rows
                else (slice(None), lanes_at(start, self.tile))
            )
            pairs = [(self.ref.at[at], self.targets[0].at[at])]
        else:
            block = self.ref.shape[2]
            count = self.tile // (2 * block)
            core = lax.axis_index(ROWS) % 2
            pairs = []
            for target, which in zip(self.targets, (core, 1 - core)):
                if self.by_rows:
                    rows = pl.ds(i * count, count)
                    pairs.append((self.ref.at[rows, which], target.at[rows]))
                else:
                    lanes = lanes_at(start, self.tile)
                    pairs.append((self.ref.at[:, which, :, lanes], target.at[:, :, lanes]))
        base = self.first_sem + i * len(pairs)
        return [
            pltpu.make_async_copy(source, target, self.sems.at[base + k])
            for k, (source, target) in enumerate(pairs)
        ]

    def put(self, i, value):
        value = value.astype(BF16)
        start = i * self.tile
        if self.plain and self.by_rows:
            self.ref[pl.ds(pl.multiple_of(start, 16), self.tile), :] = value
        elif self.plain:
            self.ref[:, lanes_at(start, self.tile)] = value
        else:
            split = value.reshape(-1, 2, self.ref.shape[2], value.shape[1])
            if self.by_rows:
                self.ref[pl.ds(i * split.shape[0], split.shape[0])] = split
            else:
                self.ref[:, :, :, lanes_at(start, self.tile)] = split
        for move in self.moves(i):
            move.start()

    def finish(self):
        for i in range(N_TILES):
            for move in self.moves(i):
                move.wait()


def loop_tiles(step):
    def body(i, carry):
        step(i)
        return carry

    lax.fori_loop(0, N_TILES, body, 0)


def down_kernel(n_in, n_old, n_out, *refs):
    ins, outs, refs = split_refs(n_in, n_old, n_out, refs)
    g_hbm, gain2, n2, r2, act_hbm, share = ins
    dffn_out, sums_out, wide_out = outs[:3]
    at = dict(zip((G, N2, R2, WIDE, SUMS_A, ACT, DFFN, DX), refs))
    total, sems = refs[-2:]
    copies = Copies(at, sems)
    own = Copies(at, sems)
    own.used = 10
    own.load(G, g_hbm, now=False)
    own.load(N2, n2, now=False)
    own.load(R2, r2, now=False)
    for name, target in ((DFFN, dffn_out), (SUMS_A, sums_out), (WIDE, wide_out)):
        own.store(at[name], target, now=False)
    other = Copies(at, sems)
    other.used = 20
    other.load(DFFN, dffn_out, now=False)
    is_first = lax.axis_index(LAYER) == 0

    @pl.when(is_first)
    def _():
        own.go()
        at[SUMS_A][...] = jnp.zeros(at[SUMS_A].shape, F32)
        own.ready(G, N2, R2)

    copies.load(ACT, act_hbm)
    copies.load(DX, share)

    @pl.when(is_first)
    def _():
        second_norm_back(at, gain2, at[DFFN], 0)
        for way in own.stores:
            way.start()

    @pl.when(jnp.logical_not(is_first))
    def _():
        other.go()
        other.ready(DFFN)

    copies.ready(ACT, DX)
    way_out = GradientOut(total, outs[3:], sems, 24, True)

    def step(i):
        part = lanes_at(i * way_out.tile, way_out.tile)
        made = mm(at[ACT][:, part], at[DFFN][...], TN)
        way_out.put(i, made + at[DX][part, :].astype(F32))

    loop_tiles(step)
    way_out.finish()

    @pl.when(is_first)
    def _():
        own.finish()


def up_kernel(n_in, n_old, n_out, *refs):
    ins, outs, refs = split_refs(n_in, n_old, n_out, refs)
    wd_hbm, gp_hbm, hid_hbm, dffn_hbm, share = ins
    dup_out, sums_out = outs[:2]
    at = dict(zip((WD, GP, HID, DUP, DFFN, SUMS_A, DX), refs))
    total, sems = refs[-2:]
    is_first = lax.axis_index(LAYER) == 0
    way_out = GradientOut(total, outs[2:], sems, 24, False)
    copies = Copies(at, sems)
    copies.load(HID, hid_hbm)
    own = Copies(at, sems)
    own.used = 1
    own.load(DFFN, dffn_hbm, now=False)
    own.load(SUMS_A, sums_out, now=False)
    own.store(at[SUMS_A], sums_out, now=False)
    other = Copies(at, sems)
    other.used = 4
    other.load(DUP, dup_out, now=False)

    def fetch(i):
        part = lanes_at(i * way_out.tile, way_out.tile)
        pairs = (
            (share.at[:, part], at[DX].at[:, part]),
            (wd_hbm.at[0, part, :], at[WD].at[part, :]),
            (gp_hbm.at[:, part], at[GP].at[:, part]),
        )
        return [
            pltpu.make_async_copy(source, target, sems.at[8 + 3 * i + k])
            for k, (source, target) in enumerate(pairs)
        ]

    def away(i):
        part = lanes_at(i * way_out.tile, way_out.tile)
        return pltpu.make_async_copy(at[DUP].at[:, part], dup_out.at[:, part], sems.at[20 + i])

    def fetch_start(i):
        moves = fetch(i)
        moves[0].start()

        @pl.when(is_first)
        def _():
            for move in fetch(i)[1:]:
                move.start()

    @pl.when(is_first)
    def _():
        own.go()

    @pl.when(jnp.logical_not(is_first))
    def _():
        other.go()
        other.ready(DUP)

    fetch_start(0)
    copies.ready(HID)

    @pl.when(is_first)
    def _():
        own.ready(DFFN, SUMS_A)

    def step(i):
        @pl.when(i < N_TILES - 1)
        def _():
            fetch_start(i + 1)

        part = lanes_at(i * way_out.tile, way_out.tile)

        @pl.when(is_first)
        def _():
            for move in fetch(i)[1:]:
                move.wait()
            at[DUP][:, part] = up_back(at, at[DFFN][...], part)
            away(i).start()

        fetch(i)[0].wait()
        made = mm(at[HID][...], at[DUP][:, part], TN)
        way_out.put(i, made + at[DX][:, part].astype(F32))

    loop_tiles(step)
    way_out.finish()

    @pl.when(is_first)
    def _():
        own.stores[0].start()
        for i in range(N_TILES):
            away(i).wait()
        own.finish()


def middle_kernel(n_in, n_old, n_out, *refs):
    ins, outs, refs = split_refs(n_in, n_old, n_out, refs)
    dup_hbm, wide_in, wu_hbm, gain1, n1, r1, wo_hbm, ctx_hbm = ins
    at = dict(zip((DUP, WIDE, WU, N1, R1, WO, CTX, DBR, DCTX, DELTA, SUMS_B), refs))

    @pl.when(lax.axis_index(LAYER) == 0)
    def _():
        copies = Copies(at, refs[-1])
        parts = [pl.ds(i * at[DUP].shape[1] // 2, at[DUP].shape[1] // 2) for i in range(2)]

        def get_half(i):
            copies.load(DUP, dup_hbm.at[:, parts[i]], at[DUP].at[:, parts[i]])
            copies.load(WU, wu_hbm.at[0, :, parts[i]], at[WU].at[:, parts[i]])

        get_half(0)
        copies.load(WIDE, wide_in)
        at[SUMS_B][...] = jnp.zeros(at[SUMS_B].shape, F32)
        copies.ready(DUP, WU, WIDE)
        get_half(1)
        at[WIDE][...] += mm(at[DUP][:, parts[0]], at[WU][:, parts[0]], NT)
        copies.ready(DUP, WU)
        copies.load(N1, n1)
        copies.load(R1, r1)
        copies.load(WO, wo_hbm.at[0])
        copies.load(CTX, ctx_hbm)
        at[WIDE][...] += mm(at[DUP][:, parts[1]], at[WU][:, parts[1]], NT)
        copies.ready(N1, R1)
        first_norm_back(at, gain1, at[DBR], 0)
        for name, target in ((DBR, outs[0]), (WIDE, outs[1]), (SUMS_B, outs[4])):
            copies.store(at[name], target)
        copies.ready(WO, CTX)
        context_back(at, at[DBR][...], at[CTX][...])
        copies.store(at[DCTX], outs[2])
        copies.store(at[DELTA], outs[3])
        copies.finish()


ATTEND_READ = (QKV, DCTX, KID, QID, LSE, DELTA)


def attend_kernel(n_in, n_old, n_out, *refs):
    ins, outs, refs = split_refs(n_in, n_old, n_out, refs)
    x_hbm, ctx_hbm, dbr_hbm, share = ins[len(ATTEND_READ) :]
    dqkv_out, sums_out = outs[:2]
    at = dict(zip(ATTEND_READ + (X, CTX, DBR, DX, DQKV, SUMS_C), refs))
    total, sems = refs[-2:]
    width = at[X].shape[1]
    is_first = lax.axis_index(LAYER) == 0
    copies = Copies(at, sems)
    own = Copies(at, sems)
    own.used = 6
    for name, source in zip(ATTEND_READ, ins):
        own.load(name, source, now=False)
    own.store(at[DQKV], dqkv_out, now=False)
    own.store(at[SUMS_C], sums_out, now=False)
    other = Copies(at, sems)
    other.used = 20
    other.load(DQKV, dqkv_out, now=False)

    @pl.when(is_first)
    def _():
        own.go()
        own.ready(*ATTEND_READ)

    for name, source in ((X, x_hbm), (CTX, ctx_hbm), (DBR, dbr_hbm), (DX, share)):
        copies.load(name, source)

    @pl.when(is_first)
    def _():
        over_pairs(width, lambda j: attend_pair_back(j, width, at, at[DQKV], 0))
        for way in own.stores:
            way.start()

    @pl.when(jnp.logical_not(is_first))
    def _():
        other.go()
        other.ready(DQKV)

    copies.ready(X, CTX, DBR, DX)
    way_out = GradientOut(total, outs[2:], sems, 24, False)
    way_out.put(0, mm(at[CTX][...], at[DBR][...], TN) + at[DX][:, 0:width].astype(F32))

    def step(i, carry):
        made = mm(at[X][...], at[DQKV][:, lanes_at((i - 1) * width, width)], TN)
        way_out.put(i, made + at[DX][:, lanes_at(i * width, width)].astype(F32))
        return carry

    lax.fori_loop(1, N_TILES, step, 0)
    way_out.finish()

    @pl.when(is_first)
    def _():
        own.finish()


def input_kernel(n_in, n_old, n_out, *refs):
    ins, outs, refs = split_refs(n_in, n_old, n_out, refs)
    dqkv1, wide_in, wq, wk, wv = ins
    at = dict(zip((DQKV, WIDE, WQKV, DX), refs))

    @pl.when(lax.axis_index(LAYER) == 0)
    def _():
        copies = Copies(at, refs[-1])
        copies.load(DQKV, dqkv1)
        load_qkv(copies, (wq, wk, wv), at[WIDE].shape[1])
        copies.load(WIDE, wide_in)
        copies.ready(DQKV, WQKV, WIDE)
        at[DX][...] = (at[WIDE][...] + mm(at[DQKV][...], at[WQKV][...], NT)).astype(BF16)
        copies.store(at[DX], outs[0])
        copies.finish()


def swap(array, stride):
    count = lax.axis_size(ROWS)
    return lax.ppermute(array, ROWS, [(d, d ^ stride) for d in range(count)])


def halves_kernel(ways, merged, n_in, n_old, n_out, *refs):
    ins, outs, refs = split_refs(n_in, n_old, n_out, refs)
    copies = Copies({}, refs[-1])
    jobs = []
    for side in (0, 1):
        for way, (stride, before, after) in enumerate(ways):
            left, right, total = refs[3 * len(jobs) : 3 * len(jobs) + 3]
            size = total.shape[-1]
            own = (lax.axis_index(ROWS) // stride) % 2
            which = own if side else 1 - own
            sources = ins if n_in == 2 else ins[2 * way : 2 * way + 2]
            columns = pl.ds(way * size if n_in == 2 and len(ways) == 2 else 0, size)
            for i in range(before):
                taken = pl.ds((2 * i + which) * after, after)
                for source, buffer in zip(sources, (left, right)):
                    target = buffer.at[pl.ds(i * after, after)]
                    copies.load(len(jobs), source.at[taken, :, columns], target)
            if merged:
                target = outs[side].at[:, :, pl.ds(way * size, size)]
            else:
                target = outs[2 * way + side]
            jobs.append((left, right, total, target))
    for i, (left, right, total, target) in enumerate(jobs):
        copies.ready(i)
        total[...] = (left[...].astype(F32) + right[...].astype(F32)).astype(BF16)
        copies.store(total, target)
    copies.finish()


def halves(ways, arrays, merged=False):
    block = arrays[0].shape[1:]
    columns = block[1] // 2 if len(arrays) == 2 else block[1]
    parts = [((before * after, block[0], columns), BF16) for _, before, after in ways]
    if merged:
        outs = [((1, block[0], 2 * columns), BF16)] * 2
    else:
        outs = [part for part in parts for _ in (0, 1)]
    scratch = [part for _ in (0, 1) for part in parts for _ in range(3)]
    inputs = [(array, ANY) for array in arrays]
    return call(partial(halves_kernel, ways, merged), "halves", inputs, {}, outs, scratch, 32)


class ScatterSum:
    def __init__(self, blocks):
        self.shape = blocks[0].shape[1:]
        self.blocks = blocks
        self.done = 0
        self.plain = lax.axis_size(ROWS) != 16
        self.kept = blocks[0]

    def advance(self, first=None):
        if self.plain:
            return self.blocks[0]
        if first is not None:
            self.kept = lax.optimization_barrier((self.kept, first))[0]
        self.done += 1
        if self.done == 1:
            self.kept, send = self.blocks
            self.arrived = swap(send, 1)
            return send
        before = self.arrived
        if self.done == 2:
            made = halves(((2, 4, 1), (4, 2, 2)), (self.kept, before))
            self.kept = made[1::2]
            self.arrived = (swap(made[0], 2), swap(made[2], 4))
        elif self.done == 3:
            arrays = (self.kept[0], before[0], self.kept[1], before[1])
            made = halves(((4, 2, 1), (2, 2, 1)), arrays)
            self.kept = made[1::2]
            self.arrived = (swap(made[0], 4), swap(made[2], 2))
        else:
            arrays = (self.kept[0], before[0], self.kept[1], before[1])
            send, self.kept = halves(((8, 1, 1), (8, 1, 1)), arrays, True)
            self.arrived = swap(send, 8)
        return before

    def finish(self):
        if self.plain:
            total = lax.psum_scatter(self.blocks[0], ROWS, scatter_dimension=0, tiled=True)
            return total.astype(F32)
        while self.done < 4:
            self.advance()
        return (self.kept.astype(F32) + self.arrived.astype(F32)).reshape(self.shape)


def small_sum(values, beside, after):
    if lax.axis_size(ROWS) != 16:
        return lax.psum(values, ROWS)
    for stride, first in zip((1, 2, 4, 8), (*beside, None)):
        values = values + swap(values, stride)
        if first is not None:
            values = after(values, first)
    return values


def on_device(tokens, cotangent, segment_ids, valid_mask, cluster_perm, *params):
    section = lax.axis_index(LAYER)
    is_first = section == 0
    wq, _, wk, wv, _, wo, _, gain1, _, wu, _, wd, _, gain2, _ = params
    width, inner = wu.shape[1:]
    ids = (cluster_perm, segment_ids, valid_mask)
    shapes = shapes_of(width, inner)

    def hop(array, source, target):
        return lax.ppermute(array, LAYER, [(source, target)])

    def after(array, first):
        return lax.optimization_barrier((array, first))[0]

    row0, y0, stats00 = forward(0, 0, tokens, 0, ids, params, None)
    in0 = hop(y0, 0, 1)
    row1, y1, stats01 = forward(0, 1, tokens, 1, ids, params, None)
    in1 = hop(y1, 0, 1)
    row0, out0, stats10 = forward(1, 0, in0, 0, ids, params, row0)
    grads0, (dx0,) = backward(1, cotangent, 0, params, row0, None)
    in1 = after(in1, dx0)
    g0 = hop(dx0, 1, 0)
    row1, out1, stats11 = forward(1, 1, in1, 0, ids, params, row1)
    grads1, (dx1,) = backward(1, cotangent, 1, params, row1, None)
    g0 = after(g0, dx1)
    g1 = hop(dx1, 1, 0)
    grads0, (dx0, down_share, up_share, rest_share) = backward(0, g0, 0, params, row0, grads0)
    g1 = after(g1, dx0)

    def at_hbm(*arrays):
        return [(array, ANY) for array in arrays]

    def of(*names):
        return [shapes[name] for name in names]

    total, parts = gradient_shapes(inner, width)
    made = call(
        down_kernel,
        "down_gradient",
        at_hbm(g1)
        + [(gain2, WHOLE)]
        + at_hbm(row1[N2], row1[R2], row1[ACT], down_share),
        {0: grads1[DFFN], 1: grads1[SUMS_A]},
        of(DFFN, SUMS_A, WIDE) + parts,
        of(G, N2, R2, WIDE, SUMS_A, ACT, DFFN) + of(WD) + [total],
        40,
    )
    dffn1, sums_a1, wide = made[:3]
    down_sum = ScatterSum(made[3:])
    down_sum.advance()

    total, parts = gradient_shapes(width, inner)
    made = call(
        up_kernel,
        "up_gradient",
        at_hbm(wd, row1[GP], row1[HID], dffn1, up_share),
        {0: grads1[DUP], 1: sums_a1},
        of(DUP, SUMS_A) + parts,
        of(WD, GP, HID, DUP, DFFN, SUMS_A) + of(WU) + [total],
        40,
    )
    dup1, sums_a1 = made[:2]
    down_sum.advance(dup1)
    up_sum = ScatterSum(after(tuple(made[2:]), down_sum.kept))
    up_sum.advance()
    wide = after(wide, down_sum.kept)

    made = call(
        middle_kernel,
        "middle",
        at_hbm(dup1, wide, wu) + [(gain1, WHOLE)] + at_hbm(row1[N1], row1[R1], wo, row1[CTX]),
        {0: grads1[DBR], 4: grads1[SUMS_B]},
        of(DBR, WIDE, DCTX, DELTA, SUMS_B),
        of(DUP, WIDE, WU, N1, R1, WO, CTX, DBR, DCTX, DELTA, SUMS_B),
        20,
    )
    dbr1, wide, dctx, delta, sums_b1 = made
    up_sum.advance(dctx)
    dctx = after(dctx, up_sum.kept)

    total, parts = gradient_shapes(width, 4 * width)
    made = call(
        attend_kernel,
        "attend_gradient",
        at_hbm(row1[QKV], dctx, *(row1[name] for name in (KID, QID, LSE)), delta)
        + at_hbm(row1[X], row1[CTX], dbr1, rest_share),
        {0: grads1[DQKV], 1: grads1[SUMS_C]},
        of(DQKV, SUMS_C) + parts,
        of(*ATTEND_READ) + of(X, CTX, DBR) + of(REST) + of(DQKV, SUMS_C) + [total],
        40,
    )
    dqkv1, sums_c1 = made[:2]
    down_sum.advance(dqkv1)
    up_sum.advance(down_sum.kept)
    rest_sum = ScatterSum(after(tuple(made[2:]), (down_sum.kept, up_sum.kept)))
    rest_sum.advance()
    wide = after(wide, up_sum.kept)
    made = call(
        input_kernel,
        "input_gradient",
        at_hbm(dqkv1, wide, wq, wk, wv),
        {},
        of(DX),
        of(DQKV, WIDE, WQKV, DX),
        8,
    )
    dx1 = made[0]
    came = [rest_sum.advance(dx1)]
    down_sum.advance(rest_sum.kept)
    up_sum.advance(down_sum.kept)
    came.append(rest_sum.advance(up_sum.kept))
    came.append(rest_sum.advance())

    sums_a1, sums_b1, sums_c1 = (after(array, dx1) for array in (sums_a1, sums_b1, sums_c1))
    stats10 = after(stats10, dx1)
    sum_a = (grads0[SUMS_A] + sums_a1).reshape(4, 8, inner).sum(axis=1)
    sum_b = (grads0[SUMS_B] + sums_b1).reshape(3, 8, width).sum(axis=1)
    sum_c = (grads0[SUMS_C] + sums_c1).reshape(2, 8, width).sum(axis=1)
    stats = jnp.where(is_first, stats00 + stats01, stats10 + stats11)
    stats = stats.reshape(3, 8 * width).sum(axis=1)
    count = jnp.sum(valid_mask.astype(F32))
    pieces = [sum_a[:3, :width].reshape(-1), sum_b.reshape(-1), sum_c.reshape(-1), sum_a[3]]
    base = 8 * width + inner
    spare = -(base + 4) % (8 * LANES)
    tail = jnp.concatenate([stats, jnp.broadcast_to(count, (1,)), jnp.zeros((spare,), F32)])
    small = jnp.concatenate(pieces + [tail]).reshape(-1, LANES)
    small = small_sum(small, came, after).reshape(-1)
    w_down = down_sum.finish()
    w_up = up_sum.finish()
    w_rest = rest_sum.finish()
    shares = lax.axis_size(ROWS)
    me = lax.axis_index(ROWS)

    def small_part(place, size):
        own = size // shares
        return lax.dynamic_slice_in_dim(small, place * width + me * own, own, 0)[None]

    gain2_sum, shift2_sum, down_bias, gain1_sum, shift1_sum, out_bias, query_bias, value_bias = (
        small_part(i, width) for i in range(8)
    )
    up_bias = small_part(8, inner)
    root_means = jnp.sqrt(small[base : base + 3] / (small[base + 3] * width))[None, :]

    half = width // 2
    dx0, out0, out1 = (after(array, dx1) for array in (dx0, out0, out1))
    outgoing = jnp.concatenate(
        [
            jnp.where(is_first, grad[:, half:], made[:, :half])
            for grad, made in ((dx0, out0), (dx1, out1))
        ]
    )
    arrived = lax.ppermute(outgoing, LAYER, [(0, 1), (1, 0)])
    block_own = jnp.concatenate([out0[:, half:], out1[:, half:]])
    grad_own = jnp.concatenate([dx0[:, :half], dx1[:, :half]])
    block_part = jnp.where(is_first, arrived, block_own)
    grad_part = jnp.where(is_first, grad_own, arrived)
    return (
        block_part,
        grad_part,
        w_rest[None, :, width : 2 * width],
        query_bias,
        w_rest[None, :, 2 * width : 3 * width],
        w_rest[None, :, 3 * width :],
        value_bias,
        w_rest[None, :, :width],
        out_bias,
        gain1_sum,
        shift1_sum,
        w_up[None],
        up_bias,
        w_down[None],
        down_bias,
        gain2_sum,
        shift2_sum,
        root_means,
    )


def solution(mesh):
    by_layer = P(LAYER, None)
    matrix = P(LAYER, None, None)
    share = P(LAYER, ROWS)
    matrix_share = P(LAYER, ROWS, None)
    rows = P(ROWS, None)
    vectors = {1, 4, 6, 7, 8, 10, 12, 13, 14}
    matrices = {2, 4, 5, 7, 11, 13}
    return jax.shard_map(
        on_device,
        mesh=mesh,
        in_specs=(rows, rows, rows, rows, P(LAYER, ROWS, None, None))
        + tuple(by_layer if i in vectors else matrix for i in range(15)),
        out_specs=(P(ROWS, LAYER), P(ROWS, LAYER))
        + tuple(matrix_share if i in matrices else share for i in range(2, 17))
        + (P(LAYER, None),),
        check_vma=False,
    )
```

time: 3480 us -> 355 us (0.10)
  local copies, waits for them, and re-layouts: 1730 us -> 17.1 us
  waiting for transfers between devices: 1250 us -> 93.5 us
  matrix products: 220 us -> 0 us
  Pallas kernels: 0 us -> 197 us
  other arithmetic: 168 us -> 10.2 us
  blocking collectives: 60.9 us -> 0 us
    gather x72 -> x0, local copies, waits for them, and re-layouts: 1480 us -> none  [the longest x32 645 us: arrange(): picked = jnp.take_along_axis(head_split, orders[..., None], axis=2)]
    ppermute x5 -> x27, waiting for transfers between devices: 884 us -> 93.5 us  [the longest x4 62.7 us: hop(): return lax.ppermute(array, LAYER, [(source, target)])]
    reduce_scatter x6 -> x0, waiting for transfers between devices: 364 us -> none  [the longest x1 117 us: sum_end(): lax.psum_scatter(parts[11], 'dp', scatter_dimension=0, tiled=True)]
    dot_general x48 -> x0, matrix products: 218 us -> none  [the longest x12 69.2 us: project_back(): jnp.einsum('rse,de->rsd', left, right, preferred_element_type=jnp.float32)]
    pallas_call x0 -> x21, Pallas kernels: none -> 197 us  [call(): pl.pallas_call(partial(body, n_in, len(old), len(outs)), out_shape=[jax.S...]
    another operation x93 -> x0, local copies, waits for them, and re-layouts: 95.9 us -> none
    unnamed x1 -> x0, blocking collectives: 60.9 us -> none
    unnamed x132 -> x73, local copies, waits for them, and re-layouts: 65.9 us -> 13.6 us
  transfers between devices with their start and end apart: 11 -> 27, of which waited for: 5 -> 11; matrix products, arithmetic and copies ran while one was open for 4% -> 3% of each run, Pallas kernels for 0% -> 44%
where the time goes in v3:
time: 355 us; the launch traced here: 348 us
  Pallas kernels  197 us (55%)
  waiting for transfers between devices  93.5 us (26%)
  starting transfers between devices  28.1 us (8%)
  local copies, waits for them, and re-layouts  17.1 us (5%)
  other arithmetic  10.2 us (3%)
    pallas_call x21, Pallas kernels, call(): pl.pallas_call(partial(body, n_in, len(old), len(outs)), out_shape=[jax.S...  197 us
    ppermute x4, waiting for transfers between devices, hop(): return lax.ppermute(array, LAYER, [(source, target)])  62.7 us
    ppermute x22, waiting for transfers between devices, swap(): return lax.ppermute(array, ROWS, [(d, d ^ stride) for d in range(count)])  30.8 us
    ppermute x22, starting transfers between devices, swap(): return lax.ppermute(array, ROWS, [(d, d ^ stride) for d in range(count)])  22.8 us
    unnamed x73, local copies, waits for them, and re-layouts  13.6 us
  transfers between devices with their start and end apart: 27, of which 11 were waited for; matrix products, arithmetic and copies ran while one was open for 3% of the time, Pallas kernels for 44%

profile of v3, /device:TPU:0, one launch (start us, length us, event | category | flops | bytes accessed | tf_op | source)
XLA Modules:
  0.0 348.1 jit_solution(15229008491534145659)
XLA Ops:
  2.1 25.6 %forward.4 = (bf16[512,768]{1,0:T(8,128)(2,1)}, bf16[512,2304]{1,0:T(8,128)(2,1)}, bf16[512,768]{1,0:T(8,128)(2,1)}, f32[16,512]{1,0:T(8,128)}, f32[512,768]{1,0...) custom-call(bf16[1024,768]{1,0:T(8,128)(2,1)} %refs_0_.7, ...), custom_call_target="tpu_custom_call" | custom-call | flops 1 | bytes 1 | tf_op jit(solution)/shard_map/forward/pallas_call | solution.py:141
  29.0 25.8 %forward.6 = (bf16[512,768]{1,0:T(8,128)(2,1)}, bf16[512,2304]{1,0:T(8,128)(2,1)}, bf16[512,768]{1,0:T(8,128)(2,1)}, f32[16,512]{1,0:T(8,128)}, f32[512,768]{1,0...) custom-call(bf16[1024,768]{1,0:T(8,128)(2,1)} %refs_0_.7, ...), custom_call_target="tpu_custom_call" | custom-call | flops 1 | bytes 1 | tf_op jit(solution)/shard_map/forward/pallas_call | solution.py:141
  58.5 7.3 %backward.3 = (bf16[512,768]{1,0:T(8,128)(2,1)}, bf16[512,3072]{1,0:T(8,128)(2,1)}, bf16[512,768]{1,0:T(8,128)(2,1)}, bf16[512,2304]{1,0:T(8,128)(2,1)}, f32[32,...) custom-call(bf16[1024,768]{1,0:T(8,128)(2,1)} %refs_0_.8, ...), custom_call_target="tpu_custom_call" | custom-call | flops 1 | bytes 1 | tf_op jit(solution)/shard_map/backward/pallas_call | solution.py:141
  67.1 7.0 %collective-permute-done.2.refs_0_ = bf16[512,768]{1,0:T(8,128)(2,1)S(1)} collective-permute-done((bf16[512,768]{1,0:T(8,128)(2,1)}, bf16[512,768]{1,0:T(8,128)(2,1)S(1)}, u32[]{:S(2)}, u32[]{:S(2)}) %collective-permute-start.2) | collective-permute-done | bytes 786464 | tf_op jit(solution)/shard_map/ppermute | solution.py:1030
  76.4 7.0 %backward.4 = (bf16[512,768]{1,0:T(8,128)(2,1)}, bf16[512,3072]{1,0:T(8,128)(2,1)}, bf16[512,768]{1,0:T(8,128)(2,1)}, bf16[512,2304]{1,0:T(8,128)(2,1)}, f32[32,...) custom-call(bf16[1024,768]{1,0:T(8,128)(2,1)} %refs_0_.8, ...), custom_call_target="tpu_custom_call" | custom-call | flops 1 | bytes 1 | tf_op jit(solution)/shard_map/backward/pallas_call | solution.py:141
  84.7 41.0 %collective-permute-done.1.refs_0_ = bf16[512,768]{1,0:T(8,128)(2,1)S(1)} collective-permute-done((bf16[512,768]{1,0:T(8,128)(2,1)}, bf16[512,768]{1,0:T(8,128)(2,1)S(1)}, u32[]{:S(2)}, u32[]{:S(2)}) %collective-permute-start.1) | collective-permute-done | bytes 786464 | tf_op jit(solution)/shard_map/ppermute | solution.py:1030
  126.6 42.7 %backward.5 = (bf16[512,768]{1,0:T(8,128)(2,1)}, bf16[512,3072]{1,0:T(8,128)(2,1)}, bf16[512,768]{1,0:T(8,128)(2,1)}, bf16[512,2304]{1,0:T(8,128)(2,1)}, f32[32,...) custom-call(bf16[512,768]{1,0:T(8,128)(2,1)} %copy-done.10, ...), custom_call_target="tpu_custom_call", output_to_operand_aliasing={{0}: (22, {}), {1}: (23, {}), {2}: (24, {}), {3}: (25, {}),... | custom-call | flops 1 | bytes 1 | tf_op jit(solution)/shard_map/backward/pallas_call | solution.py:141
  169.3 14.7 %collective-permute-done.3.refs_0_ = bf16[512,768]{1,0:T(8,128)(2,1)S(1)} collective-permute-done((bf16[512,768]{1,0:T(8,128)(2,1)}, bf16[512,768]{1,0:T(8,128)(2,1)S(1)}, u32[]{:S(2)}, u32[]{:S(2)}) %collective-permute-start.3) | collective-permute-done | bytes 786464 | tf_op jit(solution)/shard_map/ppermute | solution.py:1030
  184.9 11.3 %down_gradient.1 = (bf16[512,768]{1,0:T(8,128)(2,1)}, f32[32,3072]{1,0:T(8,128)}, f32[512,768]{1,0:T(8,128)}, bf16[8,192,768]{2,1,0:T(8,128)(2,1)}, bf16[8,192,768]{2,1,0:T(8,128)(2,1)}) custom-call(bf16[512,768]{1,0:T(8,128)(2,1)} %copy-done.6, bf16[1,768]{1,0:T(2,128)(2,1)} %refs_1_.11, ...), custom_call_target="tpu_custom_call", output_to_operand_aliasing={{0}: (6, {}), {1}: (7, {})} | custom-call | flops 1 | bytes 1 | tf_op jit(solution)/shard_map/down_gradient/pallas_call | solution.py:141
  196.3 12.3 %up_gradient.1 = (bf16[512,3072]{1,0:T(8,128)(2,1)}, f32[32,3072]{1,0:T(8,128)}, bf16[8,48,3072]{2,1,0:T(8,128)(2,1)}, bf16[8,48,3072]{2,1,0:T(8,128)(2,1)}) custom-call(bf16[1,3072,768]{2,1,0:T(8,128)(2,1)} %refs_0_.9, bf16[512,3072]{1,0:T(8,128)(2,1)} %get-tuple-element.224.refs_11_.refs_1_, ...), custom_call_target="tpu_custom_call", output_to_operand_aliasing={{0}: (5, {}), {1}: (6, {})} | custom-call | flops 1 | bytes 1 | tf_op jit(solution)/shard_map/up_gradient/pallas_call | solution.py:141
  210.1 3.8 %halves.9 = (bf16[4,192,384]{2,1,0:T(8,128)(2,1)}, bf16[4,192,384]{2,1,0:T(8,128)(2,1)}, bf16[4,192,384]{2,1,0:T(8,128)(2,1)}, bf16[4,192,384]{2,1,0:T(8,128)(2,1)}) custom-call(bf16[8,192,768]{2,1,0:T(8,128)(2,1)} %get-tuple-element.258.refs_0_, bf16[8,192,768]{2,1,0:T(8,128)(2,1)} %copy-done.3), custom_call_target="tpu_custom_call" | custom-call | flops 1 | bytes 1 | tf_op jit(solution)/shard_map/halves/pallas_call | solution.py:141
  217.8 11.2 %middle.1 = (bf16[512,768]{1,0:T(8,128)(2,1)}, f32[512,768]{1,0:T(8,128)}, bf16[512,768]{1,0:T(8,128)(2,1)}, f32[16,512]{1,0:T(8,128)}, f32[24,768]{1,0:T(8,128)}) custom-call(bf16[512,3072]{1,0:T(8,128)(2,1)} %get-tuple-element.255.refs_0_, f32[512,768]{1,0:T(8,128)} %get-tuple-element.262.refs_1_, ...), custom_call_target="tpu_custom_call", output_to_operand_aliasing={{0}: (8, {}), {4}: (9, {})} | custom-call | flops 1 | bytes 1 | tf_op jit(solution)/shard_map/middle/pallas_call | solution.py:141
  230.4 3.7 %halves.10 = (bf16[4,48,1536]{2,1,0:T(8,128)(2,1)}, bf16[4,48,1536]{2,1,0:T(8,128)(2,1)}, bf16[4,48,1536]{2,1,0:T(8,128)(2,1)}, bf16[4,48,1536]{2,1,0:T(8,128)(2,1)}) custom-call(bf16[8,48,3072]{2,1,0:T(8,128)(2,1)} %get-tuple-element.269.refs_0_, bf16[8,48,3072]{2,1,0:T(8,128)(2,1)} %copy-done.2), custom_call_target="tpu_custom_call" | custom-call | flops 1 | bytes 1 | tf_op jit(solution)/shard_map/halves/pallas_call | solution.py:141
  235.0 18.1 %attend_gradient.1 = (bf16[512,2304]{1,0:T(8,128)(2,1)}, f32[16,768]{1,0:T(8,128)}, bf16[8,48,3072]{2,1,0:T(8,128)(2,1)}, bf16[8,48,3072]{2,1,0:T(8,128)(2,1)}) custom-call(bf16[512,2304]{1,0:T(8,128)(2,1)} %get-tuple-element.231.refs_18_.refs_0_, bf16[512,768]{1,0:T(8,128)(2,1)} %get-tuple-element.273.refs_1_, ...), custom_call_target="tpu_custom_call", output_to_operand_aliasing={{0}: (10, {}), {1}: (11, {})} | custom-call | flops 1 | bytes 1 | tf_op jit(solution)/shard_map/attend_gradient/pallas_call | solution.py:141
  254.7 2.8 halves.11
  259.1 2.8 halves.12
  262.0 6.3 %input_gradient.1 = bf16[512,768]{1,0:T(8,128)(2,1)} custom-call(bf16[512,2304]{1,0:T(8,128)(2,1)} %get-tuple-element.280.refs_0_, f32[512,768]{1,0:T(8,128)} %get-tuple-element.294.refs_1_, bf16[1,768,768]{2,1,0:T(8,128)(2,1)} %refs_2_.17, bf16[1,768,768]{2,1,0:T(8,128)(2,1)} %refs_3_.17, bf16[1,768,768]{2,1,0:T(8,128)(2,1)} %refs_4_.15), custom_call_target="tpu_custom_call" | custom-call | flops 1 | bytes 1 | tf_op jit(solution)/shard_map/input_gradient/pallas_call | solution.py:141
  268.4 2.2 fusion.2
  272.2 1.8 collective-permute-start.12
  277.6 3.8 %halves.13 = (bf16[4,48,1536]{2,1,0:T(8,128)(2,1)}, bf16[4,48,1536]{2,1,0:T(8,128)(2,1)}, bf16[4,48,1536]{2,1,0:T(8,128)(2,1)}, bf16[4,48,1536]{2,1,0:T(8,128)(2,1)}) custom-call(bf16[8,48,3072]{2,1,0:T(8,128)(2,1)} %get-tuple-element.303.refs_0_, bf16[8,48,3072]{2,1,0:T(8,128)(2,1)} %copy-done.1), custom_call_target="tpu_custom_call" | custom-call | flops 1 | bytes 1 | tf_op jit(solution)/shard_map/halves/pallas_call | solution.py:141
  288.7 2.3 halves.14
  291.0 2.4 halves.15
  293.4 2.9 collective-permute-start.25
  297.8 2.7 maximum_select_fusion.1
  300.9 2.3 collective-permute-done.22
  303.2 2.8 collective-permute-done.17.refs_3_
  306.9 2.8 halves.16
  312.5 4.7 %collective-permute-done.25 = bf16[1,48,3072]{2,1,0:T(8,128)(2,1)S(1)} collective-permute-done((bf16[1,48,3072]{2,1,0:T(8,128)(2,1)}, bf16[1,48,3072]{2,1,0:T(8,128)(2,1)S(1)}, u32[]{:S(2)}, u32[]{:S(2)}) %collective-permute-start.25) | collective-permute-done | bytes 294944 | tf_op jit(solution)/shard_map/ppermute | solution.py:923
  318.1 7.8 %collective-permute-done.18.refs_1_ = bf16[2,48,1536]{2,1,0:T(8,128)(2,1)S(1)} collective-permute-done((bf16[2,48,1536]{2,1,0:T(8,128)(2,1)}, bf16[2,48,1536]{2,1,0:T(8,128)(2,1)S(1)}, u32[]{:S(2)}, u32[]{:S(2)}) %collective-permute-start.18) | collective-permute-done | bytes 294944 | tf_op jit(solution)/shard_map/ppermute | solution.py:923
  325.9 2.0 collective-permute-start.24
  328.8 2.3 halves.17
  335.2 10.8 %collective-permute-done.20 = bf16[1,48,3072]{2,1,0:T(8,128)(2,1)S(1)} collective-permute-done((bf16[1,48,3072]{2,1,0:T(8,128)(2,1)}, bf16[1,48,3072]{2,1,0:T(8,128)(2,1)S(1)}, u32[]{:S(2)}, u32[]{:S(2)}) %collective-permute-start.20) | collective-permute-done | bytes 294944 | tf_op jit(solution)/shard_map/ppermute | solution.py:923
  (145 shorter events, 49.0 us)
Async XLA Ops:
  27.6 28.6 %collective-permute-start = (bf16[512,768]{1,0:T(8,128)(2,1)}, bf16[512,768]{1,0:T(8,128)(2,1)S(1)}, u32[]{:S(2)}, u32[]{:S(2)}) collective-permute-start(bf16[512,768]{1,0:T(8,128)(2,1)} %get-tuple-element.182), channel_id=1, source_target_pairs={{0,16},{1,17},{2,18},{3,19},{4,20},{5,21},{6,22},{7,23},{8,24},{9,... | collective-permute-start | bytes 2359304 | tf_op jit(solution)/shard_map/ppermute | solution.py:1030
  54.8 19.3 %collective-permute-start.2 = (bf16[512,768]{1,0:T(8,128)(2,1)}, bf16[512,768]{1,0:T(8,128)(2,1)S(1)}, u32[]{:S(2)}, u32[]{:S(2)}) collective-permute-start(bf16[512,768]{1,0:T(8,128)(2,1)} %get-tuple-element.207), channel_id=1, source_target_pairs={{0,16},{1,17},{2,18},{3,19},{4,20},{5,21},{6,22},{7,23},{8,24},{9,... | collective-permute-start | bytes 2359304 | tf_op jit(solution)/shard_map/ppermute | solution.py:1030
  65.8 59.9 %collective-permute-start.1 = (bf16[512,768]{1,0:T(8,128)(2,1)}, bf16[512,768]{1,0:T(8,128)(2,1)S(1)}, u32[]{:S(2)}, u32[]{:S(2)}) collective-permute-start(bf16[512,768]{1,0:T(8,128)(2,1)} %get-tuple-element.206), channel_id=1, source_target_pairs={{16,0},{17,1},{18,2},{19,3},{20,4},{21,5},{22,6},{23,7},{24,8},{25... | collective-permute-start | bytes 2359304 | tf_op jit(solution)/shard_map/ppermute | solution.py:1030
  83.4 100.6 %collective-permute-start.3 = (bf16[512,768]{1,0:T(8,128)(2,1)}, bf16[512,768]{1,0:T(8,128)(2,1)S(1)}, u32[]{:S(2)}, u32[]{:S(2)}) collective-permute-start(bf16[512,768]{1,0:T(8,128)(2,1)} %get-tuple-element.232), channel_id=1, source_target_pairs={{16,0},{17,1},{18,2},{19,3},{20,4},{21,5},{22,6},{23,7},{24,8},{25... | collective-permute-start | bytes 2359304 | tf_op jit(solution)/shard_map/ppermute | solution.py:1030
  196.2 12.4 %collective-permute-start.4 = (bf16[8,192,768]{2,1,0:T(8,128)(2,1)}, bf16[8,192,768]{2,1,0:T(8,128)(2,1)S(1)}, u32[]{:S(2)}, u32[]{:S(2)}) collective-permute-start(bf16[8,192,768]{2,1,0:T(8,128)(2,1)} %get-tuple-element.259), channel_id=1, source_target_pairs={{0,1},{1,0},{2,3},{3,2},{4,5},{5,4},{6,7},{7,6},{8,9},{9,8},{10,11... | collective-permute-start | bytes 7077896 | tf_op jit(solution)/shard_map/ppermute | solution.py:923
  213.9 15.1 %collective-permute-start.5 = (bf16[8,48,3072]{2,1,0:T(8,128)(2,1)S(1)}, bf16[8,48,3072]{2,1,0:T(8,128)(2,1)S(1)}, u32[]{:S(2)}, u32[]{:S(2)}) collective-permute-start(bf16[8,48,3072]{2,1,0:T(8,128)(2,1)S(1)} %copy-done.34), channel_id=1, source_target_pairs={{0,1},{1,0},{2,3},{3,2},{4,5},{5,4},{6,7},{7,6},{8,9},{9,8},{10,11... | collective-permute-start | bytes 7077896 | tf_op jit(solution)/shard_map/ppermute | solution.py:923
  214.5 38.6 %collective-permute-start.6 = (bf16[4,192,384]{2,1,0:T(8,128)(2,1)}, bf16[4,192,384]{2,1,0:T(8,128)(2,1)S(1)}, u32[]{:S(2)}, u32[]{:S(2)}) collective-permute-start(bf16[4,192,384]{2,1,0:T(8,128)(2,1)} %get-tuple-element.283), channel_id=1, source_target_pairs={{0,2},{1,3},{2,0},{3,1},{4,6},{5,7},{6,4},{7,5},{8,10},{9,11},{10,... | collective-permute-start | bytes 1769480 | tf_op jit(solution)/shard_map/ppermute | solution.py:923
  216.2 36.9 %collective-permute-start.7 = (bf16[4,192,384]{2,1,0:T(8,128)(2,1)}, bf16[4,192,384]{2,1,0:T(8,128)(2,1)S(1)}, u32[]{:S(2)}, u32[]{:S(2)}) collective-permute-start(bf16[4,192,384]{2,1,0:T(8,128)(2,1)} %get-tuple-element.285), channel_id=1, source_target_pairs={{0,4},{1,5},{2,6},{3,7},{4,0},{5,1},{6,2},{7,3},{8,12},{9,13},{10,... | collective-permute-start | bytes 1769480 | tf_op jit(solution)/shard_map/ppermute | solution.py:923
  234.2 23.3 %collective-permute-start.8 = (bf16[4,48,1536]{2,1,0:T(8,128)(2,1)}, bf16[4,48,1536]{2,1,0:T(8,128)(2,1)S(1)}, u32[]{:S(2)}, u32[]{:S(2)}) collective-permute-start(bf16[4,48,1536]{2,1,0:T(8,128)(2,1)} %get-tuple-element.289), channel_id=1, source_target_pairs={{0,2},{1,3},{2,0},{3,1},{4,6},{5,7},{6,4},{7,5},{8,10},{9,11},{10,... | collective-permute-start | bytes 1769480 | tf_op jit(solution)/shard_map/ppermute | solution.py:923
  234.7 22.8 %collective-permute-start.9 = (bf16[4,48,1536]{2,1,0:T(8,128)(2,1)}, bf16[4,48,1536]{2,1,0:T(8,128)(2,1)S(1)}, u32[]{:S(2)}, u32[]{:S(2)}) collective-permute-start(bf16[4,48,1536]{2,1,0:T(8,128)(2,1)} %get-tuple-element.291), channel_id=1, source_target_pairs={{0,4},{1,5},{2,6},{3,7},{4,0},{5,1},{6,2},{7,3},{8,12},{9,13},{10,... | collective-permute-start | bytes 1769480 | tf_op jit(solution)/shard_map/ppermute | solution.py:923
  261.9 14.3 %collective-permute-start.11 = (bf16[8,48,3072]{2,1,0:T(8,128)(2,1)}, bf16[8,48,3072]{2,1,0:T(8,128)(2,1)S(1)}, u32[]{:S(2)}, u32[]{:S(2)}) collective-permute-start(bf16[8,48,3072]{2,1,0:T(8,128)(2,1)} %get-tuple-element.304), channel_id=1, source_target_pairs={{0,1},{1,0},{2,3},{3,2},{4,5},{5,4},{6,7},{7,6},{8,9},{9,8},{10,11... | collective-permute-start | bytes 7077896 | tf_op jit(solution)/shard_map/ppermute | solution.py:923
  271.6 26.2 %collective-permute-start.10 = (bf16[1024,384]{1,0:T(8,128)(2,1)}, bf16[1024,384]{1,0:T(8,128)(2,1)}, u32[]{:S(2)}, u32[]{:S(2)}) collective-permute-start(bf16[1024,384]{1,0:T(8,128)(2,1)} %pad_maximum_fusion), channel_id=1, source_target_pairs={{0,16},{16,0},{1,17},{17,1},{2,18},{18,2},{3,19},{19,3},{4,20},{20... | collective-permute-start | bytes 2359304 | tf_op jit(solution)/shard_map/ppermute | solution.py:1172
  272.2 10.0 %collective-permute-start.12 = (bf16[2,192,384]{2,1,0:T(8,128)(2,1)}, bf16[2,192,384]{2,1,0:T(8,128)(2,1)S(1)}, u32[]{:S(2)}, u32[]{:S(2)}) collective-permute-start(bf16[2,192,384]{2,1,0:T(8,128)(2,1)} %get-tuple-element.308), channel_id=1, source_target_pairs={{0,4},{1,5},{2,6},{3,7},{4,0},{5,1},{6,2},{7,3},{8,12},{9,13},{10,... | collective-permute-start | bytes 884744 | tf_op jit(solution)/shard_map/ppermute | solution.py:923
  274.0 10.1 %collective-permute-start.13 = (bf16[2,192,384]{2,1,0:T(8,128)(2,1)}, bf16[2,192,384]{2,1,0:T(8,128)(2,1)S(1)}, u32[]{:S(2)}, u32[]{:S(2)}) collective-permute-start(bf16[2,192,384]{2,1,0:T(8,128)(2,1)} %get-tuple-element.310), channel_id=1, source_target_pairs={{0,2},{1,3},{2,0},{3,1},{4,6},{5,7},{6,4},{7,5},{8,10},{9,11},{10,... | collective-permute-start | bytes 884744 | tf_op jit(solution)/shard_map/ppermute | solution.py:923
  275.5 13.1 %collective-permute-start.14 = (bf16[2,48,1536]{2,1,0:T(8,128)(2,1)}, bf16[2,48,1536]{2,1,0:T(8,128)(2,1)}, u32[]{:S(2)}, u32[]{:S(2)}) collective-permute-start(bf16[2,48,1536]{2,1,0:T(8,128)(2,1)} %get-tuple-element.313), channel_id=1, source_target_pairs={{0,4},{1,5},{2,6},{3,7},{4,0},{5,1},{6,2},{7,3},{8,12},{9,13},{10,... | collective-permute-start | bytes 884744 | tf_op jit(solution)/shard_map/ppermute | solution.py:923
  276.2 14.8 %collective-permute-start.15 = (bf16[2,48,1536]{2,1,0:T(8,128)(2,1)}, bf16[2,48,1536]{2,1,0:T(8,128)(2,1)}, u32[]{:S(2)}, u32[]{:S(2)}) collective-permute-start(bf16[2,48,1536]{2,1,0:T(8,128)(2,1)} %get-tuple-element.315), channel_id=1, source_target_pairs={{0,2},{1,3},{2,0},{3,1},{4,6},{5,7},{6,4},{7,5},{8,10},{9,11},{10,... | collective-permute-start | bytes 884744 | tf_op jit(solution)/shard_map/ppermute | solution.py:923
  277.6 8.7 %copy-start.28 = (f32[16,768]{1,0:T(8,128)S(1)}, f32[16,768]{1,0:T(8,128)}, u32[]{:S(2)}) copy-start(f32[16,768]{1,0:T(8,128)} %get-tuple-element.335) | copy-start | bytes 147460
  281.4 16.5 %copy-start.5 = (bf16[512,384]{1,0:T(8,128)(2,1)S(1)}, bf16[512,384]{1,0:T(8,128)(2,1)}, u32[]{:S(2)}) copy-start(bf16[512,384]{1,0:T(8,128)(2,1)} %get-tuple-element.368) | copy-start | bytes 1179652
  282.2 20.9 %collective-permute-start.16 = (bf16[4,48,1536]{2,1,0:T(8,128)(2,1)}, bf16[4,48,1536]{2,1,0:T(8,128)(2,1)S(1)}, u32[]{:S(2)}, u32[]{:S(2)}) collective-permute-start(bf16[4,48,1536]{2,1,0:T(8,128)(2,1)} %get-tuple-element.318), channel_id=1, source_target_pairs={{0,2},{1,3},{2,0},{3,1},{4,6},{5,7},{6,4},{7,5},{8,10},{9,11},{10,... | collective-permute-start | bytes 1769480 | tf_op jit(solution)/shard_map/ppermute | solution.py:923
  284.8 21.2 %collective-permute-start.17 = (bf16[4,48,1536]{2,1,0:T(8,128)(2,1)}, bf16[4,48,1536]{2,1,0:T(8,128)(2,1)S(1)}, u32[]{:S(2)}, u32[]{:S(2)}) collective-permute-start(bf16[4,48,1536]{2,1,0:T(8,128)(2,1)} %get-tuple-element.320), channel_id=1, source_target_pairs={{0,4},{1,5},{2,6},{3,7},{4,0},{5,1},{6,2},{7,3},{8,12},{9,13},{10,... | collective-permute-start | bytes 1769480 | tf_op jit(solution)/shard_map/ppermute | solution.py:923
  288.7 7.6 %collective-permute-start.21 = (f32[80,128]{1,0:T(8,128)S(1)}, f32[80,128]{1,0:T(8,128)S(1)}, u32[]{:S(2)}, u32[]{:S(2)}) collective-permute-start(f32[80,128]{1,0:T(8,128)S(1)} %bitcast.42), channel_id=1, source_target_pairs={{0,1},{1,0},{2,3},{3,2},{4,5},{5,4},{6,7},{7,6},{8,9},{9,8},{10,11... | collective-permute-start | bytes 122888 | tf_op jit(solution)/shard_map/ppermute | solution.py:923
  291.0 9.5 %copy-start.35 = (bf16[1,192,768]{2,1,0:T(8,128)(2,1)S(1)}, bf16[1,192,768]{2,1,0:T(8,128)(2,1)}, u32[]{:S(2)}) copy-start(bf16[1,192,768]{2,1,0:T(8,128)(2,1)} %get-tuple-element.345) | copy-start | bytes 884740
  293.4 23.8 %collective-permute-start.25 = (bf16[1,48,3072]{2,1,0:T(8,128)(2,1)}, bf16[1,48,3072]{2,1,0:T(8,128)(2,1)S(1)}, u32[]{:S(2)}, u32[]{:S(2)}) collective-permute-start(bf16[1,48,3072]{2,1,0:T(8,128)(2,1)} %get-tuple-element.344), channel_id=1, source_target_pairs={{0,8},{1,9},{2,10},{3,11},{4,12},{5,13},{6,14},{7,15},{8,0},{9,1},... | collective-permute-start | bytes 884744 | tf_op jit(solution)/shard_map/ppermute | solution.py:923
  296.3 6.9 %collective-permute-start.22 = (f32[80,128]{1,0:T(8,128)S(1)}, f32[80,128]{1,0:T(8,128)S(1)}, u32[]{:S(2)}, u32[]{:S(2)}) collective-permute-start(f32[80,128]{1,0:T(8,128)S(1)} %bitcast_add_fusion), channel_id=1, source_target_pairs={{0,2},{1,3},{2,0},{3,1},{4,6},{5,7},{6,4},{7,5},{8,10},{9,11},{10,... | collective-permute-start | bytes 122888 | tf_op jit(solution)/shard_map/ppermute | solution.py:923
  297.8 19.4 %copy-start.24 = (bf16[1,48,3072]{2,1,0:T(8,128)(2,1)S(1)}, bf16[1,48,3072]{2,1,0:T(8,128)(2,1)}, u32[]{:S(2)}) copy-start(bf16[1,48,3072]{2,1,0:T(8,128)(2,1)} %get-tuple-element.316) | copy-start | bytes 884740
  300.5 27.4 %copy-start.23 = (bf16[1,192,768]{2,1,0:T(8,128)(2,1)S(1)}, bf16[1,192,768]{2,1,0:T(8,128)(2,1)}, u32[]{:S(2)}) copy-start(bf16[1,192,768]{2,1,0:T(8,128)(2,1)} %get-tuple-element.311) | copy-start | bytes 884740
  300.5 27.4 %collective-permute-start.26 = (bf16[1,192,768]{2,1,0:T(8,128)(2,1)S(1)}, bf16[1,192,768]{2,1,0:T(8,128)(2,1)S(1)}, u32[]{:S(2)}, u32[]{:S(2)}) collective-permute-start(bf16[1,192,768]{2,1,0:T(8,128)(2,1)S(1)} %copy-done.35), channel_id=1, source_target_pairs={{0,8},{1,9},{2,10},{3,11},{4,12},{5,13},{6,14},{7,15},{8,0},{9,1},... | collective-permute-start | bytes 884744 | tf_op jit(solution)/shard_map/ppermute | solution.py:923
  306.0 12.1 %collective-permute-start.23 = (f32[80,128]{1,0:T(8,128)S(1)}, f32[80,128]{1,0:T(8,128)S(1)}, u32[]{:S(2)}, u32[]{:S(2)}) collective-permute-start(f32[80,128]{1,0:T(8,128)S(1)} %add.86), channel_id=1, source_target_pairs={{0,4},{1,5},{2,6},{3,7},{4,0},{5,1},{6,2},{7,3},{8,12},{9,13},{10,... | collective-permute-start | bytes 122888 | tf_op jit(solution)/shard_map/ppermute | solution.py:923
  309.7 16.2 %collective-permute-start.18 = (bf16[2,48,1536]{2,1,0:T(8,128)(2,1)}, bf16[2,48,1536]{2,1,0:T(8,128)(2,1)S(1)}, u32[]{:S(2)}, u32[]{:S(2)}) collective-permute-start(bf16[2,48,1536]{2,1,0:T(8,128)(2,1)} %get-tuple-element.322), channel_id=1, source_target_pairs={{0,4},{1,5},{2,6},{3,7},{4,0},{5,1},{6,2},{7,3},{8,12},{9,13},{10,... | collective-permute-start | bytes 884744 | tf_op jit(solution)/shard_map/ppermute | solution.py:923
  310.9 15.0 %collective-permute-start.19 = (bf16[2,48,1536]{2,1,0:T(8,128)(2,1)}, bf16[2,48,1536]{2,1,0:T(8,128)(2,1)S(1)}, u32[]{:S(2)}, u32[]{:S(2)}) collective-permute-start(bf16[2,48,1536]{2,1,0:T(8,128)(2,1)} %get-tuple-element.324), channel_id=1, source_target_pairs={{0,2},{1,3},{2,0},{3,1},{4,6},{5,7},{6,4},{7,5},{8,10},{9,11},{10,... | collective-permute-start | bytes 884744 | tf_op jit(solution)/shard_map/ppermute | solution.py:923
  325.9 6.3 %collective-permute-start.24 = (f32[80,128]{1,0:T(8,128)S(1)}, f32[80,128]{1,0:T(8,128)S(1)}, u32[]{:S(2)}, u32[]{:S(2)}) collective-permute-start(f32[80,128]{1,0:T(8,128)S(1)} %add.87), channel_id=1, source_target_pairs={{0,8},{1,9},{2,10},{3,11},{4,12},{5,13},{6,14},{7,15},{8,0},{9,1},... | collective-permute-start | bytes 122888 | tf_op jit(solution)/shard_map/ppermute | solution.py:923
  331.2 14.9 %collective-permute-start.20 = (bf16[1,48,3072]{2,1,0:T(8,128)(2,1)}, bf16[1,48,3072]{2,1,0:T(8,128)(2,1)S(1)}, u32[]{:S(2)}, u32[]{:S(2)}) collective-permute-start(bf16[1,48,3072]{2,1,0:T(8,128)(2,1)} %get-tuple-element.326), channel_id=1, source_target_pairs={{0,8},{1,9},{2,10},{3,11},{4,12},{5,13},{6,14},{7,15},{8,0},{9,1},... | collective-permute-start | bytes 884744 | tf_op jit(solution)/shard_map/ppermute | solution.py:923
  (31 other events, 121.6 us)

commit v4 on v3

--- a/solution.py
+++ b/solution.py
@@ -284,13 +284,90 @@
 FORWARD_HELD = SAVED + (WQKV, WO, WU, WD, WIDE, FEED, Y, STATS, LIVE, BIAS)
 
 
-def forward_kernel(section, row, x_row, heads, n_in, n_old, n_out, *refs):
+def run_forward(at, copies, save, row, source, ids, params, later=None):
+    perm_ref, seg_ref, valid_ref = ids
+    wq, bq, wk, wv, bv, wo, bo, g1, s1, wu, bu, wd, bd, g2, s2 = params
+    width, inner = at[WU].shape
+    heads = width // HEAD_DIM
+    copies.load(X, source)
+    first = copies.used
+    load_qkv(copies, (wq, wk, wv), width)
+    live = token_ids(row, heads, perm_ref, seg_ref, valid_ref, at[KID], at[QID])
+    at[LIVE][...] = jnp.broadcast_to(live, (SEQ, LANES))
+    at[LSE][...] = jnp.zeros((16, SEQ), F32)
+    at[STATS][...] = jnp.zeros((24, width), F32)
+    at[BIAS][0:1, :] = vec(bq)
+    at[BIAS][1:2, :] = jnp.zeros((1, width), F32)
+    at[BIAS][2:3, :] = vec(bv)
+    copies.ready(X)
+
+    def to_qkv(i, carry):
+        part = pl.ds(pl.multiple_of(i * width, LANES), width)
+        weight = at[WQKV].at[:, part]
+        pltpu.make_async_copy(weight, weight, copies.sems.at[first + i]).wait()
+        made = mm(at[X][...], at[WQKV][:, part], NN) + at[BIAS][pl.ds(i, 1), :]
+        at[QKV][:, part] = made.astype(BF16)
+        return carry
+
+    lax.fori_loop(0, 3, to_qkv, 0)
+    copies.loads.pop(WQKV)
+    copies.load(WO, wo.at[0])
+    copies.load(WU, wu.at[0])
+    copies.load(WD, wd.at[0])
+    if later is not None:
+        later()
+    save(KID, QID, X, QKV)
+    over_pairs(width, lambda j: attend_pair(j, width, at))
+    save(LSE, CTX)
+    copies.ready(WO)
+    at[WIDE][...] = mm(at[CTX][...], at[WO][...], NN)
+
+    def first_norm(rows):
+        branch = at[WIDE][rows, :] + vec(bo)
+        alive = at[LIVE][rows, 0:1]
+        at[STATS][0:8, :] += fold8(branch * branch * alive)
+        unit, rate = normed(at[X][rows, :].astype(F32) + branch)
+        hidden = unit * vec(g1) + vec(s1)
+        at[N1][rows, :] = unit.astype(BF16)
+        at[R1][rows, :] = jnp.broadcast_to(rate, (ROW_BLOCK, LANES))
+        at[HID][rows, :] = hidden.astype(BF16)
+        at[WIDE][rows, :] = hidden
+
+    over_rows(first_norm)
+    save(N1, R1, HID)
+    copies.ready(WU)
+
+    def up(part):
+        upper = mm(at[HID][...], at[WU][:, part], NN) + bu[0:1, part].astype(F32)
+        half = 0.5 + 0.5 * lax.erf(upper * 0.5**0.5)
+        bell = jnp.exp2(upper * upper * (-0.5 * LOG2E)) * 0.3989422804014327
+        at[ACT][:, part] = (upper * half).astype(BF16)
+        at[GP][:, part] = (half + upper * bell).astype(BF16)
+
+    over_tiles(inner, inner // 4, up)
+    save(ACT, GP)
+    copies.ready(WD)
+    at[FEED][...] = mm(at[ACT][...], at[WD][...], NN)
+
+    def second_norm(rows):
+        ffn = at[FEED][rows, :] + vec(bd)
+        alive = at[LIVE][rows, 0:1]
+        at[STATS][8:16, :] += fold8(ffn * ffn * alive)
+        unit, rate = normed(at[WIDE][rows, :] + ffn)
+        result = unit * vec(g2) + vec(s2)
+        at[STATS][16:24, :] += fold8(result * result * alive)
+        at[N2][rows, :] = unit.astype(BF16)
+        at[R2][rows, :] = jnp.broadcast_to(rate, (ROW_BLOCK, LANES))
+        at[Y][rows, :] = result.astype(BF16)
+
+    over_rows(second_norm)
+    save(Y, STATS, N2, R2)
+
+
+def forward_kernel(section, row, x_row, n_in, n_old, n_out, *refs):
     ins, outs, refs = split_refs(n_in, n_old, n_out, refs)
-    x_hbm, perm_ref, seg_ref, valid_ref = ins[:4]
-    wq, bq, wk, wv, bv, wo, bo, g1, s1, wu, bu, wd, bd, g2, s2 = ins[4:]
     out = dict(zip(SAVED + (Y, STATS), outs))
     at = dict(zip(FORWARD_HELD, refs))
-    width, inner = at[WU].shape
 
     @pl.when(lax.axis_index(LAYER) == section)
     def _():
@@ -300,76 +377,8 @@
             for name in names:
                 copies.store(at[name], out[name])
 
-        copies.load(X, x_hbm.at[pl.ds(x_row * SEQ, SEQ), :])
-        first = copies.used
-        load_qkv(copies, (wq, wk, wv), width)
-        live = token_ids(row, heads, perm_ref, seg_ref, valid_ref, at[KID], at[QID])
-        at[LIVE][...] = jnp.broadcast_to(live, (SEQ, LANES))
-        at[LSE][...] = jnp.zeros((16, SEQ), F32)
-        at[STATS][...] = jnp.zeros((24, width), F32)
-        at[BIAS][0:1, :] = vec(bq)
-        at[BIAS][1:2, :] = jnp.zeros((1, width), F32)
-        at[BIAS][2:3, :] = vec(bv)
-        copies.ready(X)
-
-        def to_qkv(i, carry):
-            part = pl.ds(pl.multiple_of(i * width, LANES), width)
-            weight = at[WQKV].at[:, part]
-            pltpu.make_async_copy(weight, weight, copies.sems.at[first + i]).wait()
-            made = mm(at[X][...], at[WQKV][:, part], NN) + at[BIAS][pl.ds(i, 1), :]
-            at[QKV][:, part] = made.astype(BF16)
-            return carry
-
-        lax.fori_loop(0, 3, to_qkv, 0)
-        copies.load(WO, wo.at[0])
-        copies.load(WU, wu.at[0])
-        copies.load(WD, wd.at[0])
-        save(KID, QID, X, QKV)
-        over_pairs(width, lambda j: attend_pair(j, width, at))
-        save(LSE, CTX)
-        copies.ready(WO)
-        at[WIDE][...] = mm(at[CTX][...], at[WO][...], NN)
-
-        def first_norm(rows):
-            branch = at[WIDE][rows, :] + vec(bo)
-            alive = at[LIVE][rows, 0:1]
-            at[STATS][0:8, :] += fold8(branch * branch * alive)
-            unit, rate = normed(at[X][rows, :].astype(F32) + branch)
-            hidden = unit * vec(g1) + vec(s1)
-            at[N1][rows, :] = unit.astype(BF16)
-            at[R1][rows, :] = jnp.broadcast_to(rate, (ROW_BLOCK, LANES))
-            at[HID][rows, :] = hidden.astype(BF16)
-            at[WIDE][rows, :] = hidden
-
-        over_rows(first_norm)
-        save(N1, R1, HID)
-        copies.ready(WU)
-
-        def up(part):
-            upper = mm(at[HID][...], at[WU][:, part], NN) + bu[0:1, part].astype(F32)
-            half = 0.5 + 0.5 * lax.erf(upper * 0.5**0.5)
-            bell = jnp.exp2(upper * upper * (-0.5 * LOG2E)) * 0.3989422804014327
-            at[ACT][:, part] = (upper * half).astype(BF16)
-            at[GP][:, part] = (half + upper * bell).astype(BF16)
-
-        over_tiles(inner, inner // 4, up)
-        save(ACT, GP)
-        copies.ready(WD)
-        at[FEED][...] = mm(at[ACT][...], at[WD][...], NN)
-
-        def second_norm(rows):
-            ffn = at[FEED][rows, :] + vec(bd)
-            alive = at[LIVE][rows, 0:1]
-            at[STATS][8:16, :] += fold8(ffn * ffn * alive)
-            unit, rate = normed(at[WIDE][rows, :] + ffn)
-            result = unit * vec(g2) + vec(s2)
-            at[STATS][16:24, :] += fold8(result * result * alive)
-            at[N2][rows, :] = unit.astype(BF16)
-            at[R2][rows, :] = jnp.broadcast_to(rate, (ROW_BLOCK, LANES))
-            at[Y][rows, :] = result.astype(BF16)
-
-        over_rows(second_norm)
-        save(Y, STATS, N2, R2)
+        source = ins[0].at[pl.ds(x_row * SEQ, SEQ), :]
+        run_forward(at, copies, save, row, source, ins[1:4], ins[4:])
         copies.finish()
 
 
@@ -379,7 +388,7 @@
     inputs = [(x, ANY)] + [(array, WHOLE) for array in ids]
     inputs += [(array, ANY if array.ndim == 3 else WHOLE) for array in params]
     made = call(
-        partial(forward_kernel, section, row, x_row, width // HEAD_DIM),
+        partial(forward_kernel, section, row, x_row),
         "forward",
         inputs,
         {} if kept is None else {i: kept[name] for i, name in enumerate(SAVED)},
@@ -453,6 +462,42 @@
     at[DELTA][...] = mm(pick, high, NT) + mm(pick, rest, NT)
 
 
+def run_backward(at, copies, get, save, params, shared):
+    gain1, gain2 = params[:2]
+    width, inner = at[WU].shape
+    get(G, N2, R2)
+    for name in (SUMS_A, SUMS_B):
+        at[name][...] = jnp.zeros(at[name].shape, F32)
+    copies.ready(G, N2, R2)
+    get(WD, GP)
+    second_norm_back(at, gain2, at[DFFN], 0)
+    save(DFFN)
+    get(WU, N1, R1, WO, CTX)
+    copies.ready(WD, GP)
+
+    def up(part):
+        at[DUP][:, part] = up_back(at, at[DFFN][...], part)
+
+    over_tiles(inner, inner // 4, up)
+    save(DUP, SUMS_A)
+    get(QKV, KID, QID, LSE, WQKV)
+    copies.ready(WU)
+    at[WIDE][...] += mm(at[DUP][...], at[WU][...], NT)
+    copies.ready(N1, R1)
+    first_norm_back(at, gain1, at[DBR], 0)
+    save(DBR, SUMS_B)
+    copies.ready(WO, CTX)
+    context_back(at, at[DBR][...], at[CTX][...])
+    copies.ready(QKV, KID, QID, LSE)
+    if shared is not None:
+        shared.go()
+    over_pairs(width, lambda j: attend_pair_back(j, width, at, at[DQKV], 0))
+    save(DQKV, SUMS_C)
+    copies.ready(WQKV)
+    at[DX][...] = (at[WIDE][...] + mm(at[DQKV][...], at[WQKV][...], NT)).astype(BF16)
+    save(DX)
+
+
 BACK_READ = (N2, R2, GP, N1, R1, CTX, LSE, KID, QID, QKV)
 SHARE_READ = (ACT, HID, X)
 BACK_HELD = (G,) + BACK_READ + GRADS + (WIDE, DCTX, DELTA, DX, WQKV, WO, WU, WD)
@@ -462,6 +507,8 @@
     ins, outs, refs = split_refs(n_in, n_old, n_out, refs)
     g_hbm, gain1, gain2, wq, wk, wv, wo, wu, wd = ins[:9]
     given = dict(zip(BACK_READ + SHARE_READ, ins[9:]))
+    given.update({WO: wo.at[0], WU: wu.at[0], WD: wd.at[0]})
+    given[G] = g_hbm.at[pl.ds(g_row * SEQ, SEQ), :]
     with_shares = section == 0
     out = dict(zip(GRADS + (DX,), outs))
     at = dict(zip(BACK_HELD + (SHARE_READ if with_shares else ()), refs))
@@ -488,49 +535,16 @@
 
         def get(*names):
             for name in names:
-                copies.load(name, given[name])
+                if name == WQKV:
+                    load_qkv(copies, (wq, wk, wv), width)
+                else:
+                    copies.load(name, given[name])
 
         def save(*names):
             for name in names:
                 copies.store(at[name], out[name])
 
-        copies.load(G, g_hbm.at[pl.ds(g_row * SEQ, SEQ), :])
-        get(N2, R2)
-        for name in (SUMS_A, SUMS_B):
-            at[name][...] = jnp.zeros(at[name].shape, F32)
-        copies.ready(G, N2, R2)
-        copies.load(WD, wd.at[0])
-        get(GP)
-        second_norm_back(at, gain2, at[DFFN], 0)
-        save(DFFN)
-        copies.ready(WD, GP)
-        copies.load(WU, wu.at[0])
-        get(N1, R1)
-        copies.load(WO, wo.at[0])
-        get(CTX)
-
-        def up(part):
-            at[DUP][:, part] = up_back(at, at[DFFN][...], part)
-
-        over_tiles(inner, inner // 4, up)
-        save(DUP, SUMS_A)
-        copies.ready(WU)
-        get(QKV, KID, QID, LSE)
-        load_qkv(copies, (wq, wk, wv), width)
-        at[WIDE][...] += mm(at[DUP][...], at[WU][...], NT)
-        copies.ready(N1, R1)
-        first_norm_back(at, gain1, at[DBR], 0)
-        save(DBR, SUMS_B)
-        copies.ready(WO, CTX)
-        context_back(at, at[DBR][...], at[CTX][...])
-        copies.ready(QKV, KID, QID, LSE)
-        if with_shares:
-            shared.go()
-        over_pairs(width, lambda j: attend_pair_back(j, width, at, at[DQKV], 0))
-        save(DQKV, SUMS_C)
-        copies.ready(WQKV)
-        at[DX][...] = (at[WIDE][...] + mm(at[DQKV][...], at[WQKV][...], NT)).astype(BF16)
-        save(DX)
+        run_backward(at, copies, get, save, ins[1:3], shared if with_shares else None)
         copies.finish()
 
     if not with_shares:
@@ -584,48 +598,95 @@
     return dict(zip(GRADS, made)), made[len(GRADS) :]
 
 
+KEPT = (X, CTX, HID, ACT)
+BOTH_HELD = FORWARD_HELD + (G,) + GRADS + (DCTX, DELTA, DX)
+
+
+def both_kernel(row, n_in, n_old, n_out, *refs):
+    ins, outs, refs = split_refs(n_in, n_old, n_out, refs)
+    out = dict(zip(KEPT + (Y, STATS) + GRADS + (DX,), outs))
+    at = dict(zip(BOTH_HELD, refs))
+    params = ins[5:]
+
+    @pl.when(lax.axis_index(LAYER) == 1)
+    def _():
+        copies = Copies(at, refs[-1])
+
+        def save(*names):
+            for name in names:
+                if name in out:
+                    copies.store(at[name], out[name])
+
+        def get(*names):
+            pass
+
+        def later():
+            copies.load(G, ins[1].at[pl.ds(row * SEQ, SEQ), :])
+
+        run_forward(at, copies, save, row, ins[0], ins[2:5], params, later)
+        run_backward(at, copies, get, save, (params[7], params[13]), None)
+        copies.finish()
+
+
+def through_and_back(row, x, g, ids, params, kept):
+    shapes = shapes_of(*params[9].shape[1:])
+    inputs = [(x, ANY), (g, ANY)] + [(array, WHOLE) for array in ids]
+    inputs += [(array, ANY if array.ndim == 3 else WHOLE) for array in params]
+    names = KEPT + (Y, STATS) + GRADS + (DX,)
+    made = call(
+        partial(both_kernel, row),
+        "both",
+        inputs,
+        {i: kept[name] for i, name in enumerate(KEPT)},
+        [shapes[name] for name in names],
+        [shapes[name] for name in BOTH_HELD],
+        48,
+    )
+    made = dict(zip(names, made))
+    kept = {**kept, **{name: made[name] for name in KEPT}}
+    return kept, made[Y], made[STATS], {name: made[name] for name in GRADS}, made[DX]
+
+
 N_TILES = 4
 
 
-def gradient_shapes(rows, columns):
+def gradient_shapes(*sizes):
     count = lax.axis_size(ROWS)
-    if count == 16:
-        return ((8, 2, rows // count, columns), BF16), [((8, rows // count, columns), BF16)] * 2
-    return ((rows, columns), BF16), [((rows, columns), BF16)]
+    if count != 16:
+        shapes = [(size, BF16) for size in sizes]
+        return shapes, shapes
+    tall = sum(rows * columns for rows, columns in sizes) // (count * min(map(min, sizes)))
+    width = min(map(min, sizes))
+    return [((8, 2, tall, width), BF16)], [((8, tall, width), BF16)] * 2
 
 
 class GradientOut:
-    def __init__(self, ref, targets, sems, first_sem, by_rows):
+    def __init__(self, ref, targets, sems, first_sem, tile, by_rows, base=0):
         self.ref, self.targets, self.sems, self.first_sem = ref, targets, sems, first_sem
-        self.by_rows = by_rows
+        self.tile, self.by_rows, self.base = tile, by_rows, base
         self.plain = len(targets) == 1
+        self.tall = tile // 4 if by_rows else tile // 16
+
+    def at(self, i):
+        start = i * self.tile
+        if self.plain and self.by_rows:
+            return (pl.ds(pl.multiple_of(start, 16), self.tile),)
         if self.plain:
-            self.rows, self.columns = ref.shape
-        else:
-            self.rows, self.columns = ref.shape[0] * 2 * ref.shape[2], ref.shape[3]
-        self.tile = (self.rows if by_rows else self.columns) // N_TILES
+            return (slice(None), lanes_at(start, self.tile))
+        if self.by_rows:
+            return (pl.ds(2 * i, 2), pl.ds(self.base, self.tall))
+        return (slice(None), pl.ds(pl.multiple_of(self.base + i * self.tall, 16), self.tall))
 
     def moves(self, i):
-        start = i * self.tile
+        at = self.at(i)
         if self.plain:
-            at = (
-                (pl.ds(start, self.tile), slice(None))
-                if self.by_rows
-                else (slice(None), lanes_at(start, self.tile))
-            )
             pairs = [(self.ref.at[at], self.targets[0].at[at])]
         else:
-            block = self.ref.shape[2]
-            count = self.tile // (2 * block)
             core = lax.axis_index(ROWS) % 2
-            pairs = []
-            for target, which in zip(self.targets, (core, 1 - core)):
-                if self.by_rows:
-                    rows = pl.ds(i * count, count)
-                    pairs.append((self.ref.at[rows, which], target.at[rows]))
-                else:
-                    lanes = lanes_at(start, self.tile)
-                    pairs.append((self.ref.at[:, which, :, lanes], target.at[:, :, lanes]))
+            pairs = [
+                (self.ref.at[at[0], which, at[1]], target.at[at])
+                for target, which in zip(self.targets, (core, 1 - core))
+            ]
         base = self.first_sem + i * len(pairs)
         return [
             pltpu.make_async_copy(source, target, self.sems.at[base + k])
@@ -634,17 +695,12 @@
 
     def put(self, i, value):
         value = value.astype(BF16)
-        start = i * self.tile
-        if self.plain and self.by_rows:
-            self.ref[pl.ds(pl.multiple_of(start, 16), self.tile), :] = value
-        elif self.plain:
-            self.ref[:, lanes_at(start, self.tile)] = value
+        at = self.at(i)
+        if self.plain:
+            self.ref[at] = value
         else:
-            split = value.reshape(-1, 2, self.ref.shape[2], value.shape[1])
-            if self.by_rows:
-                self.ref[pl.ds(i * split.shape[0], split.shape[0])] = split
-            else:
-                self.ref[:, :, :, lanes_at(start, self.tile)] = split
+            split = value.reshape(-1, 2, self.tall, value.shape[1])
+            self.ref[at[0], :, at[1], :] = split
         for move in self.moves(i):
             move.start()
 
@@ -662,24 +718,59 @@
     lax.fori_loop(0, N_TILES, body, 0)
 
 
-def down_kernel(n_in, n_old, n_out, *refs):
+FEED_HELD = (G, N2, R2, WIDE, SUMS_A, ACT, DFFN, WD, GP, HID, DUP, FEED, REST)
+
+
+def feed_kernel(n_in, n_old, n_out, *refs):
     ins, outs, refs = split_refs(n_in, n_old, n_out, refs)
-    g_hbm, gain2, n2, r2, act_hbm, share = ins
-    dffn_out, sums_out, wide_out = outs[:3]
-    at = dict(zip((G, N2, R2, WIDE, SUMS_A, ACT, DFFN, DX), refs))
-    total, sems = refs[-2:]
+    g_hbm, gain2, n2, r2, act_hbm, down_share, wd_hbm, gp_hbm, hid_hbm, up_share = ins
+    dffn_out, dup_out, sums_out, wide_out = outs[:4]
+    at = dict(zip(FEED_HELD, refs))
+    totals, sems = refs[len(FEED_HELD) : -1], refs[-1]
+    inner, width = at[WD].shape
+    tile = inner // N_TILES
+    if len(totals) == 1:
+        ways = [(totals[0], outs[4:]), (totals[0], outs[4:])]
+    else:
+        ways = [(total, [target]) for total, target in zip(totals, outs[4:])]
+    down_way = GradientOut(*ways[0], sems, 40, tile, True)
+    up_way = GradientOut(*ways[1], sems, 50, tile, False, tile // 4)
+    is_first = lax.axis_index(LAYER) == 0
     copies = Copies(at, sems)
     own = Copies(at, sems)
-    own.used = 10
-    own.load(G, g_hbm, now=False)
-    own.load(N2, n2, now=False)
-    own.load(R2, r2, now=False)
-    for name, target in ((DFFN, dffn_out), (SUMS_A, sums_out), (WIDE, wide_out)):
-        own.store(at[name], target, now=False)
+    own.used = 4
+    for name, source in ((G, g_hbm), (N2, n2), (R2, r2)):
+        own.load(name, source, now=False)
+    targets = ((DFFN, dffn_out), (WIDE, wide_out), (SUMS_A, sums_out))
+    stores = [own.store(at[name], target, now=False) for name, target in targets]
     other = Copies(at, sems)
-    other.used = 20
+    other.used = 12
     other.load(DFFN, dffn_out, now=False)
-    is_first = lax.axis_index(LAYER) == 0
+    other.load(DUP, dup_out, now=False)
+
+    def fetch(i):
+        part = lanes_at(i * tile, tile)
+        pairs = (
+            (up_share.at[:, part], at[REST].at[:, part]),
+            (wd_hbm.at[0, part, :], at[WD].at[part, :]),
+            (gp_hbm.at[:, part], at[GP].at[:, part]),
+        )
+        return [
+            pltpu.make_async_copy(source, target, sems.at[16 + 3 * i + k])
+            for k, (source, target) in enumerate(pairs)
+        ]
+
+    def fetch_start(i):
+        fetch(i)[0].start()
+
+        @pl.when(is_first)
+        def _():
+            for move in fetch(i)[1:]:
+                move.start()
+
+    def away(i):
+        part = lanes_at(i * tile, tile)
+        return pltpu.make_async_copy(at[DUP].at[:, part], dup_out.at[:, part], sems.at[32 + i])
 
     @pl.when(is_first)
     def _():
@@ -688,101 +779,36 @@
         own.ready(G, N2, R2)
 
     copies.load(ACT, act_hbm)
-    copies.load(DX, share)
+    copies.load(FEED, down_share)
 
     @pl.when(is_first)
     def _():
         second_norm_back(at, gain2, at[DFFN], 0)
-        for way in own.stores:
+        for way in stores[:2]:
             way.start()
 
     @pl.when(jnp.logical_not(is_first))
     def _():
         other.go()
-        other.ready(DFFN)
-
-    copies.ready(ACT, DX)
-    way_out = GradientOut(total, outs[3:], sems, 24, True)
-
-    def step(i):
-        part = lanes_at(i * way_out.tile, way_out.tile)
+        other.ready(DFFN, DUP)
+
+    copies.load(HID, hid_hbm)
+    fetch_start(0)
+    copies.ready(ACT, FEED)
+    fetch_start(1)
+
+    def down_step(i):
+        part = lanes_at(i * tile, tile)
         made = mm(at[ACT][:, part], at[DFFN][...], TN)
-        way_out.put(i, made + at[DX][part, :].astype(F32))
-
-    loop_tiles(step)
-    way_out.finish()
-
-    @pl.when(is_first)
-    def _():
-        own.finish()
-
-
-def up_kernel(n_in, n_old, n_out, *refs):
-    ins, outs, refs = split_refs(n_in, n_old, n_out, refs)
-    wd_hbm, gp_hbm, hid_hbm, dffn_hbm, share = ins
-    dup_out, sums_out = outs[:2]
-    at = dict(zip((WD, GP, HID, DUP, DFFN, SUMS_A, DX), refs))
-    total, sems = refs[-2:]
-    is_first = lax.axis_index(LAYER) == 0
-    way_out = GradientOut(total, outs[2:], sems, 24, False)
-    copies = Copies(at, sems)
-    copies.load(HID, hid_hbm)
-    own = Copies(at, sems)
-    own.used = 1
-    own.load(DFFN, dffn_hbm, now=False)
-    own.load(SUMS_A, sums_out, now=False)
-    own.store(at[SUMS_A], sums_out, now=False)
-    other = Copies(at, sems)
-    other.used = 4
-    other.load(DUP, dup_out, now=False)
-
-    def fetch(i):
-        part = lanes_at(i * way_out.tile, way_out.tile)
-        pairs = (
-            (share.at[:, part], at[DX].at[:, part]),
-            (wd_hbm.at[0, part, :], at[WD].at[part, :]),
-            (gp_hbm.at[:, part], at[GP].at[:, part]),
-        )
-        return [
-            pltpu.make_async_copy(source, target, sems.at[8 + 3 * i + k])
-            for k, (source, target) in enumerate(pairs)
-        ]
-
-    def away(i):
-        part = lanes_at(i * way_out.tile, way_out.tile)
-        return pltpu.make_async_copy(at[DUP].at[:, part], dup_out.at[:, part], sems.at[20 + i])
-
-    def fetch_start(i):
-        moves = fetch(i)
-        moves[0].start()
-
-        @pl.when(is_first)
-        def _():
-            for move in fetch(i)[1:]:
-                move.start()
-
-    @pl.when(is_first)
-    def _():
-        own.go()
-
-    @pl.when(jnp.logical_not(is_first))
-    def _():
-        other.go()
-        other.ready(DUP)
-
-    fetch_start(0)
+        down_way.put(i, made + at[FEED][part, :].astype(F32))
+
+    loop_tiles(down_step)
+    fetch_start(2)
+    fetch_start(3)
     copies.ready(HID)
 
-    @pl.when(is_first)
-    def _():
-        own.ready(DFFN, SUMS_A)
-
-    def step(i):
-        @pl.when(i < N_TILES - 1)
-        def _():
-            fetch_start(i + 1)
-
-        part = lanes_at(i * way_out.tile, way_out.tile)
+    def up_step(i):
+        part = lanes_at(i * tile, tile)
 
         @pl.when(is_first)
         def _():
@@ -793,14 +819,15 @@
 
         fetch(i)[0].wait()
         made = mm(at[HID][...], at[DUP][:, part], TN)
-        way_out.put(i, made + at[DX][:, part].astype(F32))
-
-    loop_tiles(step)
-    way_out.finish()
+        up_way.put(i, made + at[REST][:, part].astype(F32))
+
+    loop_tiles(up_step)
+    down_way.finish()
+    up_way.finish()
 
     @pl.when(is_first)
     def _():
-        own.stores[0].start()
+        stores[2].start()
         for i in range(N_TILES):
             away(i).wait()
         own.finish()
@@ -844,13 +871,14 @@
 
 
 ATTEND_READ = (QKV, DCTX, KID, QID, LSE, DELTA)
+ATTEND_HELD = ATTEND_READ + (X, CTX, DBR, REST, WIDE, WQKV, DQKV, SUMS_C, DX)
 
 
 def attend_kernel(n_in, n_old, n_out, *refs):
     ins, outs, refs = split_refs(n_in, n_old, n_out, refs)
-    x_hbm, ctx_hbm, dbr_hbm, share = ins[len(ATTEND_READ) :]
-    dqkv_out, sums_out = outs[:2]
-    at = dict(zip(ATTEND_READ + (X, CTX, DBR, DX, DQKV, SUMS_C), refs))
+    x_hbm, ctx_hbm, dbr_hbm, share, wide_hbm, wq, wk, wv = ins[len(ATTEND_READ) :]
+    dqkv_out, sums_out, dx_out = outs[:3]
+    at = dict(zip(ATTEND_HELD, refs))
     total, sems = refs[-2:]
     width = at[X].shape[1]
     is_first = lax.axis_index(LAYER) == 0
@@ -859,10 +887,15 @@
     own.used = 6
     for name, source in zip(ATTEND_READ, ins):
         own.load(name, source, now=False)
-    own.store(at[DQKV], dqkv_out, now=False)
-    own.store(at[SUMS_C], sums_out, now=False)
+    targets = ((DQKV, dqkv_out), (SUMS_C, sums_out), (DX, dx_out))
+    stores = [own.store(at[name], target, now=False) for name, target in targets]
+    late = Copies(at, sems)
+    late.used = 16
+    late.load(WIDE, wide_hbm, now=False)
+    for i, weight in enumerate((wq, wk, wv)):
+        late.load(WQKV, weight.at[0], at[WQKV].at[:, pl.ds(i * width, width)], now=False)
     other = Copies(at, sems)
-    other.used = 20
+    other.used = 22
     other.load(DQKV, dqkv_out, now=False)
 
     @pl.when(is_first)
@@ -870,13 +903,14 @@
         own.go()
         own.ready(*ATTEND_READ)
 
-    for name, source in ((X, x_hbm), (CTX, ctx_hbm), (DBR, dbr_hbm), (DX, share)):
+    for name, source in ((X, x_hbm), (CTX, ctx_hbm), (DBR, dbr_hbm), (REST, share)):
         copies.load(name, source)
 
     @pl.when(is_first)
     def _():
+        late.go()
         over_pairs(width, lambda j: attend_pair_back(j, width, at, at[DQKV], 0))
-        for way in own.stores:
+        for way in stores[:2]:
             way.start()
 
     @pl.when(jnp.logical_not(is_first))
@@ -884,38 +918,25 @@
         other.go()
         other.ready(DQKV)
 
-    copies.ready(X, CTX, DBR, DX)
-    way_out = GradientOut(total, outs[2:], sems, 24, False)
-    way_out.put(0, mm(at[CTX][...], at[DBR][...], TN) + at[DX][:, 0:width].astype(F32))
+    copies.ready(X, CTX, DBR, REST)
+    way_out = GradientOut(total, outs[3:], sems, 24, width, False)
+    way_out.put(0, mm(at[CTX][...], at[DBR][...], TN) + at[REST][:, 0:width].astype(F32))
 
     def step(i, carry):
         made = mm(at[X][...], at[DQKV][:, lanes_at((i - 1) * width, width)], TN)
-        way_out.put(i, made + at[DX][:, lanes_at(i * width, width)].astype(F32))
+        way_out.put(i, made + at[REST][:, lanes_at(i * width, width)].astype(F32))
         return carry
 
     lax.fori_loop(1, N_TILES, step, 0)
-    way_out.finish()
 
     @pl.when(is_first)
     def _():
+        late.ready(WIDE, WQKV)
+        at[DX][...] = (at[WIDE][...] + mm(at[DQKV][...], at[WQKV][...], NT)).astype(BF16)
+        stores[2].start()
         own.finish()
 
-
-def input_kernel(n_in, n_old, n_out, *refs):
-    ins, outs, refs = split_refs(n_in, n_old, n_out, refs)
-    dqkv1, wide_in, wq, wk, wv = ins
-    at = dict(zip((DQKV, WIDE, WQKV, DX), refs))
-
-    @pl.when(lax.axis_index(LAYER) == 0)
-    def _():
-        copies = Copies(at, refs[-1])
-        copies.load(DQKV, dqkv1)
-        load_qkv(copies, (wq, wk, wv), at[WIDE].shape[1])
-        copies.load(WIDE, wide_in)
-        copies.ready(DQKV, WQKV, WIDE)
-        at[DX][...] = (at[WIDE][...] + mm(at[DQKV][...], at[WQKV][...], NT)).astype(BF16)
-        copies.store(at[DX], outs[0])
-        copies.finish()
+    way_out.finish()
 
 
 def swap(array, stride):
@@ -923,89 +944,77 @@
     return lax.ppermute(array, ROWS, [(d, d ^ stride) for d in range(count)])
 
 
-def halves_kernel(ways, merged, n_in, n_old, n_out, *refs):
+def halves_kernel(jobs, n_in, n_old, n_out, *refs):
     ins, outs, refs = split_refs(n_in, n_old, n_out, refs)
     copies = Copies({}, refs[-1])
-    jobs = []
-    for side in (0, 1):
-        for way, (stride, before, after) in enumerate(ways):
-            left, right, total = refs[3 * len(jobs) : 3 * len(jobs) + 3]
-            size = total.shape[-1]
-            own = (lax.axis_index(ROWS) // stride) % 2
-            which = own if side else 1 - own
-            sources = ins if n_in == 2 else ins[2 * way : 2 * way + 2]
-            columns = pl.ds(way * size if n_in == 2 and len(ways) == 2 else 0, size)
-            for i in range(before):
-                taken = pl.ds((2 * i + which) * after, after)
-                for source, buffer in zip(sources, (left, right)):
-                    target = buffer.at[pl.ds(i * after, after)]
-                    copies.load(len(jobs), source.at[taken, :, columns], target)
-            if merged:
-                target = outs[side].at[:, :, pl.ds(way * size, size)]
-            else:
-                target = outs[2 * way + side]
-            jobs.append((left, right, total, target))
-    for i, (left, right, total, target) in enumerate(jobs):
+    buffers = [refs[3 * i : 3 * i + 3] for i in range(len(jobs))]
+    for i, job in enumerate(jobs):
+        sources, stride, before, after, start, size, keep = job[:7]
+        own = (lax.axis_index(ROWS) // stride) % 2
+        which = own if keep else 1 - own
+        for k in range(before):
+            taken = pl.ds((2 * k + which) * after, after)
+            for source, buffer in zip(sources, buffers[i]):
+                target = buffer.at[pl.ds(k * after, after)]
+                copies.load(i, ins[source].at[taken, :, pl.ds(start, size)], target)
+    for i, job in enumerate(jobs):
+        left, right, total = buffers[i]
         copies.ready(i)
         total[...] = (left[...].astype(F32) + right[...].astype(F32)).astype(BF16)
-        copies.store(total, target)
+        place, start = job[7:]
+        copies.store(total, outs[place].at[:, :, pl.ds(start, total.shape[-1])])
     copies.finish()
 
 
-def halves(ways, arrays, merged=False):
-    block = arrays[0].shape[1:]
-    columns = block[1] // 2 if len(arrays) == 2 else block[1]
-    parts = [((before * after, block[0], columns), BF16) for _, before, after in ways]
-    if merged:
-        outs = [((1, block[0], 2 * columns), BF16)] * 2
-    else:
-        outs = [part for part in parts for _ in (0, 1)]
-    scratch = [part for _ in (0, 1) for part in parts for _ in range(3)]
+def halves(ways, arrays, n_outs):
+    tall = arrays[0].shape[1]
+    jobs, scratch = [], []
+    outs = [None] * (2 * n_outs)
+    for keep in (0, 1):
+        for sources, stride, before, after, start, size, place, column in ways:
+            jobs.append((sources, stride, before, after, start, size, keep, place + keep * n_outs, column))
+            scratch += [((before * after, tall, size), BF16)] * 3
+            outs[place + keep * n_outs] = ((before * after, tall, column + size), BF16)
     inputs = [(array, ANY) for array in arrays]
-    return call(partial(halves_kernel, ways, merged), "halves", inputs, {}, outs, scratch, 32)
+    made = call(partial(halves_kernel, tuple(jobs)), "halves", inputs, {}, outs, scratch, 48)
+    return made[:n_outs], made[n_outs:]
 
 
 class ScatterSum:
-    def __init__(self, blocks):
-        self.shape = blocks[0].shape[1:]
-        self.blocks = blocks
-        self.done = 0
-        self.plain = lax.axis_size(ROWS) != 16
-        self.kept = blocks[0]
-
-    def advance(self, first=None):
-        if self.plain:
-            return self.blocks[0]
-        if first is not None:
-            self.kept = lax.optimization_barrier((self.kept, first))[0]
-        self.done += 1
-        if self.done == 1:
-            self.kept, send = self.blocks
-            self.arrived = swap(send, 1)
-            return send
-        before = self.arrived
-        if self.done == 2:
-            made = halves(((2, 4, 1), (4, 2, 2)), (self.kept, before))
-            self.kept = made[1::2]
-            self.arrived = (swap(made[0], 2), swap(made[2], 4))
-        elif self.done == 3:
-            arrays = (self.kept[0], before[0], self.kept[1], before[1])
-            made = halves(((4, 2, 1), (2, 2, 1)), arrays)
-            self.kept = made[1::2]
-            self.arrived = (swap(made[0], 4), swap(made[2], 2))
-        else:
-            arrays = (self.kept[0], before[0], self.kept[1], before[1])
-            send, self.kept = halves(((8, 1, 1), (8, 1, 1)), arrays, True)
-            self.arrived = swap(send, 8)
-        return before
+    def __init__(self, kept, came):
+        self.kept, self.came = kept, came
+
+    @staticmethod
+    def cores(blocks):
+        return ScatterSum(blocks[0], swap(blocks[1], 1))
+
+    def second(self, first):
+        kept = lax.optimization_barrier((self.kept, first))[0]
+        half = kept.shape[-1] // 2
+        ways = (((0, 1), 2, 4, 1, 0, half, 0, 0), ((0, 1), 4, 2, 2, half, half, 1, 0))
+        sent, kept = halves(ways, (kept, self.came), 2)
+        return ScatterSum(tuple(kept), (swap(sent[0], 2), swap(sent[1], 4)))
+
+    def third(self, first):
+        kept = lax.optimization_barrier((self.kept, first))[0]
+        half = kept[0].shape[-1]
+        ways = (((0, 1), 4, 2, 1, 0, half, 0, 0), ((2, 3), 2, 2, 1, 0, half, 1, 0))
+        sent, kept = halves(ways, (kept[0], self.came[0], kept[1], self.came[1]), 2)
+        return ScatterSum(tuple(kept), (swap(sent[0], 4), swap(sent[1], 2)))
+
+    def fourth(self, first):
+        kept = lax.optimization_barrier((self.kept, first))[0]
+        half = kept[0].shape[-1]
+        ways = tuple(((2 * i, 2 * i + 1), 8, 1, 1, 0, half, 0, i * half) for i in range(2))
+        sent, kept = halves(ways, (kept[0], self.came[0], kept[1], self.came[1]), 1)
+        return ScatterSum(kept[0], swap(sent[0], 8))
 
     def finish(self):
-        if self.plain:
-            total = lax.psum_scatter(self.blocks[0], ROWS, scatter_dimension=0, tiled=True)
-            return total.astype(F32)
-        while self.done < 4:
-            self.advance()
-        return (self.kept.astype(F32) + self.arrived.astype(F32)).reshape(self.shape)
+        return (self.kept.astype(F32) + self.came.astype(F32))[0]
+
+
+def whole_sum(partial_sum):
+    return lax.psum_scatter(partial_sum, ROWS, scatter_dimension=0, tiled=True).astype(F32)
 
 
 def small_sum(values, beside, after):
@@ -1036,12 +1045,10 @@
     in0 = hop(y0, 0, 1)
     row1, y1, stats01 = forward(0, 1, tokens, 1, ids, params, None)
     in1 = hop(y1, 0, 1)
-    row0, out0, stats10 = forward(1, 0, in0, 0, ids, params, row0)
-    grads0, (dx0,) = backward(1, cotangent, 0, params, row0, None)
+    row0, out0, stats10, grads0, dx0 = through_and_back(0, in0, cotangent, ids, params, row0)
     in1 = after(in1, dx0)
     g0 = hop(dx0, 1, 0)
-    row1, out1, stats11 = forward(1, 1, in1, 0, ids, params, row1)
-    grads1, (dx1,) = backward(1, cotangent, 1, params, row1, None)
+    row1, out1, stats11, grads1, dx1 = through_and_back(1, in1, cotangent, ids, params, row1)
     g0 = after(g0, dx1)
     g1 = hop(dx1, 1, 0)
     grads0, (dx0, down_share, up_share, rest_share) = backward(0, g0, 0, params, row0, grads0)
@@ -1053,37 +1060,23 @@
     def of(*names):
         return [shapes[name] for name in names]
 
-    total, parts = gradient_shapes(inner, width)
+    totals, parts = gradient_shapes((inner, width), (width, inner))
+    plain = len(totals) == 2
     made = call(
-        down_kernel,
-        "down_gradient",
+        feed_kernel,
+        "feed",
         at_hbm(g1)
         + [(gain2, WHOLE)]
-        + at_hbm(row1[N2], row1[R2], row1[ACT], down_share),
-        {0: grads1[DFFN], 1: grads1[SUMS_A]},
-        of(DFFN, SUMS_A, WIDE) + parts,
-        of(G, N2, R2, WIDE, SUMS_A, ACT, DFFN) + of(WD) + [total],
-        40,
+        + at_hbm(row1[N2], row1[R2], row1[ACT], down_share, wd, row1[GP], row1[HID], up_share),
+        {0: grads1[DFFN], 1: grads1[DUP], 2: grads1[SUMS_A]},
+        of(DFFN, DUP, SUMS_A, WIDE) + parts,
+        of(G, N2, R2, WIDE, SUMS_A, ACT, DFFN, WD, GP, HID, DUP, WD, WU) + totals,
+        60,
     )
-    dffn1, sums_a1, wide = made[:3]
-    down_sum = ScatterSum(made[3:])
-    down_sum.advance()
-
-    total, parts = gradient_shapes(width, inner)
-    made = call(
-        up_kernel,
-        "up_gradient",
-        at_hbm(wd, row1[GP], row1[HID], dffn1, up_share),
-        {0: grads1[DUP], 1: sums_a1},
-        of(DUP, SUMS_A) + parts,
-        of(WD, GP, HID, DUP, DFFN, SUMS_A) + of(WU) + [total],
-        40,
-    )
-    dup1, sums_a1 = made[:2]
-    down_sum.advance(dup1)
-    up_sum = ScatterSum(after(tuple(made[2:]), down_sum.kept))
-    up_sum.advance()
-    wide = after(wide, down_sum.kept)
+    _, dup1, sums_a1, wide = made[:4]
+    feed_parts = made[4:]
+    if not plain:
+        feed_sum = ScatterSum.cores(feed_parts)
 
     made = call(
         middle_kernel,
@@ -1095,41 +1088,42 @@
         20,
     )
     dbr1, wide, dctx, delta, sums_b1 = made
-    up_sum.advance(dctx)
-    dctx = after(dctx, up_sum.kept)
-
-    total, parts = gradient_shapes(width, 4 * width)
+    if not plain:
+        feed_sum = feed_sum.second(dctx)
+        dctx = after(dctx, feed_sum.kept)
+
+    totals, parts = gradient_shapes((width, 4 * width))
     made = call(
         attend_kernel,
-        "attend_gradient",
+        "attend",
         at_hbm(row1[QKV], dctx, *(row1[name] for name in (KID, QID, LSE)), delta)
-        + at_hbm(row1[X], row1[CTX], dbr1, rest_share),
+        + at_hbm(row1[X], row1[CTX], dbr1, rest_share, wide, wq, wk, wv),
         {0: grads1[DQKV], 1: grads1[SUMS_C]},
-        of(DQKV, SUMS_C) + parts,
-        of(*ATTEND_READ) + of(X, CTX, DBR) + of(REST) + of(DQKV, SUMS_C) + [total],
+        of(DQKV, SUMS_C, DX) + parts,
+        of(*ATTEND_HELD) + totals,
         40,
     )
-    dqkv1, sums_c1 = made[:2]
-    down_sum.advance(dqkv1)
-    up_sum.advance(down_sum.kept)
-    rest_sum = ScatterSum(after(tuple(made[2:]), (down_sum.kept, up_sum.kept)))
-    rest_sum.advance()
-    wide = after(wide, up_sum.kept)
-    made = call(
-        input_kernel,
-        "input_gradient",
-        at_hbm(dqkv1, wide, wq, wk, wv),
-        {},
-        of(DX),
-        of(DQKV, WIDE, WQKV, DX),
-        8,
-    )
-    dx1 = made[0]
-    came = [rest_sum.advance(dx1)]
-    down_sum.advance(rest_sum.kept)
-    up_sum.advance(down_sum.kept)
-    came.append(rest_sum.advance(up_sum.kept))
-    came.append(rest_sum.advance())
+    _, sums_c1, dx1 = made[:3]
+    came = []
+    if plain:
+        w_down, w_up, w_rest = (whole_sum(part) for part in (*feed_parts, made[3]))
+        w_out, w_query, w_key, w_value = jnp.split(w_rest, 4, axis=1)
+    else:
+        feed_sum = feed_sum.third(dx1)
+        rest_sum = ScatterSum.cores(after(tuple(made[3:]), feed_sum.kept))
+        came.append(rest_sum.came)
+        rest_sum = rest_sum.second(feed_sum.kept)
+        dx1 = after(dx1, rest_sum.kept)
+        came.append(rest_sum.came)
+        feed_sum = feed_sum.fourth(rest_sum.kept)
+        rest_sum = rest_sum.third(feed_sum.kept)
+        came.append(rest_sum.came)
+        rest_sum = rest_sum.fourth(rest_sum.kept)
+        w_feed, w_rest = feed_sum.finish(), rest_sum.finish()
+        tall = inner // 16
+        w_down = w_feed[:tall]
+        w_up = jnp.concatenate(jnp.split(w_feed[tall:], N_TILES, axis=0), axis=1)
+        w_out, w_query, w_key, w_value = jnp.split(w_rest, 4, axis=0)
 
     sums_a1, sums_b1, sums_c1 = (after(array, dx1) for array in (sums_a1, sums_b1, sums_c1))
     stats10 = after(stats10, dx1)
@@ -1145,9 +1139,6 @@
     tail = jnp.concatenate([stats, jnp.broadcast_to(count, (1,)), jnp.zeros((spare,), F32)])
     small = jnp.concatenate(pieces + [tail]).reshape(-1, LANES)
     small = small_sum(small, came, after).reshape(-1)
-    w_down = down_sum.finish()
-    w_up = up_sum.finish()
-    w_rest = rest_sum.finish()
     shares = lax.axis_size(ROWS)
     me = lax.axis_index(ROWS)
 
@@ -1177,12 +1168,12 @@
     return (
         block_part,
         grad_part,
-        w_rest[None, :, width : 2 * width],
+        w_query[None],
         query_bias,
-        w_rest[None, :, 2 * width : 3 * width],
-        w_rest[None, :, 3 * width :],
+        w_key[None],
+        w_value[None],
         value_bias,
-        w_rest[None, :, :width],
+        w_out[None],
         out_bias,
         gain1_sum,
         shift1_sum,

time: 355 us -> 329 us (0.927)
  waiting for transfers between devices: 93.5 us -> 83.7 us
  Pallas kernels: 197 us -> 192 us
  starting transfers between devices: 28.1 us -> 24.1 us
  other arithmetic: 10.2 us -> 6.44 us
    ppermute x4, waiting for transfers between devices: 62.7 us -> 41.2 us  [hop(): return lax.ppermute(array, LAYER, [(source, target)])]
    ppermute x22 -> x16, waiting for transfers between devices: 30.8 us -> 42.5 us  [swap(): return lax.ppermute(array, ROWS, [(d, d ^ stride) for d in range(count)])]
    pallas_call x21 -> x14, Pallas kernels: 197 us -> 192 us  [call(): pl.pallas_call(partial(body, n_in, len(old), len(outs)), out_shape=[jax.S...]
    ppermute x22 -> x16, starting transfers between devices: 22.8 us -> 18.8 us  [swap(): return lax.ppermute(array, ROWS, [(d, d ^ stride) for d in range(count)])]
    unnamed x73 -> x53, local copies, waits for them, and re-layouts: 13.6 us -> 9.69 us
  transfers between devices with their start and end apart: 27 -> 21, of which waited for: 11 -> 13; matrix products, arithmetic and copies ran while one was open for 3% -> 3% of each run, Pallas kernels for 44% -> 43%
where the time goes in v4:
time: 329 us; the launch traced here: 322 us
  Pallas kernels  192 us (58%)
  waiting for transfers between devices  83.7 us (25%)
  starting transfers between devices  24.1 us (7%)
  local copies, waits for them, and re-layouts  14.4 us (4%)
  other arithmetic  6.44 us (2%)
    pallas_call x14, Pallas kernels, call(): pl.pallas_call(partial(body, n_in, len(old), len(outs)), out_shape=[jax.S...  192 us
    ppermute x16, waiting for transfers between devices, swap(): return lax.ppermute(array, ROWS, [(d, d ^ stride) for d in range(count)])  42.5 us
    ppermute x4, waiting for transfers between devices, hop(): return lax.ppermute(array, LAYER, [(source, target)])  41.2 us
    ppermute x16, starting transfers between devices, swap(): return lax.ppermute(array, ROWS, [(d, d ^ stride) for d in range(count)])  18.8 us
    unnamed x53, local copies, waits for them, and re-layouts  9.69 us
  transfers between devices with their start and end apart: 21, of which 13 were waited for; matrix products, arithmetic and copies ran while one was open for 3% of the time, Pallas kernels for 43%

profile of v4, /device:TPU:0, one launch (start us, length us, event | category | flops | bytes accessed | tf_op | source)
XLA Modules:
  0.0 322.2 jit_solution(5503339195958186391)
XLA Ops:
  2.1 25.6 %forward.2 = (bf16[512,768]{1,0:T(8,128)(2,1)}, bf16[512,2304]{1,0:T(8,128)(2,1)}, bf16[512,768]{1,0:T(8,128)(2,1)}, f32[16,512]{1,0:T(8,128)}, f32[512,768]{1,0...) custom-call(bf16[1024,768]{1,0:T(8,128)(2,1)} %refs_0_.3, ...), custom_call_target="tpu_custom_call" | custom-call | flops 1 | bytes 1 | tf_op jit(solution)/shard_map/forward/pallas_call | solution.py:141
  29.0 41.4 %forward.3 = (bf16[512,768]{1,0:T(8,128)(2,1)}, bf16[512,2304]{1,0:T(8,128)(2,1)}, bf16[512,768]{1,0:T(8,128)(2,1)}, f32[16,512]{1,0:T(8,128)}, f32[512,768]{1,0...) custom-call(bf16[1024,768]{1,0:T(8,128)(2,1)} %refs_0_.3, ...), custom_call_target="tpu_custom_call" | custom-call | flops 1 | bytes 1 | tf_op jit(solution)/shard_map/forward/pallas_call | solution.py:141
  72.7 1.7 both.2
  75.8 14.0 %collective-permute-done.2.refs_0_ = bf16[512,768]{1,0:T(8,128)(2,1)S(1)} collective-permute-done((bf16[512,768]{1,0:T(8,128)(2,1)}, bf16[512,768]{1,0:T(8,128)(2,1)S(1)}, u32[]{:S(2)}, u32[]{:S(2)}) %collective-permute-start.2) | collective-permute-done | bytes 786464 | tf_op jit(solution)/shard_map/ppermute | solution.py:1039
  90.6 8.2 %both.3 = (bf16[512,768]{1,0:T(8,128)(2,1)}, bf16[512,768]{1,0:T(8,128)(2,1)}, bf16[512,768]{1,0:T(8,128)(2,1)}, bf16[512,3072]{1,0:T(8,128)(2,1)}, bf16[512,768...) custom-call(bf16[512,768]{1,0:T(8,128)(2,1)} %copy-done.7, ...), custom_call_target="tpu_custom_call", output_to_operand_aliasing={{0}: (20, {}), {1}: (21, {}), {2}: (22, {}), {3}: (23, {})} | custom-call | flops 1 | bytes 1 | tf_op jit(solution)/shard_map/both/pallas_call | solution.py:141
  100.1 18.9 %collective-permute-done.1.refs_0_ = bf16[512,768]{1,0:T(8,128)(2,1)S(1)} collective-permute-done((bf16[512,768]{1,0:T(8,128)(2,1)}, bf16[512,768]{1,0:T(8,128)(2,1)S(1)}, u32[]{:S(2)}, u32[]{:S(2)}) %collective-permute-start.1) | collective-permute-done | bytes 786464 | tf_op jit(solution)/shard_map/ppermute | solution.py:1039
  119.9 42.7 %backward.1 = (bf16[512,768]{1,0:T(8,128)(2,1)}, bf16[512,3072]{1,0:T(8,128)(2,1)}, bf16[512,768]{1,0:T(8,128)(2,1)}, bf16[512,2304]{1,0:T(8,128)(2,1)}, f32[32,...) custom-call(bf16[512,768]{1,0:T(8,128)(2,1)} %copy-done.13, ...), custom_call_target="tpu_custom_call", output_to_operand_aliasing={{0}: (22, {}), {1}: (23, {}), {2}: (24, {}), {3}: (25, {}),... | custom-call | flops 1 | bytes 1 | tf_op jit(solution)/shard_map/backward/pallas_call | solution.py:141
  162.6 8.4 %collective-permute-done.3.refs_0_ = bf16[512,768]{1,0:T(8,128)(2,1)S(1)} collective-permute-done((bf16[512,768]{1,0:T(8,128)(2,1)}, bf16[512,768]{1,0:T(8,128)(2,1)S(1)}, u32[]{:S(2)}, u32[]{:S(2)}) %collective-permute-start.3) | collective-permute-done | bytes 786464 | tf_op jit(solution)/shard_map/ppermute | solution.py:1039
  171.8 18.7 %feed.1 = (bf16[512,768]{1,0:T(8,128)(2,1)}, bf16[512,3072]{1,0:T(8,128)(2,1)}, f32[32,3072]{1,0:T(8,128)}, f32[512,768]{1,0:T(8,128)}, bf16[8,384,768]{2,1,0:T(8,128)(2,1)}, /*index=5*/bf16[8,384,768]{2,1,0:T(8,128)(2,1)}) custom-call(bf16[512,768]{1,0:T(8,128)(2,1)} %copy-done.6, ...), custom_call_target="tpu_custom_call", output_to_operand_aliasing={{0}: (10, {}), {1}: (11, {}), {2}: (12, {})} | custom-call | flops 1 | bytes 1 | tf_op jit(solution)/shard_map/feed/pallas_call | solution.py:141
  190.7 11.2 %middle.1 = (bf16[512,768]{1,0:T(8,128)(2,1)}, f32[512,768]{1,0:T(8,128)}, bf16[512,768]{1,0:T(8,128)(2,1)}, f32[16,512]{1,0:T(8,128)}, f32[24,768]{1,0:T(8,128)}) custom-call(bf16[512,3072]{1,0:T(8,128)(2,1)} %get-tuple-element.191.refs_0_, f32[512,768]{1,0:T(8,128)} %get-tuple-element.192.refs_1_, ...), custom_call_target="tpu_custom_call", output_to_operand_aliasing={{0}: (8, {}), {4}: (9, {})} | custom-call | flops 1 | bytes 1 | tf_op jit(solution)/shard_map/middle/pallas_call | solution.py:141
  201.9 2.2 copy-done
  204.1 6.3 %halves.6 = (bf16[4,384,384]{2,1,0:T(8,128)(2,1)}, bf16[4,384,384]{2,1,0:T(8,128)(2,1)}, bf16[4,384,384]{2,1,0:T(8,128)(2,1)}, bf16[4,384,384]{2,1,0:T(8,128)(2,1)}) custom-call(bf16[8,384,768]{2,1,0:T(8,128)(2,1)} %get-tuple-element.200.refs_0_, bf16[8,384,768]{2,1,0:T(8,128)(2,1)} %copy-done), custom_call_target="tpu_custom_call" | custom-call | flops 1 | bytes 1 | tf_op jit(solution)/shard_map/halves/pallas_call | solution.py:141
  210.4 1.8 collective-permute-start.5
  212.2 1.6 collective-permute-start.6
  213.7 19.9 %attend.1 = (bf16[512,2304]{1,0:T(8,128)(2,1)}, f32[16,768]{1,0:T(8,128)}, bf16[512,768]{1,0:T(8,128)(2,1)}, bf16[8,192,768]{2,1,0:T(8,128)(2,1)}, bf16[8,192,768]{2,1,0:T(8,128)(2,1)}) custom-call(bf16[512,2304]{1,0:T(8,128)(2,1)} %get-tuple-element.179.refs_0_, ...), custom_call_target="tpu_custom_call", output_to_operand_aliasing={{0}: (14, {}), {1}: (15, {})} | custom-call | flops 1 | bytes 1 | tf_op jit(solution)/shard_map/attend/pallas_call | solution.py:141
  233.6 5.4 %collective-permute-done.5.refs_1_ = bf16[4,384,384]{2,1,0:T(8,128)(2,1)S(1)} collective-permute-done((bf16[4,384,384]{2,1,0:T(8,128)(2,1)}, bf16[4,384,384]{2,1,0:T(8,128)(2,1)S(1)}, u32[]{:S(2)}, u32[]{:S(2)}) %collective-permute-start.5) | collective-permute-done | bytes 1179680 | tf_op jit(solution)/shard_map/ppermute | solution.py:944
  241.5 3.7 %halves.7 = (bf16[2,384,384]{2,1,0:T(8,128)(2,1)}, bf16[2,384,384]{2,1,0:T(8,128)(2,1)}, bf16[2,384,384]{2,1,0:T(8,128)(2,1)}, bf16[2,384,384]{2,1,0:T(8,128)(2,1)}) custom-call(bf16[4,384,384]{2,1,0:T(8,128)(2,1)} %get-tuple-element.218.refs_0_, bf16[4,384,384]{2,1,0:T(8,128)(2,1)} %copy-done.4, bf16[4,384,384]{2,1,0:T(8,128)(2,1)} %get-tuple-element.220.refs_2_, ...), custom_call_target="tpu_custom_call" | custom-call | flops 1 | bytes 1 | tf_op jit(solution)/shard_map/halves/pallas_call | solution.py:141
  246.7 1.6 collective-permute-start.9
  251.5 3.9 %halves.8 = (bf16[4,192,384]{2,1,0:T(8,128)(2,1)}, bf16[4,192,384]{2,1,0:T(8,128)(2,1)}, bf16[4,192,384]{2,1,0:T(8,128)(2,1)}, bf16[4,192,384]{2,1,0:T(8,128)(2,1)}) custom-call(bf16[8,192,768]{2,1,0:T(8,128)(2,1)} %get-tuple-element.225.refs_0_, bf16[8,192,768]{2,1,0:T(8,128)(2,1)} %copy-done.1), custom_call_target="tpu_custom_call" | custom-call | flops 1 | bytes 1 | tf_op jit(solution)/shard_map/halves/pallas_call | solution.py:141
  258.6 1.6 collective-permute-start.12
  260.2 1.7 collective-permute-done.10.refs_3_
  263.2 2.8 halves.9
  266.0 2.6 collective-permute-start.20
  269.9 4.9 %collective-permute-done.17 = f32[80,128]{1,0:T(8,128)S(1)} collective-permute-done((f32[80,128]{1,0:T(8,128)S(1)}, f32[80,128]{1,0:T(8,128)S(1)}, u32[]{:S(2)}, u32[]{:S(2)}) %collective-permute-start.17) | collective-permute-done | bytes 40992 | tf_op jit(solution)/shard_map/ppermute | solution.py:944
  274.8 9.0 %collective-permute-done.12.refs_3_ = bf16[4,192,384]{2,1,0:T(8,128)(2,1)} collective-permute-done((bf16[4,192,384]{2,1,0:T(8,128)(2,1)}, bf16[4,192,384]{2,1,0:T(8,128)(2,1)}, u32[]{:S(2)}, u32[]{:S(2)}) %collective-permute-start.12) | collective-permute-done | bytes 589856 | tf_op jit(solution)/shard_map/ppermute | solution.py:944
  283.8 2.9 halves.10
  286.7 2.1 collective-permute-start.13
  289.5 4.4 %collective-permute-done.20 = bf16[1,384,768]{2,1,0:T(8,128)(2,1)} collective-permute-done((bf16[1,384,768]{2,1,0:T(8,128)(2,1)}, bf16[1,384,768]{2,1,0:T(8,128)(2,1)}, u32[]{:S(2)}, u32[]{:S(2)}) %collective-permute-start.20) | collective-permute-done | bytes 589856 | tf_op jit(solution)/shard_map/ppermute | solution.py:944
  296.8 2.3 collective-permute-done.13.refs_1_
  299.2 1.8 collective-permute-start.19
  302.4 2.5 halves.11
  309.2 11.0 %collective-permute-done.15 = bf16[1,192,768]{2,1,0:T(8,128)(2,1)S(1)} collective-permute-done((bf16[1,192,768]{2,1,0:T(8,128)(2,1)}, bf16[1,192,768]{2,1,0:T(8,128)(2,1)S(1)}, u32[]{:S(2)}, u32[]{:S(2)}) %collective-permute-start.15) | collective-permute-done | bytes 294944 | tf_op jit(solution)/shard_map/ppermute | solution.py:944
  (108 shorter events, 33.7 us)
Async XLA Ops:
  27.7 44.1 %collective-permute-start = (bf16[512,768]{1,0:T(8,128)(2,1)}, bf16[512,768]{1,0:T(8,128)(2,1)S(1)}, u32[]{:S(2)}, u32[]{:S(2)}) collective-permute-start(bf16[512,768]{1,0:T(8,128)(2,1)} %get-tuple-element.144), channel_id=1, source_target_pairs={{0,16},{1,17},{2,18},{3,19},{4,20},{5,21},{6,22},{7,23},{8,24},{9,... | collective-permute-start | bytes 2359304 | tf_op jit(solution)/shard_map/ppermute | solution.py:1039
  70.4 19.3 %collective-permute-start.2 = (bf16[512,768]{1,0:T(8,128)(2,1)}, bf16[512,768]{1,0:T(8,128)(2,1)S(1)}, u32[]{:S(2)}, u32[]{:S(2)}) collective-permute-start(bf16[512,768]{1,0:T(8,128)(2,1)} %get-tuple-element.150), channel_id=1, source_target_pairs={{0,16},{1,17},{2,18},{3,19},{4,20},{5,21},{6,22},{7,23},{8,24},{9,... | collective-permute-start | bytes 2359304 | tf_op jit(solution)/shard_map/ppermute | solution.py:1039
  74.5 44.5 %collective-permute-start.1 = (bf16[512,768]{1,0:T(8,128)(2,1)}, bf16[512,768]{1,0:T(8,128)(2,1)S(1)}, u32[]{:S(2)}, u32[]{:S(2)}) collective-permute-start(bf16[512,768]{1,0:T(8,128)(2,1)} %get-tuple-element.149), channel_id=1, source_target_pairs={{16,0},{17,1},{18,2},{19,3},{20,4},{21,5},{22,6},{23,7},{24,8},{25... | collective-permute-start | bytes 2359304 | tf_op jit(solution)/shard_map/ppermute | solution.py:1039
  98.8 72.1 %collective-permute-start.3 = (bf16[512,768]{1,0:T(8,128)(2,1)}, bf16[512,768]{1,0:T(8,128)(2,1)S(1)}, u32[]{:S(2)}, u32[]{:S(2)}) collective-permute-start(bf16[512,768]{1,0:T(8,128)(2,1)} %get-tuple-element.156), channel_id=1, source_target_pairs={{16,0},{17,1},{18,2},{19,3},{20,4},{21,5},{22,6},{23,7},{24,8},{25... | collective-permute-start | bytes 2359304 | tf_op jit(solution)/shard_map/ppermute | solution.py:1039
  190.6 11.3 %collective-permute-start.4 = (bf16[8,384,768]{2,1,0:T(8,128)(2,1)}, bf16[8,384,768]{2,1,0:T(8,128)(2,1)S(1)}, u32[]{:S(2)}, u32[]{:S(2)}) collective-permute-start(bf16[8,384,768]{2,1,0:T(8,128)(2,1)} %get-tuple-element.201), channel_id=1, source_target_pairs={{0,1},{1,0},{2,3},{3,2},{4,5},{5,4},{6,7},{7,6},{8,9},{9,8},{10,11... | collective-permute-start | bytes 14155784 | tf_op jit(solution)/shard_map/ppermute | solution.py:944
  210.4 28.6 %collective-permute-start.5 = (bf16[4,384,384]{2,1,0:T(8,128)(2,1)}, bf16[4,384,384]{2,1,0:T(8,128)(2,1)S(1)}, u32[]{:S(2)}, u32[]{:S(2)}) collective-permute-start(bf16[4,384,384]{2,1,0:T(8,128)(2,1)} %get-tuple-element.219), channel_id=1, source_target_pairs={{0,2},{1,3},{2,0},{3,1},{4,6},{5,7},{6,4},{7,5},{8,10},{9,11},{10,... | collective-permute-start | bytes 3538952 | tf_op jit(solution)/shard_map/ppermute | solution.py:944
  212.2 28.3 %collective-permute-start.6 = (bf16[4,384,384]{2,1,0:T(8,128)(2,1)}, bf16[4,384,384]{2,1,0:T(8,128)(2,1)S(1)}, u32[]{:S(2)}, u32[]{:S(2)}) collective-permute-start(bf16[4,384,384]{2,1,0:T(8,128)(2,1)} %get-tuple-element.221), channel_id=1, source_target_pairs={{0,4},{1,5},{2,6},{3,7},{4,0},{5,1},{6,2},{7,3},{8,12},{9,13},{10,... | collective-permute-start | bytes 3538952 | tf_op jit(solution)/shard_map/ppermute | solution.py:944
  233.6 14.7 %copy-start.21 = (s32[2,512]{1,0:T(2,128)S(1)}, s32[2,512]{1,0:T(2,128)}, u32[]{:S(2)}) copy-start(s32[2,512]{1,0:T(2,128)} %refs_4_.8) | copy-start | bytes 12292
  245.2 4.8 %collective-permute-start.7 = (bf16[8,192,768]{2,1,0:T(8,128)(2,1)}, bf16[8,192,768]{2,1,0:T(8,128)(2,1)S(1)}, u32[]{:S(2)}, u32[]{:S(2)}) collective-permute-start(bf16[8,192,768]{2,1,0:T(8,128)(2,1)} %get-tuple-element.226), channel_id=1, source_target_pairs={{0,1},{1,0},{2,3},{3,2},{4,5},{5,4},{6,7},{7,6},{8,9},{9,8},{10,11... | collective-permute-start | bytes 7077896 | tf_op jit(solution)/shard_map/ppermute | solution.py:944
  245.3 16.5 %collective-permute-start.10 = (bf16[2,384,384]{2,1,0:T(8,128)(2,1)}, bf16[2,384,384]{2,1,0:T(8,128)(2,1)}, u32[]{:S(2)}, u32[]{:S(2)}) collective-permute-start(bf16[2,384,384]{2,1,0:T(8,128)(2,1)} %get-tuple-element.238), channel_id=1, source_target_pairs={{0,2},{1,3},{2,0},{3,1},{4,6},{5,7},{6,4},{7,5},{8,10},{9,11},{10,... | collective-permute-start | bytes 1769480 | tf_op jit(solution)/shard_map/ppermute | solution.py:944
  246.7 16.5 %collective-permute-start.9 = (bf16[2,384,384]{2,1,0:T(8,128)(2,1)}, bf16[2,384,384]{2,1,0:T(8,128)(2,1)}, u32[]{:S(2)}, u32[]{:S(2)}) collective-permute-start(bf16[2,384,384]{2,1,0:T(8,128)(2,1)} %get-tuple-element.236), channel_id=1, source_target_pairs={{0,4},{1,5},{2,6},{3,7},{4,0},{5,1},{6,2},{7,3},{8,12},{9,13},{10,... | collective-permute-start | bytes 1769480 | tf_op jit(solution)/shard_map/ppermute | solution.py:944
  248.9 6.7 %copy-start.25 = (f32[24,768]{1,0:T(8,128)S(1)}, f32[24,768]{1,0:T(8,128)}, u32[]{:S(2)}) copy-start(f32[24,768]{1,0:T(8,128)} %get-tuple-element.265) | copy-start | bytes 221188
  248.9 6.9 %copy-start.19 = (f32[16,768]{1,0:T(8,128)S(1)}, f32[16,768]{1,0:T(8,128)}, u32[]{:S(2)}) copy-start(f32[16,768]{1,0:T(8,128)} %get-tuple-element.258) | copy-start | bytes 147460
  248.9 6.9 %copy-start.20 = (f32[16,768]{1,0:T(8,128)S(1)}, f32[16,768]{1,0:T(8,128)}, u32[]{:S(2)}) copy-start(f32[16,768]{1,0:T(8,128)} %get-tuple-element.260) | copy-start | bytes 147460
  248.9 7.0 %copy-start.15 = (f32[24,768]{1,0:T(8,128)S(1)}, f32[24,768]{1,0:T(8,128)}, u32[]{:S(2)}) copy-start(f32[24,768]{1,0:T(8,128)} %get-tuple-element.257) | copy-start | bytes 221188
  248.9 7.0 %copy-start.16 = (f32[24,768]{1,0:T(8,128)S(1)}, f32[24,768]{1,0:T(8,128)}, u32[]{:S(2)}) copy-start(f32[24,768]{1,0:T(8,128)} %get-tuple-element.255) | copy-start | bytes 221188
  255.5 13.1 %copy-start.12 = (bf16[512,768]{1,0:T(8,128)(2,1)S(1)}, bf16[512,768]{1,0:T(8,128)(2,1)}, u32[]{:S(2)}) copy-start(bf16[512,768]{1,0:T(8,128)(2,1)} %get-tuple-element.229) | copy-start | bytes 2359300
  255.5 13.1 %copy-start.9 = (bf16[512,768]{1,0:T(8,128)(2,1)S(1)}, bf16[512,768]{1,0:T(8,128)(2,1)}, u32[]{:S(2)}) copy-start(bf16[512,768]{1,0:T(8,128)(2,1)} %get-tuple-element.232) | copy-start | bytes 2359300
  255.5 13.1 %copy-start.10 = (bf16[512,768]{1,0:T(8,128)(2,1)S(1)}, bf16[512,768]{1,0:T(8,128)(2,1)}, u32[]{:S(2)}) copy-start(bf16[512,768]{1,0:T(8,128)(2,1)} %get-tuple-element.234) | copy-start | bytes 2359300
  255.6 13.1 %copy-start.11 = (bf16[512,768]{1,0:T(8,128)(2,1)S(1)}, bf16[512,768]{1,0:T(8,128)(2,1)}, u32[]{:S(2)}) copy-start(bf16[512,768]{1,0:T(8,128)(2,1)} %get-tuple-element.230) | copy-start | bytes 2359300
  257.1 11.8 %collective-permute-start.16 = (f32[80,128]{1,0:T(8,128)S(1)}, f32[80,128]{1,0:T(8,128)S(1)}, u32[]{:S(2)}, u32[]{:S(2)}) collective-permute-start(f32[80,128]{1,0:T(8,128)S(1)} %bitcast.42), channel_id=1, source_target_pairs={{0,1},{1,0},{2,3},{3,2},{4,5},{5,4},{6,7},{7,6},{8,9},{9,8},{10,11... | collective-permute-start | bytes 122888 | tf_op jit(solution)/shard_map/ppermute | solution.py:944
  257.3 17.5 %collective-permute-start.11 = (bf16[4,192,384]{2,1,0:T(8,128)(2,1)}, bf16[4,192,384]{2,1,0:T(8,128)(2,1)}, u32[]{:S(2)}, u32[]{:S(2)}) collective-permute-start(bf16[4,192,384]{2,1,0:T(8,128)(2,1)} %get-tuple-element.241), channel_id=1, source_target_pairs={{0,2},{1,3},{2,0},{3,1},{4,6},{5,7},{6,4},{7,5},{8,10},{9,11},{10,... | collective-permute-start | bytes 1769480 | tf_op jit(solution)/shard_map/ppermute | solution.py:944
  258.6 25.2 %collective-permute-start.12 = (bf16[4,192,384]{2,1,0:T(8,128)(2,1)}, bf16[4,192,384]{2,1,0:T(8,128)(2,1)}, u32[]{:S(2)}, u32[]{:S(2)}) collective-permute-start(bf16[4,192,384]{2,1,0:T(8,128)(2,1)} %get-tuple-element.243), channel_id=1, source_target_pairs={{0,4},{1,5},{2,6},{3,7},{4,0},{5,1},{6,2},{7,3},{8,12},{9,13},{10,... | collective-permute-start | bytes 1769480 | tf_op jit(solution)/shard_map/ppermute | solution.py:944
  266.0 27.9 %collective-permute-start.20 = (bf16[1,384,768]{2,1,0:T(8,128)(2,1)}, bf16[1,384,768]{2,1,0:T(8,128)(2,1)}, u32[]{:S(2)}, u32[]{:S(2)}) collective-permute-start(bf16[1,384,768]{2,1,0:T(8,128)(2,1)} %get-tuple-element.269), channel_id=1, source_target_pairs={{0,8},{1,9},{2,10},{3,11},{4,12},{5,13},{6,14},{7,15},{8,0},{9,1},... | collective-permute-start | bytes 1769480 | tf_op jit(solution)/shard_map/ppermute | solution.py:944
  268.9 5.9 %collective-permute-start.17 = (f32[80,128]{1,0:T(8,128)S(1)}, f32[80,128]{1,0:T(8,128)S(1)}, u32[]{:S(2)}, u32[]{:S(2)}) collective-permute-start(f32[80,128]{1,0:T(8,128)S(1)} %bitcast_add_fusion), channel_id=1, source_target_pairs={{0,2},{1,3},{2,0},{3,1},{4,6},{5,7},{6,4},{7,5},{8,10},{9,11},{10,... | collective-permute-start | bytes 122888 | tf_op jit(solution)/shard_map/ppermute | solution.py:944
  269.8 24.1 %copy-start.14 = (bf16[1,384,768]{2,1,0:T(8,128)(2,1)S(1)}, bf16[1,384,768]{2,1,0:T(8,128)(2,1)}, u32[]{:S(2)}) copy-start(bf16[1,384,768]{2,1,0:T(8,128)(2,1)} %get-tuple-element.239) | copy-start | bytes 1769476
  269.8 31.2 %collective-permute-start.8 = (bf16[1024,384]{1,0:T(8,128)(2,1)S(1)}, bf16[1024,384]{1,0:T(8,128)(2,1)S(1)}, u32[]{:S(2)}, u32[]{:S(2)}) collective-permute-start(bf16[1024,384]{1,0:T(8,128)(2,1)S(1)} %pad_maximum_fusion), channel_id=1, source_target_pairs={{0,16},{16,0},{1,17},{17,1},{2,18},{18,2},{3,19},{19,3},{4,20},{20... | collective-permute-start | bytes 2359304 | tf_op jit(solution)/shard_map/ppermute | solution.py:1163
  283.8 13.0 %collective-permute-start.18 = (f32[80,128]{1,0:T(8,128)S(1)}, f32[80,128]{1,0:T(8,128)S(1)}, u32[]{:S(2)}, u32[]{:S(2)}) collective-permute-start(f32[80,128]{1,0:T(8,128)S(1)} %add.83), channel_id=1, source_target_pairs={{0,4},{1,5},{2,6},{3,7},{4,0},{5,1},{6,2},{7,3},{8,12},{9,13},{10,... | collective-permute-start | bytes 122888 | tf_op jit(solution)/shard_map/ppermute | solution.py:944
  286.7 12.4 %collective-permute-start.13 = (bf16[2,192,384]{2,1,0:T(8,128)(2,1)}, bf16[2,192,384]{2,1,0:T(8,128)(2,1)S(1)}, u32[]{:S(2)}, u32[]{:S(2)}) collective-permute-start(bf16[2,192,384]{2,1,0:T(8,128)(2,1)} %get-tuple-element.247), channel_id=1, source_target_pairs={{0,4},{1,5},{2,6},{3,7},{4,0},{5,1},{6,2},{7,3},{8,12},{9,13},{10,... | collective-permute-start | bytes 884744 | tf_op jit(solution)/shard_map/ppermute | solution.py:944
  288.8 10.4 %collective-permute-start.14 = (bf16[2,192,384]{2,1,0:T(8,128)(2,1)}, bf16[2,192,384]{2,1,0:T(8,128)(2,1)S(1)}, u32[]{:S(2)}, u32[]{:S(2)}) collective-permute-start(bf16[2,192,384]{2,1,0:T(8,128)(2,1)} %get-tuple-element.249), channel_id=1, source_target_pairs={{0,2},{1,3},{2,0},{3,1},{4,6},{5,7},{6,4},{7,5},{8,10},{9,11},{10,... | collective-permute-start | bytes 884744 | tf_op jit(solution)/shard_map/ppermute | solution.py:944
  299.2 7.0 %collective-permute-start.19 = (f32[80,128]{1,0:T(8,128)S(1)}, f32[80,128]{1,0:T(8,128)S(1)}, u32[]{:S(2)}, u32[]{:S(2)}) collective-permute-start(f32[80,128]{1,0:T(8,128)S(1)} %add.84), channel_id=1, source_target_pairs={{0,8},{1,9},{2,10},{3,11},{4,12},{5,13},{6,14},{7,15},{8,0},{9,1},... | collective-permute-start | bytes 122888 | tf_op jit(solution)/shard_map/ppermute | solution.py:944
  304.9 15.3 %collective-permute-start.15 = (bf16[1,192,768]{2,1,0:T(8,128)(2,1)}, bf16[1,192,768]{2,1,0:T(8,128)(2,1)S(1)}, u32[]{:S(2)}, u32[]{:S(2)}) collective-permute-start(bf16[1,192,768]{2,1,0:T(8,128)(2,1)} %get-tuple-element.251), channel_id=1, source_target_pairs={{0,8},{1,9},{2,10},{3,11},{4,12},{5,13},{6,14},{7,15},{8,0},{9,1},... | collective-permute-start | bytes 884744 | tf_op jit(solution)/shard_map/ppermute | solution.py:944
  (15 other events, 49.2 us)
